TPU v7x, 256 devices: a whole 4x4x8 slice. The times are simulated.
256 devices in a mesh: dp: 8 (over z), mp: 32 (over x, y, core).
Axes of the slice: x: 4, y: 4, z: 8, core: 2. Of those that a mesh axis runs over, the one named last changes fastest.
Arguments:
- momentum: bfloat16 [8192, 26624], P('mp', 'dp'), may hold values from -3 to 3
- tile_values: bfloat16 [8192, 26624], P('mp', 'dp'), may hold values from -448 to 448
- exponents: int32 [64, 208], P('mp', 'dp'), may hold values from -11 to -8
- overflow: int32 [32, 8], P('mp', 'dp'), may hold values from 0 to 1, as said below
- right_prev: float32 [26624, 128], P(('dp', 'mp')), may hold values from -6 to 6
Outputs:
- momentum_new: bfloat16 [8192, 26624], P('mp', 'dp')
- right_factor: float32 [26624, 128], P(('dp', 'mp'))
- update: bfloat16 [8192, 26624], P('mp', 'dp')
Inputs may be any that keep to these rules, and one draw needn't show every extreme that they name: `overflow`: 1 marks a tile whose gradient is dropped; some tile is dropped and some is kept. `exponents`: one exponent for each block.
All inputs are finite; a program needn't handle non-finite values.
Results may differ from a plain program's by a relative error of at most 0.0075.
Values may be sent and summed in bfloat16 or wider, within the bound.
A program may use at most 64 MiB of HBM per device.

v0:
```python
import math

import jax
import jax.numpy as jnp
from jax import lax
from jax.sharding import PartitionSpec as P

BLOCK = 128


epsilon = 1e-06
retain = 0.95


def trans_dot(left_mat, right_mat):
    return lax.dot_general(
        left_mat, right_mat, (((0,), (0,)), ((), ())), preferred_element_type=jnp.float32
    )


def outer_dot(left_mat, right_mat):
    return lax.dot_general(
        left_mat, right_mat, (((1,), (1,)), ((), ())), preferred_element_type=jnp.float32
    )


def body(momentum, tile_values, exponents, overflow, right_prev):
    rows_local, cols_local = momentum.shape
    rank_cols = right_prev.shape[1]
    mp_count = lax.axis_size("mp")
    dp_count = lax.axis_size("dp")
    block_rows, block_cols = exponents.shape
    scales = jnp.exp2(exponents.astype(jnp.float32)).astype(jnp.bfloat16)
    decoded = (
        tile_values.reshape(block_rows, BLOCK, block_cols, BLOCK) * scales[:, None, :, None]
    ).reshape(rows_local, cols_local)
    kept_tile = overflow[0, 0] == 0
    gradient = jnp.where(kept_tile, decoded, jnp.zeros_like(decoded))
    healthy = lax.psum(jnp.sum((overflow == 0).astype(jnp.float32)), ("dp", "mp"))
    factor = mp_count * dp_count / jnp.maximum(healthy, 1.0)
    shard_rows = lax.all_gather(right_prev.astype(jnp.bfloat16), "mp", axis=0, tiled=True)
    mom_cols = momentum
    grad_cols = gradient
    mom_part = jnp.dot(mom_cols, shard_rows, preferred_element_type=jnp.float32)
    grad_part = jnp.dot(grad_cols, shard_rows, preferred_element_type=jnp.float32)
    left_raw = lax.psum(mom_part + factor * grad_part, "dp")
    gram_local = jnp.dot(
        left_raw.T, left_raw, precision=lax.Precision.HIGHEST, preferred_element_type=jnp.float32
    )
    lower_tri = jnp.linalg.cholesky(lax.psum(gram_local, "mp"))
    ortho_rows = jax.scipy.linalg.solve_triangular(lower_tri, left_raw.T, lower=True).T
    ortho_low = ortho_rows.astype(jnp.bfloat16)
    share_rows = cols_local // mp_count
    mom_cols = momentum
    grad_cols = gradient
    right_full = lax.psum(
        trans_dot(mom_cols, ortho_low) + factor * trans_dot(grad_cols, ortho_low), "mp"
    )
    squares = lax.psum(jnp.sum(right_full * right_full, 0), "dp")
    inverse = lax.rsqrt(squares + epsilon)
    right_out = lax.dynamic_slice_in_dim(
        right_full, lax.axis_index("mp") * share_rows, share_rows, 0
    )
    factor_low = right_full.astype(jnp.bfloat16)
    normal_low = (right_full * inverse[None, :]).astype(jnp.bfloat16)
    unit_scale = math.sqrt(rows_local * mp_count * cols_local * dp_count / rank_cols)
    correction = outer_dot(ortho_low, factor_low)
    direction = outer_dot(ortho_low, normal_low)
    momentum_new = (
        momentum.astype(jnp.float32)
        + factor * gradient.astype(jnp.float32)
        - (1.0 - retain) * correction
    ).astype(jnp.bfloat16)
    update = (unit_scale * direction).astype(jnp.bfloat16)
    return (momentum_new, right_out, update)


def solution(mesh):
    in_specs = (P("mp", "dp"), P("mp", "dp"), P("mp", "dp"), P("mp", "dp"), P(("dp", "mp"), None))
    out_specs = (P("mp", "dp"), P(("dp", "mp"), None), P("mp", "dp"))
    return jax.shard_map(body, mesh=mesh, in_specs=in_specs, out_specs=out_specs, check_vma=False)
```

profile of v0, /device:TPU:1, one launch (start us, length us, event | category | flops | bytes accessed | tf_op | source)
XLA Modules:
  0.0 473.3 jit_solution(8629263678587930556)
XLA Ops:
  7.2 0.0 all-reduce.4.cloned.1.call-start
  7.9 0.7 exponential_convert_fusion
  8.5 0.1 copy.12
  8.7 1.0 mul.56
  9.6 0.2 copy.22
  9.9 0.0 copy-start.3
  9.9 2.4 copy.13
  12.2 81.3 %psum.35 = f32[]{:T(128)} all-reduce(f32[]{:T(128)S(6)} %reduce_sum.18), channel_id=1, replica_groups=mesh['dp'=8,'mp'=32] {'dp','mp'}, use_global_device_ids=true, to_apply=%region_0.1 | all-reduce | flops 1 | bytes 8 | tf_op jit(solution)/shard_map/psum | solution.py:39
  93.6 0.0 copy-done.3
  93.6 25.5 %all_gather.3 = bf16[3328,128]{1,0:T(8,128)(2,1)} all-gather(bf16[104,128]{1,0:T(8,128)(2,1)S(1)} %convert_element_type.35), channel_id=1, replica_groups=mesh['dp'=8,'mp'=32] {'mp'}, dimensions={0}, use_global_device_ids=true | all-gather | bytes 878592 | tf_op jit(solution)/shard_map/all_gather | solution.py:41
  119.0 0.0 copy-start.1
  119.0 2.3 multiply_select_fusion
  122.0 0.0 copy-done.1
  122.0 0.0 copy-start.2
  122.0 1.8 fusion.10
  123.8 0.0 copy-done.2
  123.9 1.3 fusion.4
  125.1 0.0 all-reduce.4.cloned.1.call-update
  125.1 0.0 all-reduce.6.cloned.1.call-start
  125.2 63.0 %all-reduce.4.cloned.1.call-done = f32[256,128]{1,0:T(8,128)} async-done(((f32[256,128]{1,0:T(8,128)}), f32[256,128]{1,0:T(8,128)}) %all-reduce.4.cloned.1.call-update) | async-done | bytes 131088 | tf_op jit(solution)/shard_map/psum | solution.py:46
  188.2 2.0 fusion.11
  190.2 0.0 all-reduce.6.cloned.1.call-update
  190.2 0.2 all-reduce.8.cloned.1.call-start
  190.4 111.4 %all-reduce.6.cloned.1.call-done = f32[128,128]{0,1:T(8,128)} async-done(((f32[128,128]{0,1:T(8,128)}), f32[128,128]{0,1:T(8,128)}) %all-reduce.6.cloned.1.call-update) | async-done | bytes 65552 | tf_op jit(solution)/shard_map/psum | solution.py:50
  301.9 0.9 copy.15
  302.8 0.9 fusion.9
  303.6 11.7 %cholesky.16 = f32[128,128]{1,0:T(8,128)S(1)} custom-call(f32[128,128]{1,0:T(8,128)S(1)} %fusion.9), custom_call_target="Cholesky" | custom-call | tf_op jit(solution)/shard_map/jit(cholesky)/cholesky | solution.py:50
  315.4 0.6 compare_reduce_fusion
  316.0 0.7 fusion.7
  316.7 10.4 %custom-call.7 = f32[1,128,128]{1,2,0:T(8,128)} custom-call(f32[1,128,128]{2,1,0:T(8,128)S(1)} %fusion.7), custom_call_target="InvertDiagBlocksLowerTriangular" | custom-call | tf_op jit(solution)/shard_map/jit(_solve_triangular)/triangular_solve | solution.py:51
  327.1 1.2 convolution_convert_fusion
  328.3 0.4 convolution_bitcast_fusion
  328.7 1.6 fusion.3
  330.4 0.0 all-reduce.8.cloned.1.call-update
  330.4 114.7 %all-reduce.8.cloned.1.call-done = f32[3328,128]{0,1:T(8,128)} async-done(((f32[3328,128]{0,1:T(8,128)}), f32[3328,128]{0,1:T(8,128)}) %all-reduce.8.cloned.1.call-update) | async-done | bytes 1703952 | tf_op jit(solution)/shard_map/psum | solution.py:56
  445.1 0.0 copy-start
  445.1 1.8 multiply_reduce_fusion
  446.9 13.7 %psum.39 = f32[128]{0:T(128)S(1)} all-reduce(f32[128]{0:T(128)S(1)} %multiply_reduce_fusion), channel_id=1, replica_groups=mesh['dp'=8,'mp'=32] {'dp'}, use_global_device_ids=true, to_apply=%region_7.8 | all-reduce | flops 128 | bytes 1024 | tf_op jit(solution)/shard_map/psum | solution.py:59
  460.6 0.0 copy-done
  460.6 0.1 constant_dynamic-slice_fusion
  460.7 0.7 copy.17
  461.4 3.5 fusion.1
  464.9 1.9 fusion.2
  (3 shorter events, 0.0 us)
Async XLA Ops:
  7.2 181.0 %all-reduce.4.cloned.1.call-start = ((), (), s32[]{:S(2)}) async-start(), calls=%async_computation | async-start | bytes 262144 | tf_op jit(solution)/shard_map/psum | solution.py:46
  9.9 83.7 %copy-start.3 = (f32[104,128]{1,0:T(8,128)S(1)}, f32[104,128]{1,0:T(8,128)}, u32[]{:S(2)}) copy-start(f32[104,128]{1,0:T(8,128)} %param.9) | copy-start | bytes 159748
  119.0 3.0 copy-start.1
  122.0 1.8 copy-start.2
  125.1 176.7 %all-reduce.6.cloned.1.call-start = ((), (), s32[]{:S(2)}) async-start(), calls=%async_computation.1 | async-start | bytes 131072 | tf_op jit(solution)/shard_map/psum | solution.py:50
  190.2 254.9 %all-reduce.8.cloned.1.call-start = ((), (), s32[]{:S(2)}) async-start(), calls=%async_computation.2 | async-start | bytes 3407872 | tf_op jit(solution)/shard_map/psum | solution.py:56
  445.1 15.5 %copy-start = (f32[3328,128]{0,1:T(8,128)S(1)}, f32[3328,128]{0,1:T(8,128)}, u32[]{:S(2)}) copy-start(f32[3328,128]{0,1:T(8,128)} %all-reduce.8.cloned.1.call-done) | copy-start | bytes 5111812
Sparse Core Ops, SparseCore 0:
  125.3 62.8 all-reduce.3
  192.4 109.4 all-reduce.5
  330.5 114.5 all-reduce.7
where the time goes:
time: 478 us; the launch traced here: 473 us
  waiting for transfers between devices  289 us (60%)
  blocking collectives  120 us (25%)
  other arithmetic  29.1 us (6%)
  between operations  15.2 us (3%)
  matrix products  13.7 us (3%)
  local copies, waits for them, and re-layouts  5.41 us (1%)
    psum x1, waiting for transfers between devices, body(): lax.psum(trans_dot(mom_cols, ortho_low) + factor * trans_dot(grad_cols, o...  115 us
    psum x1, waiting for transfers between devices, body(): lower_tri = jnp.linalg.cholesky(lax.psum(gram_local, 'mp'))  111 us
    psum x1, blocking collectives, body(): lax.psum(jnp.sum((overflow == 0).astype(jnp.float32)), ('dp', 'mp'))  81.3 us
    psum x1, waiting for transfers between devices, body(): left_raw = lax.psum(mom_part + factor * grad_part, 'dp')  63 us
    all_gather x1, blocking collectives, body(): lax.all_gather(right_prev.astype(jnp.bfloat16), 'mp', axis=0, tiled=True)  25.5 us
    psum x1, blocking collectives, body(): squares = lax.psum(jnp.sum(right_full * right_full, 0), 'dp')  13.7 us
    another operation x3, other arithmetic, body(): lower_tri = jnp.linalg.cholesky(lax.psum(gram_local, 'mp'))  12.4 us
    another operation x2, other arithmetic, body(): jax.scipy.linalg.solve_triangular(lower_tri, left_raw.T, lower=True)  11.1 us
  transfers between devices with their start and end apart: 3, of which 3 were waited for; matrix products, arithmetic and copies ran while one was open for 0% of the time, Pallas kernels for 0%

commit v1 on v0

v1 whole, which is shorter than its diff:
```python
import functools
import math

import jax
import jax.numpy as jnp
from jax import lax
from jax.experimental import pallas as pl
from jax.experimental.pallas import tpu as pltpu
from jax.sharding import PartitionSpec as P

MESH = pl.DeviceIdType.MESH
F32 = jnp.float32
BF16 = jnp.bfloat16
HIGH = lax.Precision.HIGHEST
BLOCK = 128
EPSILON = 1e-06
RETAIN = 0.95
VMEM_LIMIT = 48 * 1024 * 1024


class Place:
    def __init__(self, n_dp, n_mp):
        self.nz = n_dp
        self.chips = n_mp // 2
        self.ny = int(round(math.sqrt(self.chips)))
        self.nx = self.chips // self.ny
        self.half = self.chips // 2
        mp = lax.axis_index("mp")
        self.z = lax.axis_index("dp")
        self.core = lax.rem(mp, 2)
        self.other = 1 - self.core
        self.chip = mp // 2
        self.x = self.chip // self.ny
        self.y = lax.rem(self.chip, self.ny)

    def chip_at(self, dx, dy):
        x = lax.rem(self.x + dx + self.nx, self.nx)
        y = lax.rem(self.y + dy + self.ny, self.ny)
        return x * self.ny + y

    def offset(self, i, parity):
        dx = i // (self.ny // 2)
        dy = 2 * (i % (self.ny // 2)) + lax.rem(dx + parity, 2)
        return dx, dy

    def to_chip(self, i, parity):
        dx, dy = self.offset(i, parity)
        return self.chip_at(dx, dy)

    def from_chip(self, i, parity):
        dx, dy = self.offset(i, parity)
        return self.chip_at(-dx, -dy)

    def z_at(self, dz):
        return lax.rem(self.z + dz, self.nz)

    def dev(self, z, chip, core):
        return (z, chip * 2 + core)

    def sibling(self):
        return self.dev(self.z, self.chip, self.other)

    def plane_peers(self):
        return [
            self.dev(self.z, self.chip_at(dx, dy), self.core)
            for dx in range(self.nx)
            for dy in range(self.ny)
            if dx or dy
        ]

    def z_peers(self):
        return [self.dev(self.z_at(dz), self.chip, self.core) for dz in range(1, self.nz)]

    def zc_peers(self):
        return [
            self.dev(self.z_at(dz), self.chip, self.core if dc == 0 else self.other)
            for dz in range(self.nz)
            for dc in range(2)
            if dz or dc
        ]


def remote(src, dst, send, recv, dev):
    return pltpu.make_async_remote_copy(
        src_ref=src, dst_ref=dst, send_sem=send, recv_sem=recv, device_id=dev, device_id_type=MESH
    )


def greet(peers):
    barrier = pltpu.get_barrier_semaphore()
    for dev in peers:
        pl.semaphore_signal(barrier, inc=1, device_id=dev, device_id_type=MESH)
    pl.semaphore_wait(barrier, len(peers))


def exchange(place, peers, src_of, dst, sems, slot):
    copies = [
        remote(src_of(k), dst.at[slot], sems.at[0, k], sems.at[1, k], dev) for k, dev in enumerate(peers)
    ]
    for copy in copies:
        copy.start()
    return copies


def gather_send(place, buf, rows, sems):
    block = buf.at[pl.ds(pl.multiple_of(place.chip * rows, 16), rows)]
    for i in range(place.half):
        copy = remote(
            block, block, sems.at[0, i], sems.at[1, i], place.dev(place.z, place.to_chip(i, place.core), place.core)
        )
        if i == 0:
            pl.when(place.core == 1)(copy.start)
        else:
            copy.start()


def gather_forward(place, buf, rows, sems, i):
    start = pl.multiple_of(place.from_chip(i, place.core) * rows, 16)
    block = buf.at[pl.ds(start, rows)]

    def go():
        remote(block, block, sems.at[0, i], sems.at[1, i], place.sibling()).wait_recv()
        remote(block, block, sems.at[2, i], sems.at[3, i], place.sibling()).start()

    if i == 0:
        pl.when(place.core == 1)(go)
    else:
        go()


def gather_finish(place, buf, rows, sems):
    for i in range(place.half):
        start = pl.multiple_of(place.from_chip(i, place.other) * rows, 16)
        block = buf.at[pl.ds(start, rows)]
        copy = remote(block, block, sems.at[2, i], sems.at[3, i], place.sibling())
        if i == 0:
            pl.when(place.core == 0)(copy.wait_recv)
        else:
            copy.wait_recv()
    for i in range(place.half):
        block = buf.at[pl.ds(0, rows)]
        sent = remote(block, block, sems.at[0, i], sems.at[1, i], place.sibling())
        passed = remote(block, block, sems.at[2, i], sems.at[3, i], place.sibling())

        def done(sent=sent, passed=passed):
            sent.wait_send()
            passed.wait_send()

        if i == 0:
            pl.when(place.core == 1)(done)
        else:
            done()


def left_kernel(
    n_dp, n_mp,
    mom_hbm, tile_hbm, exps_ref, over_ref, prev_ref,
    gram_ref, left_ref, factor_ref, scale_ref,
    mom, tile, pair, right, flag_z, flag_c, flag_p, part, left_in, left, gram, gram_zc, gram_p, gram_all,
    sem_in, sem_pair, sem_gather, sem_fz, sem_fc, sem_fp, sem_lr, sem_lg, sem_gr, sem_gp, sem_gg,
):
    place = Place(n_dp, n_mp)
    rows, cols = mom.shape
    share = prev_ref.shape[0]
    block = 2 * share
    loads = [
        pltpu.make_async_copy(mom_hbm, mom, sem_in.at[0]),
        pltpu.make_async_copy(tile_hbm, tile, sem_in.at[1]),
    ]
    for load in loads:
        load.start()
    plane, zline, zc = place.plane_peers(), place.z_peers(), place.zc_peers()
    kept = jnp.where(over_ref[...] == 0, 1.0, 0.0).astype(F32)
    flag_z[place.z] = jnp.broadcast_to(kept, (8, 128))
    mine = pl.ds(pl.multiple_of(place.core * share, 8), share)
    pair[mine] = prev_ref[...]
    greet(plane + zc)

    pair_copy = remote(pair.at[mine], pair.at[mine], sem_pair.at[0], sem_pair.at[1], place.sibling())
    pair_copy.start()
    fz = exchange(place, zline, lambda k: flag_z.at[place.z], flag_z, sem_fz, place.z)
    pair_copy.wait_recv()
    right[pl.ds(pl.multiple_of(place.chip * block, 16), block)] = pair[...].astype(BF16)
    gather_send(place, right, block, sem_gather)

    for copy in fz:
        copy.wait_recv()
    flag_c[place.core] = jnp.sum(flag_z[...], axis=0)
    fc = remote(flag_c.at[place.core], flag_c.at[place.core], sem_fc.at[0], sem_fc.at[1], place.sibling())
    fc.start()
    scales = jnp.exp2(exps_ref[...].astype(F32)).astype(BF16).astype(F32) * kept
    for j in range(cols // BLOCK):
        scale_ref[:, j * BLOCK:(j + 1) * BLOCK] = jnp.broadcast_to(scales[:, j:j + 1], (scales.shape[0], BLOCK))
    for load in loads:
        load.wait()
    fc.wait_recv()
    flag_p[place.chip] = flag_c[0] + flag_c[1]
    fp = exchange(place, plane, lambda k: flag_p.at[place.chip], flag_p, sem_fp, place.chip)
    for b in range(rows // BLOCK):
        scale = scale_ref[b:b + 1, :].astype(BF16)
        for r in range(0, BLOCK, 32):
            at = slice(b * BLOCK + r, b * BLOCK + r + 32)
            tile[at, :] = tile[at, :] * scale
    for i in range(place.half):
        gather_forward(place, right, block, sem_gather, i)
    for copy in fp:
        copy.wait_recv()
    healthy = jnp.sum(flag_p[...], axis=0)
    factor = float(n_dp * n_mp) / jnp.maximum(healthy, 1.0)
    factor_ref[...] = factor
    gather_finish(place, right, block, sem_gather)

    mom_part = jnp.dot(mom[...], right[...], preferred_element_type=F32)
    grad_part = jnp.dot(tile[...], right[...], preferred_element_type=F32)
    part[...] = mom_part + factor[0:1, :] * grad_part

    rz = rows // place.nz
    lr = []
    for dz in range(1, place.nz):
        z2 = place.z_at(dz)
        copy = remote(
            part.at[pl.ds(pl.multiple_of(z2 * rz, 8), rz)], left_in.at[dz - 1],
            sem_lr.at[0, dz - 1], sem_lr.at[1, dz - 1], place.dev(z2, place.chip, place.core),
        )
        copy.start()
        lr.append(copy)
    own = pl.ds(pl.multiple_of(place.z * rz, 8), rz)
    acc = part[own]
    for k, copy in enumerate(lr):
        copy.wait_recv()
        acc = acc + left_in[k]
    left[own] = acc
    gram[...] = lax.dot_general(acc, acc, (((0,), (0,)), ((), ())), precision=HIGH, preferred_element_type=F32)

    gs = gram.shape[0] // (2 * place.nz)
    gr = []
    k = 0
    for dz in range(place.nz):
        for dc in range(2):
            if dz or dc:
                z2, c2 = place.z_at(dz), place.core if dc == 0 else place.other
                copy = remote(
                    gram.at[pl.ds(pl.multiple_of((z2 * 2 + c2) * gs, 8), gs)], gram_zc.at[k],
                    sem_gr.at[0, k], sem_gr.at[1, k], place.dev(z2, place.chip, c2),
                )
                copy.start()
                gr.append(copy)
                k += 1
    lg = [
        remote(left.at[own], left.at[own], sem_lg.at[0, k], sem_lg.at[1, k], dev) for k, dev in enumerate(zline)
    ]
    for copy in lg:
        copy.start()
    piece = pl.ds(pl.multiple_of((place.z * 2 + place.core) * gs, 8), gs)
    acc = gram[piece]
    for k, copy in enumerate(gr):
        copy.wait_recv()
        acc = acc + gram_zc[k]
    gram_p[place.chip] = acc
    gp = exchange(place, plane, lambda k: gram_p.at[place.chip], gram_p, sem_gp, place.chip)
    for copy in gp:
        copy.wait_recv()
    gram_all[piece] = jnp.sum(gram_p[...], axis=0)
    gg = [
        remote(gram_all.at[piece], gram_all.at[piece], sem_gg.at[0, k], sem_gg.at[1, k], dev)
        for k, dev in enumerate(zc)
    ]
    for copy in gg:
        copy.start()
    for copy in lg:
        copy.wait_recv()
    left_ref[...] = left[...]
    for copy in gg:
        copy.wait_recv()
    gram_ref[...] = gram_all[...]
    for copy in [pair_copy, fc] + fz + fp + lr + gr + lg + gp + gg:
        copy.wait_send()


def left_stage(n_dp, n_mp, momentum, tile_values, exponents, overflow, right_prev):
    rows, cols = momentum.shape
    share, rank = right_prev.shape
    chips = n_mp // 2
    rz = rows // n_dp
    gs = rank // (2 * n_dp)
    vmem = pl.BlockSpec(memory_space=pltpu.VMEM)
    hbm = pl.BlockSpec(memory_space=pl.ANY)
    dma = pltpu.SemaphoreType.DMA
    return pl.pallas_call(
        functools.partial(left_kernel, n_dp, n_mp),
        name="left",
        out_shape=(
            jax.ShapeDtypeStruct((rank, rank), F32),
            jax.ShapeDtypeStruct((rows, rank), F32),
            jax.ShapeDtypeStruct((8, 128), F32),
            jax.ShapeDtypeStruct((rows // BLOCK, cols), F32),
        ),
        in_specs=[hbm, hbm, vmem, vmem, vmem],
        out_specs=(vmem,) * 4,
        scratch_shapes=[
            pltpu.VMEM((rows, cols), BF16),
            pltpu.VMEM((rows, cols), BF16),
            pltpu.VMEM((2 * share, rank), F32),
            pltpu.VMEM((cols, rank), BF16),
            pltpu.VMEM((n_dp, 8, 128), F32),
            pltpu.VMEM((2, 8, 128), F32),
            pltpu.VMEM((chips, 8, 128), F32),
            pltpu.VMEM((rows, rank), F32),
            pltpu.VMEM((n_dp - 1, rz, rank), F32),
            pltpu.VMEM((rows, rank), F32),
            pltpu.VMEM((rank, rank), F32),
            pltpu.VMEM((2 * n_dp - 1, gs, rank), F32),
            pltpu.VMEM((chips, gs, rank), F32),
            pltpu.VMEM((rank, rank), F32),
            dma((2,)),
            dma((2,)),
            dma((4, chips // 2)),
            dma((2, n_dp - 1)),
            dma((2,)),
            dma((2, chips - 1)),
            dma((2, n_dp - 1)),
            dma((2, n_dp - 1)),
            dma((2, 2 * n_dp - 1)),
            dma((2, chips - 1)),
            dma((2, 2 * n_dp - 1)),
        ],
        compiler_params=pltpu.CompilerParams(
            collective_id=0, has_side_effects=True, vmem_limit_bytes=VMEM_LIMIT
        ),
    )(momentum, tile_values, exponents, overflow, right_prev)


def inverse_kernel(gram_ref, out_ref, work):
    rank = gram_ref.shape[0]
    work[...] = gram_ref[...]
    lanes = lax.broadcasted_iota(jnp.int32, (8, rank), 1)
    for r in range(0, rank, 8):
        row = [work[r + i:r + i + 1, :] for i in range(8)]
        a = [[jnp.broadcast_to(row[i][:, r + j:r + j + 1], (1, rank)) for j in range(i + 1)] for i in range(8)]
        e = [[None] * 8 for _ in range(8)]
        for j in range(8):
            s = lax.rsqrt(a[j][j])
            s = s * (1.5 - 0.5 * a[j][j] * s * s)
            e[j][j] = s
            for k in range(j):
                e[j][k] = e[j][k] * s
            for i in range(j + 1, 8):
                m = a[i][j] * s
                a[i][j] = m
                for k in range(j + 1):
                    t = m * e[j][k]
                    e[i][k] = -t if e[i][k] is None else e[i][k] - t
            for i in range(j + 1, 8):
                for k in range(j + 1, i + 1):
                    a[i][k] = a[i][k] - a[i][j] * a[k][j]
        upper, mixed = [], []
        lane = lanes[0:1]
        for i in range(8):
            total = e[i][0] * row[0]
            for j in range(1, i + 1):
                total = total + e[i][j] * row[j]
            inv = total
            for j in range(8):
                here = lane == r + j
                inv = jnp.where(here, e[i][j] if j <= i else 0.0, inv)
            upper.append(total)
            mixed.append(jnp.where(lane < r + 8, inv, total))
        upper = jnp.concatenate(upper, axis=0)
        mixed = jnp.concatenate(mixed, axis=0)
        out_ref[r:r + 8, :] = jnp.where(lanes < r + 8, mixed, 0.0)
        n = rank - r - 8
        if n:
            low = lax.dot_general(
                upper[:, r + 8:], mixed, (((0,), (0,)), ((), ())), precision=HIGH, preferred_element_type=F32
            )
            spot = lax.broadcasted_iota(jnp.int32, (n, rank), 1)
            old = jnp.where((spot >= r) & (spot < r + 8), 0.0, work[r + 8:, :])
            work[r + 8:, :] = old - low


def inverse_stage(gram):
    return pl.pallas_call(
        inverse_kernel,
        name="inverse",
        out_shape=jax.ShapeDtypeStruct(gram.shape, F32),
        in_specs=[pl.BlockSpec(memory_space=pltpu.VMEM)],
        out_specs=pl.BlockSpec(memory_space=pltpu.VMEM),
        scratch_shapes=[pltpu.VMEM(gram.shape, F32)],
    )(gram)


def right_kernel(
    n_dp, n_mp,
    mom_hbm, tile_hbm, scale_ref, factor_ref, left_ref, tri_ref,
    ortho_ref, low_ref, inv_ref, share_ref,
    mom, tile, part, part_low, core_in, core_out, plane_in, mine, theirs, low, sq_z, sq_p,
    sem_in, sem_core, sem_plane, sem_pair, sem_gather, sem_sz, sem_sp,
):
    place = Place(n_dp, n_mp)
    rows, cols = mom.shape
    share, rank = share_ref.shape
    block = 2 * share
    loads = [
        pltpu.make_async_copy(mom_hbm, mom, sem_in.at[0]),
        pltpu.make_async_copy(tile_hbm, tile, sem_in.at[1]),
    ]
    for load in loads:
        load.start()
    plane, zline = place.plane_peers(), place.z_peers()
    greet(plane + zline + [place.sibling()])
    ortho = lax.dot_general(
        left_ref[...], tri_ref[...], (((1,), (1,)), ((), ())), precision=HIGH, preferred_element_type=F32
    ).astype(BF16)
    ortho_ref[...] = ortho
    factor = factor_ref[0:1, :]
    for load in loads:
        load.wait()
    step = 256
    for t in range(cols // step):
        at = slice(t * step, (t + 1) * step)
        grad = jnp.concatenate(
            [
                tile[b * BLOCK:(b + 1) * BLOCK, at] * scale_ref[b:b + 1, at].astype(BF16)
                for b in range(rows // BLOCK)
            ],
            axis=0,
        )
        both = (((0,), (0,)), ((), ()))
        mom_part = lax.dot_general(mom[:, at], ortho, both, preferred_element_type=F32)
        grad_part = lax.dot_general(grad, ortho, both, preferred_element_type=F32)
        total = mom_part + factor * grad_part
        part[at, :] = total
        part_low[at, :] = total.astype(BF16)

    def rows_of(chip):
        return pl.ds(pl.multiple_of(chip * block, 16), block)

    core_copies = []
    for i in range(place.half):
        copy = remote(
            part_low.at[rows_of(place.to_chip(i, place.other))], core_in.at[i],
            sem_core.at[0, i], sem_core.at[1, i], place.sibling(),
        )
        copy.start()
        core_copies.append(copy)
    plane_copies = []
    for i in range(place.half):
        chip = place.to_chip(i, place.core)
        copy = remote(
            core_out.at[i], plane_in.at[i], sem_plane.at[0, i], sem_plane.at[1, i], place.dev(place.z, chip, place.core)
        )
        core_copies[i].wait_recv()
        total = part[rows_of(chip)] + core_in[i].astype(F32)
        if i == 0:
            mine[...] = total
        core_out[i] = total.astype(BF16)
        if i == 0:
            pl.when(place.core == 1)(copy.start)
        else:
            copy.start()
        plane_copies.append(copy)

    def first():
        plane_copies[0].wait_recv()
        mine[...] = plane_in[0].astype(F32)

    pl.when(place.core == 1)(first)
    acc = mine[...]
    for i in range(1, place.half):
        plane_copies[i].wait_recv()
        acc = acc + plane_in[i].astype(F32)
    mine[...] = acc
    pair = remote(mine, theirs, sem_pair.at[0], sem_pair.at[1], place.sibling())
    pair.start()
    pair.wait_recv()
    total = mine[...] + theirs[...]
    theirs[...] = total
    low[rows_of(place.chip)] = total.astype(BF16)
    gather_send(place, low, block, sem_gather)
    sq = jnp.sum((total * total).reshape(block // 8, 8, rank), axis=0)
    sq_z[place.z] = sq
    sz = exchange(place, zline, lambda k: sq_z.at[place.z], sq_z, sem_sz, place.z)
    share_ref[...] = theirs[pl.ds(pl.multiple_of(place.core * share, 8), share)]
    for copy in sz:
        copy.wait_recv()
    sq_p[place.chip] = jnp.sum(sq_z[...], axis=0)
    sp = exchange(place, plane, lambda k: sq_p.at[place.chip], sq_p, sem_sp, place.chip)
    for i in range(place.half):
        gather_forward(place, low, block, sem_gather, i)
    for copy in sp:
        copy.wait_recv()
    squares = jnp.sum(jnp.sum(sq_p[...], axis=0), axis=0, keepdims=True)
    inv_ref[...] = jnp.broadcast_to(lax.rsqrt(squares + EPSILON), inv_ref.shape)
    gather_finish(place, low, block, sem_gather)
    low_ref[...] = low[...]
    for copy in core_copies + plane_copies[1:] + [pair] + sz + sp:
        copy.wait_send()
    pl.when(place.core == 1)(plane_copies[0].wait_send)


def right_stage(n_dp, n_mp, share, momentum, tile_values, scale, factor, left, tri):
    rows, cols = momentum.shape
    rank = left.shape[1]
    chips = n_mp // 2
    half = chips // 2
    block = 2 * share
    vmem = pl.BlockSpec(memory_space=pltpu.VMEM)
    hbm = pl.BlockSpec(memory_space=pl.ANY)
    dma = pltpu.SemaphoreType.DMA
    return pl.pallas_call(
        functools.partial(right_kernel, n_dp, n_mp),
        name="right",
        out_shape=(
            jax.ShapeDtypeStruct((rows, rank), BF16),
            jax.ShapeDtypeStruct((cols, rank), BF16),
            jax.ShapeDtypeStruct((8, 128), F32),
            jax.ShapeDtypeStruct((share, rank), F32),
        ),
        in_specs=[hbm, hbm, vmem, vmem, vmem, vmem],
        out_specs=(vmem,) * 4,
        scratch_shapes=[
            pltpu.VMEM((rows, cols), BF16),
            pltpu.VMEM((rows, cols), BF16),
            pltpu.VMEM((cols, rank), F32),
            pltpu.VMEM((cols, rank), BF16),
            pltpu.VMEM((half, block, rank), BF16),
            pltpu.VMEM((half, block, rank), BF16),
            pltpu.VMEM((half, block, rank), BF16),
            pltpu.VMEM((block, rank), F32),
            pltpu.VMEM((block, rank), F32),
            pltpu.VMEM((cols, rank), BF16),
            pltpu.VMEM((n_dp, 8, 128), F32),
            pltpu.VMEM((chips, 8, 128), F32),
            dma((2,)),
            dma((2, half)),
            dma((2, half)),
            dma((2,)),
            dma((4, half)),
            dma((2, n_dp - 1)),
            dma((2, chips - 1)),
        ],
        compiler_params=pltpu.CompilerParams(
            collective_id=1, has_side_effects=True, vmem_limit_bytes=VMEM_LIMIT
        ),
    )(momentum, tile_values, scale, factor, left, tri)


def finish_kernel(unit, mom, tile, scale, factor, ortho, low, inv, share, new, upd, share_out):
    rows = mom.shape[0]
    base = ortho[...]
    both = (((1,), (1,)), ((), ()))
    correction = lax.dot_general(base, low[...], both, preferred_element_type=F32)
    scaled = (base.astype(F32) * inv[0:1, :]).astype(BF16)
    direction = lax.dot_general(scaled, low[...], both, preferred_element_type=F32)
    upd[...] = (unit * direction).astype(BF16)
    f = factor[0, 0]
    for b in range(rows // BLOCK):
        at = slice(b * BLOCK, (b + 1) * BLOCK)
        grad = tile[at, :].astype(F32) * scale[b:b + 1, :]
        new[at, :] = (mom[at, :].astype(F32) + f * grad - (1.0 - RETAIN) * correction[at, :]).astype(BF16)

    @pl.when(pl.program_id(0) == 0)
    def _():
        share_out[...] = share[...]


def finish_stage(unit, momentum, tile_values, scale, factor, ortho, low, inv, share):
    rows, cols = momentum.shape
    rank = ortho.shape[1]
    step = 256
    wide = pl.BlockSpec((rows, step), lambda i: (0, i))

    def whole(a):
        return pl.BlockSpec(a.shape, lambda i: (0, 0))

    return pl.pallas_call(
        functools.partial(finish_kernel, unit),
        name="finish",
        grid=(cols // step,),
        out_shape=(
            jax.ShapeDtypeStruct((rows, cols), BF16),
            jax.ShapeDtypeStruct((rows, cols), BF16),
            jax.ShapeDtypeStruct(share.shape, F32),
        ),
        in_specs=[
            wide, wide,
            pl.BlockSpec((scale.shape[0], step), lambda i: (0, i)),
            pl.BlockSpec(memory_space=pltpu.SMEM),
            whole(ortho),
            pl.BlockSpec((step, rank), lambda i: (i, 0)),
            whole(inv), whole(share),
        ],
        out_specs=(wide, wide, whole(share)),
        compiler_params=pltpu.CompilerParams(vmem_limit_bytes=VMEM_LIMIT),
    )(momentum, tile_values, scale, factor, ortho, low, inv, share)


def body(n_dp, n_mp, momentum, tile_values, exponents, overflow, right_prev):
    rows, cols = momentum.shape
    share, rank = right_prev.shape
    unit = math.sqrt(rows * n_mp * cols * n_dp / rank)
    gram, left, factor, scale = left_stage(n_dp, n_mp, momentum, tile_values, exponents, overflow, right_prev)
    tri = inverse_stage(gram)
    ortho, low, inv, own = right_stage(n_dp, n_mp, share, momentum, tile_values, scale, factor, left, tri)
    new, update, right_out = finish_stage(unit, momentum, tile_values, scale, factor, ortho, low, inv, own)
    return new, right_out, update


def solution(mesh):
    in_specs = (P("mp", "dp"), P("mp", "dp"), P("mp", "dp"), P("mp", "dp"), P(("dp", "mp"), None))
    out_specs = (P("mp", "dp"), P(("dp", "mp"), None), P("mp", "dp"))
    step = functools.partial(body, mesh.shape["dp"], mesh.shape["mp"])
    return jax.shard_map(step, mesh=mesh, in_specs=in_specs, out_specs=out_specs, check_vma=False)
```

time: 478 us -> 100 us (0.21)
  waiting for transfers between devices: 289 us -> 0 us
  blocking collectives: 120 us -> 0 us
  Pallas kernels: 0 us -> 91.1 us
  other arithmetic: 29.1 us -> 0 us
  between operations: 15.2 us -> 1.32 us
  matrix products: 13.7 us -> 0 us
    psum x3 -> x0, waiting for transfers between devices: 289 us -> none  [the longest x1 115 us: body(): lax.psum(trans_dot(mom_cols, ortho_low) + factor * trans_dot(grad_cols, o...]
    psum x2 -> x0, blocking collectives: 95 us -> none  [the longest x1 81.3 us: body(): lax.psum(jnp.sum((overflow == 0).astype(jnp.float32)), ('dp', 'mp'))]
    pallas_call x0 -> x4, Pallas kernels: none -> 91.1 us  [the longest x1 46.9 us: left_stage(): pl.pallas_call(functools.partial(left_kernel, n_dp, n_mp), name='left', o...]
    all_gather x1 -> x0, blocking collectives: 25.5 us -> none  [body(): lax.all_gather(right_prev.astype(jnp.bfloat16), 'mp', axis=0, tiled=True)]
    another operation x5 -> x0, other arithmetic: 23.5 us -> none  [the longest x3 12.4 us: body(): lower_tri = jnp.linalg.cholesky(lax.psum(gram_local, 'mp'))]
    dot_general x7 -> x0, matrix products: 12.5 us -> none  [the longest x2 5.38 us: outer_dot(): lax.dot_general(left_mat, right_mat, (((1,), (1,)), ((), ())), preferred_...]
    unnamed x10 -> x20, local copies, waits for them, and re-layouts: 0.96 us -> 7.21 us
  transfers between devices with their start and end apart: 3 -> 0, of which waited for: 3 -> 0; matrix products, arithmetic and copies ran while one was open for 0% -> 0% of each run, Pallas kernels for 0% -> 0%
where the time goes in v1:
time: 100 us; the launch traced here: 99.6 us
  Pallas kernels  91.1 us (91%)
  local copies, waits for them, and re-layouts  7.21 us (7%)
  between operations  1.32 us (1%)
    pallas_call x1, Pallas kernels, left_stage(): pl.pallas_call(functools.partial(left_kernel, n_dp, n_mp), name='left', o...  46.9 us
    pallas_call x1, Pallas kernels, right_stage(): pl.pallas_call(functools.partial(right_kernel, n_dp, n_mp), name='right',...  27.4 us
    pallas_call x1, Pallas kernels, inverse_stage(): pl.pallas_call(inverse_kernel, name='inverse', out_shape=jax.ShapeDtypeSt...  9.38 us
    pallas_call x1, Pallas kernels, finish_stage(): pl.pallas_call(functools.partial(finish_kernel, unit), name='finish', gri...  7.42 us
    unnamed x20, local copies, waits for them, and re-layouts  7.21 us

profile of v1, /device:TPU:1, one launch (start us, length us, event | category | flops | bytes accessed | tf_op | source)
XLA Modules:
  0.0 99.6 jit_solution(3138700565078573102)
XLA Ops:
  1.3 0.0 copy-start
  1.3 1.4 %copy-done = bf16[256,3328]{1,0:T(8,128)(2,1)S(1)} copy-done((bf16[256,3328]{1,0:T(8,128)(2,1)S(1)}, bf16[256,3328]{1,0:T(8,128)(2,1)}, u32[]{:S(2)}) %copy-start) | copy-done | bytes 1703960
  2.7 0.0 copy-start.2
  2.7 1.5 %copy-done.2 = bf16[256,3328]{1,0:T(8,128)(2,1)S(1)} copy-done((bf16[256,3328]{1,0:T(8,128)(2,1)S(1)}, bf16[256,3328]{1,0:T(8,128)(2,1)}, u32[]{:S(2)}) %copy-start.2) | copy-done | bytes 1703960
  4.2 0.0 copy-start.8
  4.2 0.8 copy-done.8
  5.0 0.0 copy-start.9
  5.0 0.7 copy-done.9
  5.7 0.0 copy-start.1
  5.7 0.0 copy-start.3
  5.7 46.9 %left.1 = (f32[128,128]{1,0:T(8,128)S(1)}, f32[256,128]{1,0:T(8,128)S(1)}, f32[8,128]{1,0:T(8,128)S(1)}, f32[2,3328]{1,0:T(2,128)S(1)}) custom-call(bf16[256,3328]{1,0:T(8,128)(2,1)S(1)} %copy-done, bf16[256,3328]{1,0:T(8,128)(2,1)S(1)} %copy-done.2, s32[2,26]{1,0:T(2,128)S(1)} %copy-done.9, s32[1,1]{1,0:T(1,128)S(6)} %copy.8.over_ref, f32[104,128]{1,0:T(8,128)S(1)} %copy-done.8), custom_call_target="tpu_custom_call" | custom-call | tf_op jit(solution)/shard_map/left/pallas_call | solution.py:289
  52.5 0.0 copy-start.5
  52.6 0.6 copy-done.5
  53.2 0.0 copy-start.7
  53.2 0.6 copy-done.7
  53.8 9.4 %inverse.1.tri_ref = f32[128,128]{1,0:T(8,128)} custom-call(f32[128,128]{1,0:T(8,128)} %copy-done.7), custom_call_target="tpu_custom_call" | custom-call | tf_op jit(solution)/shard_map/inverse/pallas_call | solution.py:382
  63.2 0.0 copy-done.1
  63.2 0.0 copy-done.3
  63.2 0.0 copy-start.4
  63.2 0.8 copy-done.4
  64.0 0.0 copy-start.6
  64.0 0.7 copy-done.6
  64.8 27.4 %right.1 = (bf16[256,128]{1,0:T(8,128)(2,1)S(1)}, bf16[3328,128]{1,0:T(8,128)(2,1)S(1)}, f32[8,128]{1,0:T(8,128)S(1)}, f32[104,128]{1,0:T(8,128)S(1)}) custom-call(bf16[256,3328]{1,0:T(8,128)(2,1)S(1)} %copy-done.1, bf16[256,3328]{1,0:T(8,128)(2,1)S(1)} %copy-done.3, f32[2,3328]{1,0:T(2,128)S(1)} %copy-done.6, ...), custom_call_target="tpu_custom_call" | custom-call | tf_op jit(solution)/shard_map/right/pallas_call | solution.py:510
  92.2 7.4 %finish.1 = (bf16[256,3328]{1,0:T(8,128)(2,1)}, bf16[256,3328]{1,0:T(8,128)(2,1)}, f32[104,128]{1,0:T(8,128)}) custom-call(bf16[256,3328]{1,0:T(8,128)(2,1)S(1)} %copy-done.1, bf16[256,3328]{1,0:T(8,128)(2,1)S(1)} %copy-done.3, f32[2,3328]{1,0:T(2,128)S(1)} %copy-done.6, f32[8,128]{1,0:T(8,128)S(1)} %get-tuple-element.15.factor_ref.factor, ...), custom_call_target="tpu_custom_call" | custom-call | tf_op jit(solution)/shard_map/finish/pallas_call | solution.py:576
Async XLA Ops:
  1.3 1.5 %copy-start = (bf16[256,3328]{1,0:T(8,128)(2,1)S(1)}, bf16[256,3328]{1,0:T(8,128)(2,1)}, u32[]{:S(2)}) copy-start(bf16[256,3328]{1,0:T(8,128)(2,1)} %mom.1) | copy-start | bytes 5111812
  2.7 1.5 %copy-start.2 = (bf16[256,3328]{1,0:T(8,128)(2,1)S(1)}, bf16[256,3328]{1,0:T(8,128)(2,1)}, u32[]{:S(2)}) copy-start(bf16[256,3328]{1,0:T(8,128)(2,1)} %tile.1) | copy-start | bytes 5111812
  4.2 0.8 copy-start.8
  5.0 0.7 copy-start.9
  5.7 57.5 %copy-start.1 = (bf16[256,3328]{1,0:T(8,128)(2,1)S(1)}, bf16[256,3328]{1,0:T(8,128)(2,1)}, u32[]{:S(2)}) copy-start(bf16[256,3328]{1,0:T(8,128)(2,1)} %mom.1) | copy-start | bytes 5111812
  5.7 57.5 %copy-start.3 = (bf16[256,3328]{1,0:T(8,128)(2,1)S(1)}, bf16[256,3328]{1,0:T(8,128)(2,1)}, u32[]{:S(2)}) copy-start(bf16[256,3328]{1,0:T(8,128)(2,1)} %tile.1) | copy-start | bytes 5111812
  52.5 0.6 copy-start.5
  53.2 0.6 copy-start.7
  63.2 0.8 copy-start.4
  64.0 0.7 copy-start.6

commit v2 on v1

v2 whole, which is shorter than its diff:
```python
import functools
import math

import jax
import jax.numpy as jnp
from jax import lax
from jax.experimental import pallas as pl
from jax.experimental.pallas import tpu as pltpu
from jax.sharding import PartitionSpec as P

MESH = pl.DeviceIdType.MESH
F32 = jnp.float32
BF16 = jnp.bfloat16
HIGH = lax.Precision.HIGHEST
BLOCK = 128
EPSILON = 1e-06
RETAIN = 0.95
VMEM_LIMIT = 32 * 1024 * 1024


class Place:
    def __init__(self, n_dp, n_mp):
        self.nz = n_dp
        self.chips = n_mp // 2
        self.ny = int(round(math.sqrt(self.chips)))
        self.nx = self.chips // self.ny
        self.half = self.chips // 2
        mp = lax.axis_index("mp")
        self.z = lax.axis_index("dp")
        self.core = lax.rem(mp, 2)
        self.other = 1 - self.core
        self.chip = mp // 2
        self.x = self.chip // self.ny
        self.y = lax.rem(self.chip, self.ny)

    def chip_at(self, dx, dy):
        x = lax.rem(self.x + dx + self.nx, self.nx)
        y = lax.rem(self.y + dy + self.ny, self.ny)
        return x * self.ny + y

    def offset(self, i, parity):
        dx = i // (self.ny // 2)
        dy = 2 * (i % (self.ny // 2)) + lax.rem(dx + parity, 2)
        return dx, dy

    def to_chip(self, i, parity):
        dx, dy = self.offset(i, parity)
        return self.chip_at(dx, dy)

    def from_chip(self, i, parity):
        dx, dy = self.offset(i, parity)
        return self.chip_at(-dx, -dy)

    def z_at(self, dz):
        return lax.rem(self.z + dz, self.nz)

    def dev(self, z, chip, core):
        return (z, chip * 2 + core)

    def sibling(self):
        return self.dev(self.z, self.chip, self.other)

    def plane_peers(self):
        return [
            self.dev(self.z, self.chip_at(dx, dy), self.core)
            for dx in range(self.nx)
            for dy in range(self.ny)
            if dx or dy
        ]

    def z_peers(self):
        return [self.dev(self.z_at(dz), self.chip, self.core) for dz in range(1, self.nz)]

    def zc_peers(self):
        return [
            self.dev(self.z_at(dz), self.chip, self.core if dc == 0 else self.other)
            for dz in range(self.nz)
            for dc in range(2)
            if dz or dc
        ]


def remote(src, dst, send, recv, dev):
    return pltpu.make_async_remote_copy(
        src_ref=src, dst_ref=dst, send_sem=send, recv_sem=recv, device_id=dev, device_id_type=MESH
    )


def greet(peers):
    barrier = pltpu.get_barrier_semaphore()
    for dev in peers:
        pl.semaphore_signal(barrier, inc=1, device_id=dev, device_id_type=MESH)
    pl.semaphore_wait(barrier, len(peers))


def exchange(place, peers, src_of, dst, sems, slot):
    copies = [
        remote(src_of(k), dst.at[slot], sems.at[0, k], sems.at[1, k], dev) for k, dev in enumerate(peers)
    ]
    for copy in copies:
        copy.start()
    return copies


def gather_send(place, buf, rows, sems):
    block = buf.at[pl.ds(pl.multiple_of(place.chip * rows, 16), rows)]
    for i in range(place.half):
        copy = remote(
            block, block, sems.at[0, i], sems.at[1, i], place.dev(place.z, place.to_chip(i, place.core), place.core)
        )
        if i == 0:
            pl.when(place.core == 1)(copy.start)
        else:
            copy.start()


def gather_forward(place, buf, rows, sems, i):
    start = pl.multiple_of(place.from_chip(i, place.core) * rows, 16)
    block = buf.at[pl.ds(start, rows)]

    def go():
        remote(block, block, sems.at[0, i], sems.at[1, i], place.sibling()).wait_recv()
        remote(block, block, sems.at[2, i], sems.at[3, i], place.sibling()).start()

    if i == 0:
        pl.when(place.core == 1)(go)
    else:
        go()


def gather_finish(place, buf, rows, sems):
    for i in range(place.half):
        start = pl.multiple_of(place.from_chip(i, place.other) * rows, 16)
        block = buf.at[pl.ds(start, rows)]
        copy = remote(block, block, sems.at[2, i], sems.at[3, i], place.sibling())
        if i == 0:
            pl.when(place.core == 0)(copy.wait_recv)
        else:
            copy.wait_recv()
    for i in range(place.half):
        block = buf.at[pl.ds(0, rows)]
        sent = remote(block, block, sems.at[0, i], sems.at[1, i], place.sibling())
        passed = remote(block, block, sems.at[2, i], sems.at[3, i], place.sibling())

        def done(sent=sent, passed=passed):
            sent.wait_send()
            passed.wait_send()

        if i == 0:
            pl.when(place.core == 1)(done)
        else:
            done()


def invert(work, out_ref):
    rank = work.shape[0]
    lanes = lax.broadcasted_iota(jnp.int32, (8, rank), 1)
    for r in range(0, rank, 8):
        row = [work[r + i:r + i + 1, :] for i in range(8)]
        a = [[jnp.broadcast_to(row[i][:, r + j:r + j + 1], (1, rank)) for j in range(i + 1)] for i in range(8)]
        e = [[None] * 8 for _ in range(8)]
        for j in range(8):
            s = lax.rsqrt(a[j][j])
            s = s * (1.5 - 0.5 * a[j][j] * s * s)
            e[j][j] = s
            for k in range(j):
                e[j][k] = e[j][k] * s
            for i in range(j + 1, 8):
                m = a[i][j] * s
                a[i][j] = m
                for k in range(j + 1):
                    t = m * e[j][k]
                    e[i][k] = -t if e[i][k] is None else e[i][k] - t
            for i in range(j + 1, 8):
                for k in range(j + 1, i + 1):
                    a[i][k] = a[i][k] - a[i][j] * a[k][j]
        upper, mixed = [], []
        lane = lanes[0:1]
        for i in range(8):
            total = e[i][0] * row[0]
            for j in range(1, i + 1):
                total = total + e[i][j] * row[j]
            inv = total
            for j in range(8):
                here = lane == r + j
                inv = jnp.where(here, e[i][j] if j <= i else 0.0, inv)
            upper.append(total)
            mixed.append(jnp.where(lane < r + 8, inv, total))
        upper = jnp.concatenate(upper, axis=0)
        mixed = jnp.concatenate(mixed, axis=0)
        out_ref[r:r + 8, :] = jnp.where(lanes < r + 8, mixed, 0.0)
        n = rank - r - 8
        if n:
            low = lax.dot_general(
                upper[:, r + 8:], mixed, (((0,), (0,)), ((), ())), precision=HIGH, preferred_element_type=F32
            )
            spot = lax.broadcasted_iota(jnp.int32, (n, rank), 1)
            old = jnp.where((spot >= r) & (spot < r + 8), 0.0, work[r + 8:, :])
            work[r + 8:, :] = old - low


def mega_kernel(
    n_dp, n_mp,
    mom_hbm, tile_hbm, exps_hbm, prev_hbm, over_ref,
    ortho_ref, low_ref, inv_ref, share_ref, sum_ref,
    mom, tile, exps, pair, right, mom_t, grad_t, flag_z, flag_c, flag_p,
    part, left_in, left, gram, gram_zc, gram_p, gram_all, work, tri,
    full, full_low, core_in, core_out, plane_in, mine, theirs, sq_z, sq_p,
    sem_in, sem_pair, sem_gather, sem_fz, sem_fc, sem_fp, sem_lr, sem_lg, sem_gr, sem_gp, sem_gg,
    sem_core, sem_plane, sem_sum, sem_low, sem_sz, sem_sp,
):
    place = Place(n_dp, n_mp)
    rows, cols = mom.shape
    share, rank = share_ref.shape
    block = 2 * share
    my_share = pl.ds(pl.multiple_of(place.core * share, 8), share)
    loads = [
        pltpu.make_async_copy(src, dst, sem_in.at[k])
        for k, (src, dst) in enumerate(
            [(prev_hbm, pair.at[my_share]), (exps_hbm, exps), (mom_hbm, mom), (tile_hbm, tile)]
        )
    ]
    for load in loads:
        load.start()
    plane, zline, zc = place.plane_peers(), place.z_peers(), place.zc_peers()
    greet(plane + zc)

    loads[0].wait()
    pair_copy = remote(pair.at[my_share], pair.at[my_share], sem_pair.at[0], sem_pair.at[1], place.sibling())
    pair_copy.start()
    kept = jnp.where(over_ref[0, 0] == 0, 1.0, 0.0).astype(F32)
    flag_z[place.z] = jnp.full((8, 128), kept, F32)
    fz = exchange(place, zline, lambda k: flag_z.at[place.z], flag_z, sem_fz, place.z)
    pair_copy.wait_recv()
    pending = [pair_copy] + fz
    right[pl.ds(pl.multiple_of(place.chip * block, 16), block)] = pair[...].astype(BF16)
    gather_send(place, right, block, sem_gather)

    loads[1].wait()
    scales = jnp.exp2(exps[...].astype(F32)).astype(BF16).astype(F32) * kept
    loads[2].wait()
    loads[3].wait()
    for j in range(cols // BLOCK):
        at = slice(j * BLOCK, (j + 1) * BLOCK)
        for b in range(rows // BLOCK):
            scale = jnp.broadcast_to(scales[b:b + 1, j:j + 1], (1, BLOCK)).astype(BF16)
            tile[b * BLOCK:(b + 1) * BLOCK, at] = tile[b * BLOCK:(b + 1) * BLOCK, at] * scale

    for copy in fz:
        copy.wait_recv()
    flag_c[place.core] = jnp.sum(flag_z[...], axis=0)
    fc = remote(flag_c.at[place.core], flag_c.at[place.core], sem_fc.at[0], sem_fc.at[1], place.sibling())
    fc.start()
    for i in range(place.half // 2):
        gather_forward(place, right, block, sem_gather, i)
    fc.wait_recv()
    flag_p[place.chip] = flag_c[0] + flag_c[1]
    fp = exchange(place, plane, lambda k: flag_p.at[place.chip], flag_p, sem_fp, place.chip)
    for i in range(place.half // 2, place.half):
        gather_forward(place, right, block, sem_gather, i)
    gather_finish(place, right, block, sem_gather)
    for copy in fp:
        copy.wait_recv()
    healthy = jnp.sum(flag_p[...], axis=0)
    factor = (float(n_dp * n_mp) / jnp.maximum(healthy, 1.0))[0:1, :]
    pending += [fc] + fp

    mom_part = jnp.dot(mom[...], right[...], preferred_element_type=F32)
    grad_part = jnp.dot(tile[...], right[...], preferred_element_type=F32)
    part[...] = mom_part + factor * grad_part

    rz = rows // place.nz
    lr = []
    for dz in range(1, place.nz):
        z2 = place.z_at(dz)
        copy = remote(
            part.at[pl.ds(pl.multiple_of(z2 * rz, 8), rz)], left_in.at[dz - 1],
            sem_lr.at[0, dz - 1], sem_lr.at[1, dz - 1], place.dev(z2, place.chip, place.core),
        )
        copy.start()
        lr.append(copy)
    for j in range(cols // BLOCK):
        at = slice(j * BLOCK, (j + 1) * BLOCK)
        mom_t[at, :] = mom[:, at].T
        grad_t[at, :] = tile[:, at].T
    for b in range(0, rows, 16):
        at = slice(b, b + 16)
        wide = jnp.broadcast_to(factor[:, 0:1], (1, cols))
        sum_ref[at, :] = mom[at, :].astype(F32) + wide * tile[at, :].astype(F32)
    own = pl.ds(pl.multiple_of(place.z * rz, 8), rz)
    acc = part[own]
    for k, copy in enumerate(lr):
        copy.wait_recv()
        acc = acc + left_in[k]
    left[own] = acc
    pending += lr
    gram[...] = lax.dot_general(acc, acc, (((0,), (0,)), ((), ())), precision=HIGH, preferred_element_type=F32)

    gs = gram.shape[0] // (2 * place.nz)
    gr = []
    k = 0
    for dz in range(place.nz):
        for dc in range(2):
            if dz or dc:
                z2, c2 = place.z_at(dz), place.core if dc == 0 else place.other
                copy = remote(
                    gram.at[pl.ds(pl.multiple_of((z2 * 2 + c2) * gs, 8), gs)], gram_zc.at[k],
                    sem_gr.at[0, k], sem_gr.at[1, k], place.dev(z2, place.chip, c2),
                )
                copy.start()
                gr.append(copy)
                k += 1
    piece = pl.ds(pl.multiple_of((place.z * 2 + place.core) * gs, 8), gs)
    acc = gram[piece]
    for k, copy in enumerate(gr):
        copy.wait_recv()
        acc = acc + gram_zc[k]
    gram_p[place.chip] = acc
    pending += gr
    gp = exchange(place, plane, lambda k: gram_p.at[place.chip], gram_p, sem_gp, place.chip)
    for copy in gp:
        copy.wait_recv()
    gram_all[piece] = jnp.sum(gram_p[...], axis=0)
    pending += gp
    gg = [
        remote(gram_all.at[piece], gram_all.at[piece], sem_gg.at[0, k], sem_gg.at[1, k], dev)
        for k, dev in enumerate(zc)
    ]
    for copy in gg:
        copy.start()
    lg = [
        remote(left.at[own], left.at[own], sem_lg.at[0, k], sem_lg.at[1, k], dev) for k, dev in enumerate(zline)
    ]
    for copy in lg:
        copy.start()
    for copy in gg:
        copy.wait_recv()
    pending += gg
    work[...] = gram_all[...]
    invert(work, tri)
    for copy in lg:
        copy.wait_recv()
    pending += lg

    ortho = lax.dot_general(
        left[...], tri[...], (((1,), (1,)), ((), ())), precision=HIGH, preferred_element_type=F32
    ).astype(BF16)
    ortho_ref[...] = ortho
    step = 256
    for t in range(cols // step):
        at = slice(t * step, (t + 1) * step)
        total = jnp.dot(mom_t[at, :], ortho, preferred_element_type=F32) + factor * jnp.dot(
            grad_t[at, :], ortho, preferred_element_type=F32
        )
        full[at, :] = total
        full_low[at, :] = total.astype(BF16)

    def rows_of(chip):
        return pl.ds(pl.multiple_of(chip * block, 16), block)

    core_copies = []
    for i in range(place.half):
        copy = remote(
            full_low.at[rows_of(place.to_chip(i, place.other))], core_in.at[i],
            sem_core.at[0, i], sem_core.at[1, i], place.sibling(),
        )
        copy.start()
        core_copies.append(copy)
    plane_copies = []
    for i in range(place.half):
        chip = place.to_chip(i, place.core)
        copy = remote(
            core_out.at[i], plane_in.at[i], sem_plane.at[0, i], sem_plane.at[1, i], place.dev(place.z, chip, place.core)
        )
        core_copies[i].wait_recv()
        total = full[rows_of(chip)] + core_in[i].astype(F32)
        if i == 0:
            mine[...] = total
        core_out[i] = total.astype(BF16)
        if i == 0:
            pl.when(place.core == 1)(copy.start)
        else:
            copy.start()
        plane_copies.append(copy)

    def first():
        plane_copies[0].wait_recv()
        mine[...] = plane_in[0].astype(F32)

    pl.when(place.core == 1)(first)
    acc = mine[...]
    for i in range(1, place.half):
        plane_copies[i].wait_recv()
        acc = acc + plane_in[i].astype(F32)
    mine[...] = acc
    pending += core_copies + plane_copies[1:]
    pl.when(place.core == 1)(plane_copies[0].wait_send)
    pair_sum = remote(mine, theirs, sem_sum.at[0], sem_sum.at[1], place.sibling())
    pair_sum.start()
    pair_sum.wait_recv()
    total = mine[...] + theirs[...]
    theirs[...] = total
    pending += [pair_sum]
    low_ref[rows_of(place.chip)] = total.astype(BF16)
    gather_send(place, low_ref, block, sem_low)
    sq = jnp.sum((total * total).reshape(block // 8, 8, rank), axis=0)
    sq_z[place.z] = sq
    sz = exchange(place, zline, lambda k: sq_z.at[place.z], sq_z, sem_sz, place.z)
    share_ref[...] = theirs[my_share]
    for copy in sz:
        copy.wait_recv()
    sq_p[place.chip] = jnp.sum(sq_z[...], axis=0)
    sp = exchange(place, plane, lambda k: sq_p.at[place.chip], sq_p, sem_sp, place.chip)
    for i in range(place.half):
        gather_forward(place, low_ref, block, sem_low, i)
    gather_finish(place, low_ref, block, sem_low)
    for copy in sp:
        copy.wait_recv()
    squares = jnp.sum(jnp.sum(sq_p[...], axis=0), axis=0, keepdims=True)
    inv_ref[...] = jnp.broadcast_to(lax.rsqrt(squares + EPSILON), inv_ref.shape)
    for copy in pending + sz + sp:
        copy.wait_send()


def mega_stage(n_dp, n_mp, momentum, tile_values, exponents, right_prev, overflow):
    rows, cols = momentum.shape
    share, rank = right_prev.shape
    chips = n_mp // 2
    half = chips // 2
    block = 2 * share
    rz = rows // n_dp
    gs = rank // (2 * n_dp)
    vmem = pl.BlockSpec(memory_space=pltpu.VMEM)
    hbm = pl.BlockSpec(memory_space=pltpu.HBM)
    dma = pltpu.SemaphoreType.DMA
    return pl.pallas_call(
        functools.partial(mega_kernel, n_dp, n_mp),
        name="mega",
        out_shape=(
            jax.ShapeDtypeStruct((rows, rank), BF16),
            jax.ShapeDtypeStruct((cols, rank), BF16),
            jax.ShapeDtypeStruct((8, 128), F32),
            jax.ShapeDtypeStruct((share, rank), F32),
            jax.ShapeDtypeStruct((rows, cols), F32),
        ),
        in_specs=[hbm] * 4 + [pl.BlockSpec(memory_space=pltpu.SMEM)],
        out_specs=(vmem,) * 5,
        scratch_shapes=[
            pltpu.VMEM((rows, cols), BF16),
            pltpu.VMEM((rows, cols), BF16),
            pltpu.VMEM(exponents.shape, jnp.int32),
            pltpu.VMEM((block, rank), F32),
            pltpu.VMEM((cols, rank), BF16),
            pltpu.VMEM((cols, rows), BF16),
            pltpu.VMEM((cols, rows), BF16),
            pltpu.VMEM((n_dp, 8, 128), F32),
            pltpu.VMEM((2, 8, 128), F32),
            pltpu.VMEM((chips, 8, 128), F32),
            pltpu.VMEM((rows, rank), F32),
            pltpu.VMEM((n_dp - 1, rz, rank), F32),
            pltpu.VMEM((rows, rank), F32),
            pltpu.VMEM((rank, rank), F32),
            pltpu.VMEM((2 * n_dp - 1, gs, rank), F32),
            pltpu.VMEM((chips, gs, rank), F32),
            pltpu.VMEM((rank, rank), F32),
            pltpu.VMEM((rank, rank), F32),
            pltpu.VMEM((rank, rank), F32),
            pltpu.VMEM((cols, rank), F32),
            pltpu.VMEM((cols, rank), BF16),
            pltpu.VMEM((half, block, rank), BF16),
            pltpu.VMEM((half, block, rank), BF16),
            pltpu.VMEM((half, block, rank), BF16),
            pltpu.VMEM((block, rank), F32),
            pltpu.VMEM((block, rank), F32),
            pltpu.VMEM((n_dp, 8, 128), F32),
            pltpu.VMEM((chips, 8, 128), F32),
            dma((4,)),
            dma((2,)),
            dma((4, half)),
            dma((2, n_dp - 1)),
            dma((2,)),
            dma((2, chips - 1)),
            dma((2, n_dp - 1)),
            dma((2, n_dp - 1)),
            dma((2, 2 * n_dp - 1)),
            dma((2, chips - 1)),
            dma((2, 2 * n_dp - 1)),
            dma((2, half)),
            dma((2, half)),
            dma((2,)),
            dma((4, half)),
            dma((2, n_dp - 1)),
            dma((2, chips - 1)),
        ],
        compiler_params=pltpu.CompilerParams(
            collective_id=0, has_side_effects=True, vmem_limit_bytes=VMEM_LIMIT
        ),
    )(momentum, tile_values, exponents, right_prev, overflow)


def finish_kernel(unit, sums, ortho, low, inv, share, new, upd, share_out, new_v, upd_v, sem):
    rows, cols = sums.shape
    step = 256
    base = ortho[...]
    scaled = (base.astype(F32) * inv[0:1, :]).astype(BF16)
    both = (((1,), (1,)), ((), ()))
    share_copy = pltpu.make_async_copy(share, share_out, sem.at[2, 0])
    share_copy.start()
    copies = [share_copy]
    for t in range(cols // step):
        at = slice(t * step, (t + 1) * step)
        piece = low[at, :]
        correction = lax.dot_general(base, piece, both, preferred_element_type=F32)
        new_v[:, at] = (sums[:, at] - (1.0 - RETAIN) * correction).astype(BF16)
        direction = lax.dot_general(scaled, piece, both, preferred_element_type=F32)
        upd_v[:, at] = (unit * direction).astype(BF16)
        for k, (src, dst) in enumerate([(new_v, new), (upd_v, upd)]):
            copy = pltpu.make_async_copy(src.at[:, at], dst.at[:, at], sem.at[k, t])
            copy.start()
            copies.append(copy)
    for copy in copies:
        copy.wait()


def finish_stage(unit, sums, ortho, low, inv, share):
    rows, cols = sums.shape
    vmem = pl.BlockSpec(memory_space=pltpu.VMEM)
    hbm = pl.BlockSpec(memory_space=pltpu.HBM)
    return pl.pallas_call(
        functools.partial(finish_kernel, unit),
        name="finish",
        out_shape=(
            jax.ShapeDtypeStruct((rows, cols), BF16),
            jax.ShapeDtypeStruct((rows, cols), BF16),
            jax.ShapeDtypeStruct(share.shape, F32),
        ),
        in_specs=[vmem] * 5,
        out_specs=(hbm,) * 3,
        scratch_shapes=[
            pltpu.VMEM((rows, cols), BF16),
            pltpu.VMEM((rows, cols), BF16),
            pltpu.SemaphoreType.DMA((3, cols // 256)),
        ],
        compiler_params=pltpu.CompilerParams(vmem_limit_bytes=VMEM_LIMIT),
    )(sums, ortho, low, inv, share)


def body(n_dp, n_mp, momentum, tile_values, exponents, overflow, right_prev):
    rows, cols = momentum.shape
    rank = right_prev.shape[1]
    unit = math.sqrt(rows * n_mp * cols * n_dp / rank)
    args = [
        pltpu.with_memory_space_constraint(a, pltpu.HBM)
        for a in (momentum, tile_values, exponents, right_prev)
    ]
    ortho, low, inv, own, sums = mega_stage(n_dp, n_mp, *args, overflow)
    new, update, right_out = finish_stage(unit, sums, ortho, low, inv, own)
    return new, right_out, update


def solution(mesh):
    in_specs = (P("mp", "dp"), P("mp", "dp"), P("mp", "dp"), P("mp", "dp"), P(("dp", "mp"), None))
    out_specs = (P("mp", "dp"), P(("dp", "mp"), None), P("mp", "dp"))
    step = functools.partial(body, mesh.shape["dp"], mesh.shape["mp"])
    return jax.shard_map(step, mesh=mesh, in_specs=in_specs, out_specs=out_specs, check_vma=False)
```

time: 100 us -> 82.2 us (0.82)
  Pallas kernels: 91.1 us -> 80.8 us
  local copies, waits for them, and re-layouts: 7.21 us -> 0 us
    pallas_call x4 -> x2, Pallas kernels: 91.1 us -> 80.8 us  [the longest x1 78.5 us: mega_stage(): pl.pallas_call(functools.partial(mega_kernel, n_dp, n_mp), name='mega', o...]
    unnamed x20 -> x0, local copies, waits for them, and re-layouts: 7.21 us -> none
where the time goes in v2:
time: 82.2 us; the launch traced here: 82.1 us
  Pallas kernels  80.8 us (98%)
  between operations  1.29 us (2%)
    pallas_call x1, Pallas kernels, mega_stage(): pl.pallas_call(functools.partial(mega_kernel, n_dp, n_mp), name='mega', o...  78.5 us
    pallas_call x1, Pallas kernels, finish_stage(): pl.pallas_call(functools.partial(finish_kernel, unit), name='finish', out...  2.31 us

profile of v2, /device:TPU:1, one launch (start us, length us, event | category | flops | bytes accessed | tf_op | source)
XLA Modules:
  0.0 82.1 jit_solution(10694831168446616300)
XLA Ops:
  1.3 78.5 %mega.1 = (bf16[256,128]{1,0:T(8,128)(2,1)S(1)}, bf16[3328,128]{1,0:T(8,128)(2,1)S(1)}, f32[8,128]{1,0:T(8,128)S(1)}, f32[104,128]{1,0:T(8,128)S(1)}, f32[256,3328]{1,0:T(8,128)S(1)}) custom-call(bf16[256,3328]{1,0:T(8,128)(2,1)} %mom_hbm.1, bf16[256,3328]{1,0:T(8,128)(2,1)} %tile_hbm.1, s32[2,26]{1,0:T(2,128)} %exps_hbm.1, f32[104,128]{1,0:T(8,128)} %prev_hbm.1, ...), custom_call_target="tpu_custom_call" | custom-call | tf_op jit(solution)/shard_map/mega/pallas_call | solution.py:436
  79.8 2.3 %finish.1 = (bf16[256,3328]{1,0:T(8,128)(2,1)}, bf16[256,3328]{1,0:T(8,128)(2,1)}, f32[104,128]{1,0:T(8,128)}) custom-call(f32[256,3328]{1,0:T(8,128)S(1)} %get-tuple-element.11.sums, bf16[256,128]{1,0:T(8,128)(2,1)S(1)} %get-tuple-element.12.ortho, bf16[3328,128]{1,0:T(8,128)(2,1)S(1)} %get-tuple-element.13.low, f32[8,128]{1,0:T(8,128)S(1)} %get-tuple-element.14.inv, ...), custom_call_target="tpu_custom_call" | custom-call | tf_op jit(solution)/shard_map/finish/pallas_call | solution.py:529

commit v3 on v2

v3 whole, which is shorter than its diff:
```python
import functools
import math

import jax
import jax.numpy as jnp
from jax import lax
from jax.experimental import pallas as pl
from jax.experimental.pallas import tpu as pltpu
from jax.sharding import PartitionSpec as P

MESH = pl.DeviceIdType.MESH
F32 = jnp.float32
BF16 = jnp.bfloat16
HIGH = lax.Precision.HIGHEST
BLOCK = 128
EPSILON = 1e-06
RETAIN = 0.95
VMEM_LIMIT = 32 * 1024 * 1024


def torus(a, n):
    return min(a % n, -a % n)


class Place:
    def __init__(self, n_dp, n_mp):
        self.nz = n_dp
        self.chips = n_mp // 2
        self.ny = int(round(math.sqrt(self.chips)))
        self.nx = self.chips // self.ny
        self.half = self.chips // 2
        mp = lax.axis_index("mp")
        self.z = lax.axis_index("dp")
        self.core = lax.rem(mp, 2)
        self.other = 1 - self.core
        self.chip = mp // 2
        x = self.chip // self.ny
        y = lax.rem(self.chip, self.ny)
        xs = [lax.rem(x + d, self.nx) * self.ny for d in range(self.nx)]
        ys = [lax.rem(y + d, self.ny) for d in range(self.ny)]
        offsets = sorted(
            ((dx, dy) for dx in range(self.nx) for dy in range(self.ny)),
            key=lambda o: -torus(o[0], self.nx) - torus(o[1], self.ny),
        )
        chips = {o: xs[o[0]] + ys[o[1]] for o in offsets}
        split = [[o for o in offsets if sum(o) % 2 == parity] for parity in range(2)]

        def pick(parity, sign):
            return [
                jnp.where(parity == 0, *(chips[(sign * o[0]) % self.nx, (sign * o[1]) % self.ny] for o in pair))
                for pair in zip(*split)
            ]

        self.sibling = (self.z, self.chip * 2 + self.other)
        self.to_mine, self.from_mine = pick(self.core, 1), pick(self.core, -1)
        self.to_other, self.from_other = pick(self.other, 1), pick(self.other, -1)
        self.plane = [chips[o] for o in offsets[:-1]]
        self.plane_peers = [(self.z, chip * 2 + self.core) for chip in self.plane]
        self.z_order = sorted(range(1, self.nz), key=lambda d: -torus(d, self.nz))
        self.zs = [lax.rem(self.z + d, self.nz) for d in self.z_order]
        self.z_peers = [(z, self.chip * 2 + self.core) for z in self.zs]
        self.zc_peers = [
            (z, self.chip * 2 + core) for z in self.zs for core in (self.core, self.other)
        ] + [self.sibling]

    def same_core(self, chip):
        return (self.z, chip * 2 + self.core)


def remote(src, dst, send, recv, dev):
    return pltpu.make_async_remote_copy(
        src_ref=src, dst_ref=dst, send_sem=send, recv_sem=recv, device_id=dev, device_id_type=MESH
    )


def exchange(peers, src_of, dst, sems):
    copies = [remote(src_of(k), dst, sems.at[0, k], sems.at[1, k], dev) for k, dev in enumerate(peers)]
    for copy in copies:
        copy.start()
    return copies


def start_all(copies, place):
    for copy in copies[:-1]:
        copy.start()
    pl.when(place.core == 1)(copies[-1].start)


class Gather:
    def __init__(self, place, buf, rows, sems):
        self.place = place

        def at(chip):
            return buf.at[pl.ds(pl.multiple_of(chip * rows, 16), rows)]

        mine = at(place.chip)
        self.sends = [
            remote(mine, mine, sems.at[0, i], sems.at[1, i], place.same_core(chip))
            for i, chip in enumerate(place.to_mine)
        ]
        self.arrivals = [
            remote(at(chip), at(chip), sems.at[0, i], sems.at[1, i], place.sibling)
            for i, chip in enumerate(place.from_mine)
        ]
        self.passes = [
            remote(at(chip), at(chip), sems.at[2, i], sems.at[3, i], place.sibling)
            for i, chip in enumerate(place.from_mine)
        ]
        self.passed = [
            remote(at(chip), at(chip), sems.at[2, i], sems.at[3, i], place.sibling)
            for i, chip in enumerate(place.from_other)
        ]

    def send(self):
        start_all(self.sends, self.place)

    def forward(self, i):
        def go():
            self.arrivals[i].wait_recv()
            self.passes[i].start()

        if i == self.place.half - 1:
            pl.when(self.place.core == 1)(go)
        else:
            go()

    def finish(self):
        for copy in self.passed[:-1]:
            copy.wait_recv()
        pl.when(self.place.core == 0)(self.passed[-1].wait_recv)

    def drain(self):
        for sent, passed in list(zip(self.sends, self.passes))[:-1]:
            sent.wait_send()
            passed.wait_send()

        def last():
            self.sends[-1].wait_send()
            self.passes[-1].wait_send()

        pl.when(self.place.core == 1)(last)


def invert(work, out_ref):
    rank = work.shape[0]
    size = 8
    lanes = lax.broadcasted_iota(jnp.int32, (size, rank), 1)
    lane = lanes[0:1]
    for r in range(0, rank, size):
        row = [work[r + i:r + i + 1, :] for i in range(size)]
        a = [[jnp.broadcast_to(row[i][:, r + j:r + j + 1], (1, rank)) for j in range(i + 1)] for i in range(size)]
        inside = (lane >= r) & (lane < r + size)
        row = [jnp.where(inside, jnp.where(lane == r + i, 1.0, 0.0), row[i]) for i in range(size)]
        e = [[None] * size for _ in range(size)]
        pivot, recip = [], []
        for j in range(size):
            pivot.append(a[j][j])
            recip.append(1.0 / a[j][j])
            for i in range(j + 1, size):
                m = a[i][j] * recip[j]
                for k in range(j + 1, i + 1):
                    a[i][k] = a[i][k] - m * a[k][j]
                for k in range(j):
                    e[i][k] = e[i][k] - m * e[j][k]
                e[i][j] = -m
        z = []
        for i in range(size):
            t = row[i]
            for j in range(i):
                t = t + e[i][j] * row[j]
            z.append(t)
        y = []
        zq = [z[i] * recip[i] for i in range(size)]
        for i in range(size):
            t = zq[i]
            for k in range(i + 1, size):
                t = t + e[k][i] * zq[k]
            y.append(t)
        out = jnp.concatenate([z[i] * lax.rsqrt(pivot[i]) for i in range(size)], axis=0)
        out_ref[r:r + size, :] = jnp.where(lanes < r + size, out, 0.0)
        for s in range(r + size, rank, size):
            old = work[s:s + size, :]
            acc = jnp.where((lanes >= r) & (lanes < r + size), 0.0, old)
            for k in range(size):
                acc = acc - jnp.broadcast_to(old[:, r + k:r + k + 1], (size, rank)) * y[k]
            work[s:s + size, :] = acc


def mega_kernel(
    n_dp, n_mp,
    mom_hbm, tile_hbm, exps_hbm, prev_hbm, over_ref,
    ortho_ref, low_ref, inv_ref, share_ref, sum_ref,
    both, exps, scale, pair, right, mom_t, grad_t, flag_z, flag_c, flag_p,
    part, left_in, left, gram, gram_p, gram_zc, gram_all, work, tri,
    core_send, core_in, core_out, plane_in, mine, theirs, sq_z, sq_p,
    sem_in, sem_pair, sem_gather, sem_fz, sem_fc, sem_fp, sem_lr, sem_lg, sem_gp, sem_gz, sem_gg,
    sem_core, sem_plane, sem_sum, sem_low, sem_sz, sem_sp,
):
    place = Place(n_dp, n_mp)
    rows, cols = mom_hbm.shape
    share, rank = share_ref.shape
    block = 2 * share
    my_share = pl.ds(pl.multiple_of(place.core * share, 8), share)
    loads = [
        pltpu.make_async_copy(src, dst, sem_in.at[k])
        for k, (src, dst) in enumerate(
            [
                (prev_hbm, pair.at[my_share]), (exps_hbm, exps),
                (mom_hbm, both.at[0:rows]), (tile_hbm, both.at[rows:2 * rows]),
            ]
        )
    ]
    for load in loads:
        load.start()
    barrier = pltpu.get_barrier_semaphore()
    friends = place.plane_peers + place.zc_peers
    for dev in friends:
        pl.semaphore_signal(barrier, inc=1, device_id=dev, device_id_type=MESH)
    kept = jnp.where(over_ref[0, 0] == 0, 1.0, 0.0).astype(F32)
    flag_z[place.z] = jnp.full((8, 128), kept, F32)
    loads[1].wait()
    scales = jnp.exp2(exps[...].astype(F32)).astype(BF16).astype(F32) * kept
    for j in range(cols // BLOCK):
        for b in range(rows // BLOCK):
            scale[b, :, j * BLOCK:(j + 1) * BLOCK] = jnp.broadcast_to(scales[b:b + 1, j:j + 1], (16, BLOCK)).astype(BF16)
    loads[0].wait()
    pl.semaphore_wait(barrier, len(friends))
    pending = []

    fz = exchange(place.z_peers, lambda k: flag_z.at[place.z], flag_z.at[place.z], sem_fz)
    pair_copy = remote(pair.at[my_share], pair.at[my_share], sem_pair.at[0], sem_pair.at[1], place.sibling)
    pair_copy.start()
    pair_copy.wait_recv()
    right[pl.ds(pl.multiple_of(place.chip * block, 16), block)] = pair[...].astype(BF16)
    gather = Gather(place, right, block, sem_gather)
    gather.send()

    loads[2].wait()
    loads[3].wait()

    def decode(j, carry):
        at = pl.ds(pl.multiple_of(j * BLOCK, BLOCK), BLOCK)
        for b in range(rows // BLOCK):
            factor_of = scale[b, :, at]
            for r in range(rows + b * BLOCK, rows + (b + 1) * BLOCK, 16):
                both[r:r + 16, at] = both[r:r + 16, at] * factor_of
        return carry

    lax.fori_loop(0, cols // BLOCK, decode, 0)

    for copy in fz:
        copy.wait_recv()
    flag_c[place.core] = jnp.sum(flag_z[...], axis=0)
    fc = remote(flag_c.at[place.core], flag_c.at[place.core], sem_fc.at[0], sem_fc.at[1], place.sibling)
    fc.start()
    fc.wait_recv()
    flag_p[place.chip] = flag_c[0] + flag_c[1]
    fp = exchange(place.plane_peers, lambda k: flag_p.at[place.chip], flag_p.at[place.chip], sem_fp)
    for i in range(place.half):
        gather.forward(i)
    gather.finish()
    for copy in fp:
        copy.wait_recv()
    healthy = jnp.sum(flag_p[...], axis=0)
    factor = (float(n_dp * n_mp) / jnp.maximum(healthy, 1.0))[0:1, :]
    pending += [pair_copy, fc] + fz + fp

    parts = jnp.dot(both[...], right[...], preferred_element_type=F32)
    part[...] = parts[:rows] + factor * parts[rows:]

    rz = rows // place.nz
    lr = []
    for k, z in enumerate(place.zs):
        copy = remote(
            part.at[pl.ds(pl.multiple_of(z * rz, 8), rz)], left_in.at[k], sem_lr.at[0, k], sem_lr.at[1, k],
            place.z_peers[k],
        )
        copy.start()
        lr.append(copy)

    def transpose(j, carry):
        at = pl.ds(pl.multiple_of(j * BLOCK, BLOCK), BLOCK)
        mom_t[at, :] = both[0:rows, at].T
        grad_t[at, :] = both[rows:2 * rows, at].T
        return carry

    lax.fori_loop(0, cols // BLOCK, transpose, 0)
    wide = jnp.broadcast_to(factor[:, 0:1], (16, BLOCK))

    def add(j, carry):
        at = pl.ds(pl.multiple_of(j * BLOCK, BLOCK), BLOCK)
        for r in range(0, rows, 16):
            sum_ref[r:r + 16, at] = both[r:r + 16, at].astype(F32) + wide * both[rows + r:rows + r + 16, at].astype(F32)
        return carry

    own = pl.ds(pl.multiple_of(place.z * rz, 8), rz)
    acc = part[own]
    for k, copy in enumerate(lr):
        copy.wait_recv()
        acc = acc + left_in[k]
    left[own] = acc
    pending += lr
    gram[...] = lax.dot_general(acc, acc, (((0,), (0,)), ((), ())), precision=HIGH, preferred_element_type=F32)

    gs = rank // place.chips
    piece = pl.ds(pl.multiple_of(place.chip * gs, 8), gs)
    gp = []
    for k, chip in enumerate(place.plane):
        copy = remote(
            gram.at[pl.ds(pl.multiple_of(chip * gs, 8), gs)], gram_p.at[k], sem_gp.at[0, k], sem_gp.at[1, k],
            place.plane_peers[k],
        )
        copy.start()
        gp.append(copy)
    acc = gram[piece]
    lax.fori_loop(0, cols // BLOCK, add, 0)
    for k, copy in enumerate(gp):
        copy.wait_recv()
        acc = acc + gram_p[k]
    pending += gp
    spot = place.z * 2 + place.core
    gram_zc[spot] = acc
    gz = exchange(place.zc_peers, lambda k: gram_zc.at[spot], gram_zc.at[spot], sem_gz)
    for copy in gz:
        copy.wait_recv()
    gram_all[piece] = jnp.sum(gram_zc[...], axis=0)
    pending += gz
    gg = exchange(place.plane_peers, lambda k: gram_all.at[piece], gram_all.at[piece], sem_gg)
    lg = exchange(place.z_peers, lambda k: left.at[own], left.at[own], sem_lg)
    for copy in gg:
        copy.wait_recv()
    pending += gg + lg
    work[...] = gram_all[...]
    invert(work, tri)
    for copy in lg:
        copy.wait_recv()

    ortho = lax.dot_general(
        left[...], tri[...], (((1,), (1,)), ((), ())), precision=HIGH, preferred_element_type=F32
    ).astype(BF16)
    ortho_ref[...] = ortho

    def rows_of(chip):
        return pl.ds(pl.multiple_of(chip * block, 16), block)

    def right_part(chip):
        at = rows_of(chip)
        return jnp.dot(mom_t[at, :], ortho, preferred_element_type=F32) + factor * jnp.dot(
            grad_t[at, :], ortho, preferred_element_type=F32
        )

    core_copies = []
    for i, chip in enumerate(place.to_other):
        core_send[i] = right_part(chip).astype(BF16)
        copy = remote(core_send.at[i], core_in.at[i], sem_core.at[0, i], sem_core.at[1, i], place.sibling)
        copy.start()
        core_copies.append(copy)
    plane_copies = []
    last = place.half - 1
    for i, chip in enumerate(place.to_mine):
        total = right_part(chip)
        core_copies[i].wait_recv()
        total = total + core_in[i].astype(F32)
        if i == last:
            mine[...] = total
        core_out[i] = total.astype(BF16)
        copy = remote(
            core_out.at[i], plane_in.at[i], sem_plane.at[0, i], sem_plane.at[1, i], place.same_core(chip)
        )
        if i == last:
            pl.when(place.core == 1)(copy.start)
        else:
            copy.start()
        plane_copies.append(copy)
    pending += core_copies + plane_copies[:-1]
    acc = None
    for i in range(last):
        plane_copies[i].wait_recv()
        got = plane_in[i].astype(F32)
        acc = got if acc is None else acc + got

    def own_last():
        mine[...] = mine[...] + acc

    def got_last():
        plane_copies[last].wait_recv()
        mine[...] = plane_in[last].astype(F32) + acc

    pl.when(place.core == 0)(own_last)
    pl.when(place.core == 1)(got_last)
    pair_sum = remote(mine, theirs, sem_sum.at[0], sem_sum.at[1], place.sibling)
    pair_sum.start()
    pair_sum.wait_recv()
    total = mine[...] + theirs[...]
    pending += [pair_sum]
    sq_z[place.z] = jnp.sum((total * total).reshape(block // 8, 8, rank), axis=0)
    sz = exchange(place.z_peers, lambda k: sq_z.at[place.z], sq_z.at[place.z], sem_sz)
    low_ref[rows_of(place.chip)] = total.astype(BF16)
    last_gather = Gather(place, low_ref, block, sem_low)
    last_gather.send()
    theirs[...] = total
    share_ref[...] = theirs[my_share]
    for copy in sz:
        copy.wait_recv()
    sq_p[place.chip] = jnp.sum(sq_z[...], axis=0)
    sp = exchange(place.plane_peers, lambda k: sq_p.at[place.chip], sq_p.at[place.chip], sem_sp)
    for i in range(place.half):
        last_gather.forward(i)
    last_gather.finish()
    for copy in sp:
        copy.wait_recv()
    squares = jnp.sum(jnp.sum(sq_p[...], axis=0), axis=0, keepdims=True)
    inv_ref[...] = jnp.broadcast_to(lax.rsqrt(squares + EPSILON), inv_ref.shape)
    for copy in pending + sz + sp:
        copy.wait_send()
    pl.when(place.core == 1)(plane_copies[last].wait_send)
    gather.drain()
    last_gather.drain()


def mega_stage(n_dp, n_mp, momentum, tile_values, exponents, right_prev, overflow):
    rows, cols = momentum.shape
    share, rank = right_prev.shape
    chips = n_mp // 2
    half = chips // 2
    block = 2 * share
    vmem = pl.BlockSpec(memory_space=pltpu.VMEM)
    hbm = pl.BlockSpec(memory_space=pltpu.HBM)
    dma = pltpu.SemaphoreType.DMA
    return pl.pallas_call(
        functools.partial(mega_kernel, n_dp, n_mp),
        name="mega",
        out_shape=(
            jax.ShapeDtypeStruct((rows, rank), BF16),
            jax.ShapeDtypeStruct((cols, rank), BF16),
            jax.ShapeDtypeStruct((8, 128), F32),
            jax.ShapeDtypeStruct((share, rank), F32),
            jax.ShapeDtypeStruct((rows, cols), F32),
        ),
        in_specs=[hbm] * 4 + [pl.BlockSpec(memory_space=pltpu.SMEM)],
        out_specs=(vmem,) * 5,
        scratch_shapes=[
            pltpu.VMEM((2 * rows, cols), BF16),
            pltpu.VMEM(exponents.shape, jnp.int32),
            pltpu.VMEM((rows // BLOCK, 16, cols), BF16),
            pltpu.VMEM((block, rank), F32),
            pltpu.VMEM((cols, rank), BF16),
            pltpu.VMEM((cols, rows), BF16),
            pltpu.VMEM((cols, rows), BF16),
            pltpu.VMEM((n_dp, 8, 128), F32),
            pltpu.VMEM((2, 8, 128), F32),
            pltpu.VMEM((chips, 8, 128), F32),
            pltpu.VMEM((rows, rank), F32),
            pltpu.VMEM((n_dp - 1, rows // n_dp, rank), F32),
            pltpu.VMEM((rows, rank), F32),
            pltpu.VMEM((rank, rank), F32),
            pltpu.VMEM((chips - 1, rank // chips, rank), F32),
            pltpu.VMEM((2 * n_dp, rank // chips, rank), F32),
            pltpu.VMEM((rank, rank), F32),
            pltpu.VMEM((rank, rank), F32),
            pltpu.VMEM((rank, rank), F32),
            pltpu.VMEM((half, block, rank), BF16),
            pltpu.VMEM((half, block, rank), BF16),
            pltpu.VMEM((half, block, rank), BF16),
            pltpu.VMEM((half, block, rank), BF16),
            pltpu.VMEM((block, rank), F32),
            pltpu.VMEM((block, rank), F32),
            pltpu.VMEM((n_dp, 8, 128), F32),
            pltpu.VMEM((chips, 8, 128), F32),
            dma((4,)),
            dma((2,)),
            dma((4, half)),
            dma((2, n_dp - 1)),
            dma((2,)),
            dma((2, chips - 1)),
            dma((2, n_dp - 1)),
            dma((2, n_dp - 1)),
            dma((2, chips - 1)),
            dma((2, 2 * n_dp - 1)),
            dma((2, chips - 1)),
            dma((2, half)),
            dma((2, half)),
            dma((2,)),
            dma((4, half)),
            dma((2, n_dp - 1)),
            dma((2, chips - 1)),
        ],
        compiler_params=pltpu.CompilerParams(
            collective_id=0, has_side_effects=True, vmem_limit_bytes=VMEM_LIMIT
        ),
    )(momentum, tile_values, exponents, right_prev, overflow)


def finish_kernel(unit, sums, ortho, low, inv, share, new, upd, share_out, new_v, upd_v, sem):
    rows, cols = sums.shape
    step = 256
    base = ortho[...]
    scaled = (base.astype(F32) * inv[0:1, :]).astype(BF16)
    both = (((1,), (1,)), ((), ()))
    share_copy = pltpu.make_async_copy(share, share_out, sem.at[2, 0])
    share_copy.start()
    copies = [share_copy]
    for t in range(cols // step):
        at = slice(t * step, (t + 1) * step)
        piece = low[at, :]
        correction = lax.dot_general(base, piece, both, preferred_element_type=F32)
        new_v[:, at] = (sums[:, at] - (1.0 - RETAIN) * correction).astype(BF16)
        direction = lax.dot_general(scaled, piece, both, preferred_element_type=F32)
        upd_v[:, at] = (unit * direction).astype(BF16)
        for k, (src, dst) in enumerate([(new_v, new), (upd_v, upd)]):
            copy = pltpu.make_async_copy(src.at[:, at], dst.at[:, at], sem.at[k, t])
            copy.start()
            copies.append(copy)
    for copy in copies:
        copy.wait()


def finish_stage(unit, sums, ortho, low, inv, share):
    rows, cols = sums.shape
    vmem = pl.BlockSpec(memory_space=pltpu.VMEM)
    hbm = pl.BlockSpec(memory_space=pltpu.HBM)
    return pl.pallas_call(
        functools.partial(finish_kernel, unit),
        name="finish",
        out_shape=(
            jax.ShapeDtypeStruct((rows, cols), BF16),
            jax.ShapeDtypeStruct((rows, cols), BF16),
            jax.ShapeDtypeStruct(share.shape, F32),
        ),
        in_specs=[vmem] * 5,
        out_specs=(hbm,) * 3,
        scratch_shapes=[
            pltpu.VMEM((rows, cols), BF16),
            pltpu.VMEM((rows, cols), BF16),
            pltpu.SemaphoreType.DMA((3, cols // 256)),
        ],
        compiler_params=pltpu.CompilerParams(vmem_limit_bytes=VMEM_LIMIT),
    )(sums, ortho, low, inv, share)


def body(n_dp, n_mp, momentum, tile_values, exponents, overflow, right_prev):
    rows, cols = momentum.shape
    rank = right_prev.shape[1]
    unit = math.sqrt(rows * n_mp * cols * n_dp / rank)
    args = [
        pltpu.with_memory_space_constraint(a, pltpu.HBM)
        for a in (momentum, tile_values, exponents, right_prev)
    ]
    ortho, low, inv, own, sums = mega_stage(n_dp, n_mp, *args, overflow)
    new, update, right_out = finish_stage(unit, sums, ortho, low, inv, own)
    return new, right_out, update


def solution(mesh):
    in_specs = (P("mp", "dp"), P("mp", "dp"), P("mp", "dp"), P("mp", "dp"), P(("dp", "mp"), None))
    out_specs = (P("mp", "dp"), P(("dp", "mp"), None), P("mp", "dp"))
    step = functools.partial(body, mesh.shape["dp"], mesh.shape["mp"])
    return jax.shard_map(step, mesh=mesh, in_specs=in_specs, out_specs=out_specs, check_vma=False)
```

time: 82.2 us -> 72.3 us (0.88)
  Pallas kernels: 80.8 us -> 70.9 us
    pallas_call x1, Pallas kernels: 78.5 us -> 68.6 us  [mega_stage(): pl.pallas_call(functools.partial(mega_kernel, n_dp, n_mp), name='mega', o...]
where the time goes in v3:
time: 72.3 us; the launch traced here: 72.2 us
  Pallas kernels  70.9 us (98%)
  between operations  1.29 us (2%)
    pallas_call x1, Pallas kernels, mega_stage(): pl.pallas_call(functools.partial(mega_kernel, n_dp, n_mp), name='mega', o...  68.6 us
    pallas_call x1, Pallas kernels, finish_stage(): pl.pallas_call(functools.partial(finish_kernel, unit), name='finish', out...  2.31 us

profile of v3, /device:TPU:1, one launch (start us, length us, event | category | flops | bytes accessed | tf_op | source)
XLA Modules:
  0.0 72.2 jit_solution(7947107632146150674)
XLA Ops:
  1.3 68.6 %mega.1 = (bf16[256,128]{1,0:T(8,128)(2,1)S(1)}, bf16[3328,128]{1,0:T(8,128)(2,1)S(1)}, f32[8,128]{1,0:T(8,128)S(1)}, f32[104,128]{1,0:T(8,128)S(1)}, f32[256,3328]{1,0:T(8,128)S(1)}) custom-call(bf16[256,3328]{1,0:T(8,128)(2,1)} %mom_hbm.1, bf16[256,3328]{1,0:T(8,128)(2,1)} %tile_hbm.1, s32[2,26]{1,0:T(2,128)} %exps_hbm.1, f32[104,128]{1,0:T(8,128)} %prev_hbm.1, ...), custom_call_target="tpu_custom_call" | custom-call | tf_op jit(solution)/shard_map/mega/pallas_call | solution.py:430
  69.9 2.3 %finish.1 = (bf16[256,3328]{1,0:T(8,128)(2,1)}, bf16[256,3328]{1,0:T(8,128)(2,1)}, f32[104,128]{1,0:T(8,128)}) custom-call(f32[256,3328]{1,0:T(8,128)S(1)} %get-tuple-element.11.sums, bf16[256,128]{1,0:T(8,128)(2,1)S(1)} %get-tuple-element.12.ortho, bf16[3328,128]{1,0:T(8,128)(2,1)S(1)} %get-tuple-element.13.low, f32[8,128]{1,0:T(8,128)S(1)} %get-tuple-element.14.inv, ...), custom_call_target="tpu_custom_call" | custom-call | tf_op jit(solution)/shard_map/finish/pallas_call | solution.py:522

commit v4 on v3

--- a/solution.py
+++ b/solution.py
@@ -43,19 +43,27 @@
             key=lambda o: -torus(o[0], self.nx) - torus(o[1], self.ny),
         )
         chips = {o: xs[o[0]] + ys[o[1]] for o in offsets}
-        split = [[o for o in offsets if sum(o) % 2 == parity] for parity in range(2)]
-
-        def pick(parity, sign):
-            return [
-                jnp.where(parity == 0, *(chips[(sign * o[0]) % self.nx, (sign * o[1]) % self.ny] for o in pair))
-                for pair in zip(*split)
-            ]
+        def away(offset):
+            return torus(offset[0], self.nx) + torus(offset[1], self.ny)
+
+        def back(offset):
+            return chips[-offset[0] % self.nx, -offset[1] % self.ny]
 
         self.sibling = (self.z, self.chip * 2 + self.other)
-        self.to_mine, self.from_mine = pick(self.core, 1), pick(self.core, -1)
-        self.to_other, self.from_other = pick(self.other, 1), pick(self.other, -1)
         self.plane = [chips[o] for o in offsets[:-1]]
+        self.plane_from = [back(o) for o in offsets[:-1]]
+        far = [o for o in offsets if away(o) > 1]
+        near = [o for o in offsets if away(o) == 1]
+        self.n_far, self.n_near = len(far), len(near)
+        odd = far[0::2]
+        even = far[1::2] + odd[-1:]
+        self.far_to = [jnp.where(self.core == 0, chips[a], chips[b]) for a, b in zip(even, odd)]
+        self.far_from = [jnp.where(self.core == 0, back(a), back(b)) for a, b in zip(even, odd)]
+        self.far_passed = [jnp.where(self.core == 0, back(b), back(a)) for a, b in zip(even, odd)]
+        self.near_to = [chips[o] for o in near]
+        self.near_from = [back(o) for o in near]
         self.plane_peers = [(self.z, chip * 2 + self.core) for chip in self.plane]
+        self.plane_all = self.plane_peers + [(self.z, chip * 2 + self.other) for chip in self.plane] + [self.sibling]
         self.z_order = sorted(range(1, self.nz), key=lambda d: -torus(d, self.nz))
         self.zs = [lax.rem(self.z + d, self.nz) for d in self.z_order]
         self.z_peers = [(z, self.chip * 2 + self.core) for z in self.zs]
@@ -66,6 +74,9 @@
     def same_core(self, chip):
         return (self.z, chip * 2 + self.core)
 
+    def other_core(self, chip):
+        return (self.z, chip * 2 + self.other)
+
 
 def remote(src, dst, send, recv, dev):
     return pltpu.make_async_remote_copy(
@@ -80,65 +91,134 @@
     return copies
 
 
-def start_all(copies, place):
-    for copy in copies[:-1]:
-        copy.start()
-    pl.when(place.core == 1)(copies[-1].start)
-
-
-class Gather:
-    def __init__(self, place, buf, rows, sems):
+class BlockGather:
+    def __init__(self, place, buf, rows, sems, near_sems):
         self.place = place
 
         def at(chip):
             return buf.at[pl.ds(pl.multiple_of(chip * rows, 16), rows)]
 
         mine = at(place.chip)
-        self.sends = [
+        self.far = [
             remote(mine, mine, sems.at[0, i], sems.at[1, i], place.same_core(chip))
-            for i, chip in enumerate(place.to_mine)
+            for i, chip in enumerate(place.far_to)
         ]
         self.arrivals = [
             remote(at(chip), at(chip), sems.at[0, i], sems.at[1, i], place.sibling)
-            for i, chip in enumerate(place.from_mine)
+            for i, chip in enumerate(place.far_from)
         ]
         self.passes = [
             remote(at(chip), at(chip), sems.at[2, i], sems.at[3, i], place.sibling)
-            for i, chip in enumerate(place.from_mine)
+            for i, chip in enumerate(place.far_from)
         ]
         self.passed = [
             remote(at(chip), at(chip), sems.at[2, i], sems.at[3, i], place.sibling)
-            for i, chip in enumerate(place.from_other)
+            for i, chip in enumerate(place.far_passed)
+        ]
+        self.near = [
+            remote(mine, mine, near_sems.at[0, i], near_sems.at[1, i], place.same_core(chip))
+            for i, chip in enumerate(place.near_to)
+        ]
+        self.near_in = [
+            remote(at(chip), at(chip), near_sems.at[0, i], near_sems.at[1, i], place.sibling)
+            for i, chip in enumerate(place.near_from)
         ]
 
     def send(self):
-        start_all(self.sends, self.place)
-
-    def forward(self, i):
+        for copy in self.far[:-1]:
+            copy.start()
+        pl.when(self.place.core == 1)(self.far[-1].start)
+        for copy in self.near:
+            copy.start()
+
+    def receive(self, use):
+        place = self.place
+        for arrival, onward, chip in list(zip(self.arrivals, self.passes, place.far_from))[:-1]:
+            arrival.wait_recv()
+            onward.start()
+            use(chip)
+
         def go():
-            self.arrivals[i].wait_recv()
-            self.passes[i].start()
-
-        if i == self.place.half - 1:
-            pl.when(self.place.core == 1)(go)
-        else:
-            go()
-
-    def finish(self):
-        for copy in self.passed[:-1]:
+            self.arrivals[-1].wait_recv()
+            self.passes[-1].start()
+
+        pl.when(place.core == 1)(go)
+        for copy, chip in zip(self.near_in, place.near_from):
             copy.wait_recv()
-        pl.when(self.place.core == 0)(self.passed[-1].wait_recv)
+            use(chip)
+        for copy, chip in list(zip(self.passed, place.far_passed))[:-1]:
+            copy.wait_recv()
+            use(chip)
+        pl.when(place.core == 0)(self.passed[-1].wait_recv)
+        use(jnp.where(place.core == 1, place.far_from[-1], place.far_passed[-1]))
 
     def drain(self):
-        for sent, passed in list(zip(self.sends, self.passes))[:-1]:
-            sent.wait_send()
-            passed.wait_send()
+        for copy in self.far[:-1] + self.passes[:-1] + self.near:
+            copy.wait_send()
 
         def last():
-            self.sends[-1].wait_send()
+            self.far[-1].wait_send()
             self.passes[-1].wait_send()
 
         pl.when(self.place.core == 1)(last)
+
+
+class WindowGather:
+    def __init__(self, place, buf, block, window, sems, pass_sems, near_sems, own_sems):
+        self.place = place
+        keep = block - window
+
+        def whole(chip):
+            return buf.at[pl.ds(pl.multiple_of(chip * block + place.core * keep, 16), window)]
+
+        def rest(chip, core):
+            return buf.at[pl.ds(pl.multiple_of(chip * block + core * window, 16), keep)]
+
+        mine, lacking = whole(place.chip), rest(place.chip, place.core)
+        other = place.other
+        self.own = remote(lacking, lacking, own_sems.at[0], own_sems.at[1], place.sibling)
+        self.own_in = remote(
+            rest(place.chip, other), rest(place.chip, other), own_sems.at[0], own_sems.at[1], place.sibling
+        )
+        self.sends = [
+            remote(mine, mine, sems.at[0, k], sems.at[1, k], dev) for k, dev in enumerate(place.plane_peers)
+        ]
+        self.arrivals = [
+            remote(whole(chip), whole(chip), sems.at[0, k], sems.at[1, k], place.sibling)
+            for k, chip in enumerate(place.plane_from)
+        ]
+        far = place.plane_from[:place.n_far]
+        self.passes = [
+            remote(rest(chip, place.core), rest(chip, place.core), pass_sems.at[0, k], pass_sems.at[1, k], place.sibling)
+            for k, chip in enumerate(far)
+        ]
+        self.passed = [
+            remote(rest(chip, other), rest(chip, other), pass_sems.at[0, k], pass_sems.at[1, k], place.sibling)
+            for k, chip in enumerate(far)
+        ]
+        self.near = [
+            remote(lacking, lacking, near_sems.at[0, k], near_sems.at[1, k], place.other_core(chip))
+            for k, chip in enumerate(place.near_to)
+        ]
+        self.near_in = [
+            remote(rest(chip, other), rest(chip, other), near_sems.at[0, k], near_sems.at[1, k], place.sibling)
+            for k, chip in enumerate(place.near_from)
+        ]
+
+    def send(self):
+        for copy in self.sends + self.near + [self.own]:
+            copy.start()
+
+    def receive(self):
+        for arrival, onward in zip(self.arrivals, self.passes):
+            arrival.wait_recv()
+            onward.start()
+        for copy in self.arrivals[self.place.n_far:] + self.near_in + [self.own_in] + self.passed:
+            copy.wait_recv()
+
+    def drain(self):
+        for copy in self.sends + self.near + [self.own] + self.passes:
+            copy.wait_send()
 
 
 def invert(work, out_ref):
@@ -190,11 +270,11 @@
     n_dp, n_mp,
     mom_hbm, tile_hbm, exps_hbm, prev_hbm, over_ref,
     ortho_ref, low_ref, inv_ref, share_ref, sum_ref,
-    both, exps, scale, pair, right, mom_t, grad_t, flag_z, flag_c, flag_p,
+    both, exps, scale, pair, right, both_t, flag_z, flag_p, left_t,
     part, left_in, left, gram, gram_p, gram_zc, gram_all, work, tri,
-    core_send, core_in, core_out, plane_in, mine, theirs, sq_z, sq_p,
-    sem_in, sem_pair, sem_gather, sem_fz, sem_fc, sem_fp, sem_lr, sem_lg, sem_gp, sem_gz, sem_gg,
-    sem_core, sem_plane, sem_sum, sem_low, sem_sz, sem_sp,
+    core_send, core_in, core_out, plane_in, mine, sq_z, sq_p,
+    sem_in, sem_pair, sem_gather, sem_near, sem_fz, sem_fp, sem_lr, sem_lg, sem_gp, sem_gz, sem_gg,
+    sem_core, sem_plane, sem_low, sem_pass, sem_low_near, sem_own, sem_sz, sem_sp,
 ):
     place = Place(n_dp, n_mp)
     rows, cols = mom_hbm.shape
@@ -213,7 +293,7 @@
     for load in loads:
         load.start()
     barrier = pltpu.get_barrier_semaphore()
-    friends = place.plane_peers + place.zc_peers
+    friends = place.plane_all + place.zc_peers[:-1]
     for dev in friends:
         pl.semaphore_signal(barrier, inc=1, device_id=dev, device_id_type=MESH)
     kept = jnp.where(over_ref[0, 0] == 0, 1.0, 0.0).astype(F32)
@@ -232,7 +312,7 @@
     pair_copy.start()
     pair_copy.wait_recv()
     right[pl.ds(pl.multiple_of(place.chip * block, 16), block)] = pair[...].astype(BF16)
-    gather = Gather(place, right, block, sem_gather)
+    gather = BlockGather(place, right, block, sem_gather, sem_near)
     gather.send()
 
     loads[2].wait()
@@ -250,23 +330,36 @@
 
     for copy in fz:
         copy.wait_recv()
-    flag_c[place.core] = jnp.sum(flag_z[...], axis=0)
-    fc = remote(flag_c.at[place.core], flag_c.at[place.core], sem_fc.at[0], sem_fc.at[1], place.sibling)
-    fc.start()
-    fc.wait_recv()
-    flag_p[place.chip] = flag_c[0] + flag_c[1]
-    fp = exchange(place.plane_peers, lambda k: flag_p.at[place.chip], flag_p.at[place.chip], sem_fp)
-    for i in range(place.half):
-        gather.forward(i)
-    gather.finish()
+    me = place.chip * 2 + place.core
+    flag_p[me] = jnp.sum(flag_z[...], axis=0)
+    fp = exchange(place.plane_all, lambda k: flag_p.at[me], flag_p.at[me], sem_fp)
+
+    def transpose(j, carry):
+        at = pl.ds(pl.multiple_of(j * BLOCK, BLOCK), BLOCK)
+        both_t[at, :rows] = both[0:rows, at].T
+        both_t[at, rows:] = both[rows:2 * rows, at].T
+        return carry
+
+    lax.fori_loop(0, cols // BLOCK, transpose, 0, unroll=2)
+
+    def rows_of(chip):
+        return pl.ds(pl.multiple_of(chip * block, 16), block)
+
+    left_t[...] = jnp.zeros_like(left_t)
+
+    def use(chip):
+        at = rows_of(chip)
+        left_t[...] += jnp.dot(right[at, :].T, both_t[at, :], preferred_element_type=F32)
+
+    use(place.chip)
+    gather.receive(use)
     for copy in fp:
         copy.wait_recv()
     healthy = jnp.sum(flag_p[...], axis=0)
     factor = (float(n_dp * n_mp) / jnp.maximum(healthy, 1.0))[0:1, :]
-    pending += [pair_copy, fc] + fz + fp
-
-    parts = jnp.dot(both[...], right[...], preferred_element_type=F32)
-    part[...] = parts[:rows] + factor * parts[rows:]
+    pending += [pair_copy] + fz + fp
+    for r in range(0, rows, BLOCK):
+        part[r:r + BLOCK, :] = (left_t[:, r:r + BLOCK] + factor * left_t[:, rows + r:rows + r + BLOCK]).T
 
     rz = rows // place.nz
     lr = []
@@ -278,13 +371,6 @@
         copy.start()
         lr.append(copy)
 
-    def transpose(j, carry):
-        at = pl.ds(pl.multiple_of(j * BLOCK, BLOCK), BLOCK)
-        mom_t[at, :] = both[0:rows, at].T
-        grad_t[at, :] = both[rows:2 * rows, at].T
-        return carry
-
-    lax.fori_loop(0, cols // BLOCK, transpose, 0)
     wide = jnp.broadcast_to(factor[:, 0:1], (16, BLOCK))
 
     def add(j, carry):
@@ -340,80 +426,61 @@
     ).astype(BF16)
     ortho_ref[...] = ortho
 
-    def rows_of(chip):
-        return pl.ds(pl.multiple_of(chip * block, 16), block)
-
-    def right_part(chip):
-        at = rows_of(chip)
-        return jnp.dot(mom_t[at, :], ortho, preferred_element_type=F32) + factor * jnp.dot(
-            grad_t[at, :], ortho, preferred_element_type=F32
+    window = share + -share % 16
+    keep = block - window
+
+    def right_part(chip, core):
+        at = pl.ds(pl.multiple_of(chip * block + core * keep, 16), window)
+        return jnp.dot(both_t[at, :rows], ortho, preferred_element_type=F32) + factor * jnp.dot(
+            both_t[at, rows:], ortho, preferred_element_type=F32
         )
 
+    chips = place.plane + [place.chip]
+    chunk = len(chips) // 4
     core_copies = []
-    for i, chip in enumerate(place.to_other):
-        core_send[i] = right_part(chip).astype(BF16)
-        copy = remote(core_send.at[i], core_in.at[i], sem_core.at[0, i], sem_core.at[1, i], place.sibling)
+    for k, chip in enumerate(chips):
+        core_send[k] = right_part(chip, place.other).astype(BF16)
+        if k % chunk == chunk - 1:
+            j = k // chunk
+            at = pl.ds(j * chunk, chunk)
+            copy = remote(core_send.at[at], core_in.at[at], sem_core.at[0, j], sem_core.at[1, j], place.sibling)
+            copy.start()
+            core_copies.append(copy)
+    plane_copies = []
+    for k, chip in enumerate(chips):
+        total = right_part(chip, place.core)
+        if k % chunk == 0:
+            core_copies[k // chunk].wait_recv()
+        total = total + core_in[k].astype(F32)
+        if chip is place.chip:
+            break
+        core_out[k] = total.astype(BF16)
+        copy = remote(core_out.at[k], plane_in.at[k], sem_plane.at[0, k], sem_plane.at[1, k], place.plane_peers[k])
         copy.start()
-        core_copies.append(copy)
-    plane_copies = []
-    last = place.half - 1
-    for i, chip in enumerate(place.to_mine):
-        total = right_part(chip)
-        core_copies[i].wait_recv()
-        total = total + core_in[i].astype(F32)
-        if i == last:
-            mine[...] = total
-        core_out[i] = total.astype(BF16)
-        copy = remote(
-            core_out.at[i], plane_in.at[i], sem_plane.at[0, i], sem_plane.at[1, i], place.same_core(chip)
-        )
-        if i == last:
-            pl.when(place.core == 1)(copy.start)
-        else:
-            copy.start()
         plane_copies.append(copy)
-    pending += core_copies + plane_copies[:-1]
-    acc = None
-    for i in range(last):
-        plane_copies[i].wait_recv()
-        got = plane_in[i].astype(F32)
-        acc = got if acc is None else acc + got
-
-    def own_last():
-        mine[...] = mine[...] + acc
-
-    def got_last():
-        plane_copies[last].wait_recv()
-        mine[...] = plane_in[last].astype(F32) + acc
-
-    pl.when(place.core == 0)(own_last)
-    pl.when(place.core == 1)(got_last)
-    pair_sum = remote(mine, theirs, sem_sum.at[0], sem_sum.at[1], place.sibling)
-    pair_sum.start()
-    pair_sum.wait_recv()
-    total = mine[...] + theirs[...]
-    pending += [pair_sum]
-    sq_z[place.z] = jnp.sum((total * total).reshape(block // 8, 8, rank), axis=0)
+    for k, copy in enumerate(plane_copies):
+        copy.wait_recv()
+        total = total + plane_in[k].astype(F32)
+    pending += core_copies + plane_copies
+    mine[...] = total
+    own_share = mine[pl.ds(pl.multiple_of(place.core * (window - share), 8), share)]
+    sq_z[place.z] = jnp.sum((own_share * own_share).reshape(share // 8, 8, rank), axis=0)
     sz = exchange(place.z_peers, lambda k: sq_z.at[place.z], sq_z.at[place.z], sem_sz)
-    low_ref[rows_of(place.chip)] = total.astype(BF16)
-    last_gather = Gather(place, low_ref, block, sem_low)
+    low_ref[pl.ds(pl.multiple_of(place.chip * block + place.core * keep, 16), window)] = total.astype(BF16)
+    last_gather = WindowGather(place, low_ref, block, window, sem_low, sem_pass, sem_low_near, sem_own)
     last_gather.send()
-    theirs[...] = total
-    share_ref[...] = theirs[my_share]
+    share_ref[...] = own_share
     for copy in sz:
         copy.wait_recv()
-    sq_p[place.chip] = jnp.sum(sq_z[...], axis=0)
-    sp = exchange(place.plane_peers, lambda k: sq_p.at[place.chip], sq_p.at[place.chip], sem_sp)
-    for i in range(place.half):
-        last_gather.forward(i)
-    last_gather.finish()
+    sq_p[me] = jnp.sum(sq_z[...], axis=0)
+    sp = exchange(place.plane_all, lambda k: sq_p.at[me], sq_p.at[me], sem_sp)
+    last_gather.receive()
     for copy in sp:
         copy.wait_recv()
     squares = jnp.sum(jnp.sum(sq_p[...], axis=0), axis=0, keepdims=True)
     inv_ref[...] = jnp.broadcast_to(lax.rsqrt(squares + EPSILON), inv_ref.shape)
     for copy in pending + sz + sp:
         copy.wait_send()
-    pl.when(place.core == 1)(plane_copies[last].wait_send)
     gather.drain()
     last_gather.drain()
 
@@ -422,8 +489,10 @@
     rows, cols = momentum.shape
     share, rank = right_prev.shape
     chips = n_mp // 2
-    half = chips // 2
     block = 2 * share
+    window = share + -share % 16
+    n_near = 4 if chips == 16 else 2
+    n_far = chips - 1 - n_near
     vmem = pl.BlockSpec(memory_space=pltpu.VMEM)
     hbm = pl.BlockSpec(memory_space=pltpu.HBM)
     dma = pltpu.SemaphoreType.DMA
@@ -445,11 +514,10 @@
             pltpu.VMEM((rows // BLOCK, 16, cols), BF16),
             pltpu.VMEM((block, rank), F32),
             pltpu.VMEM((cols, rank), BF16),
-            pltpu.VMEM((cols, rows), BF16),
-            pltpu.VMEM((cols, rows), BF16),
+            pltpu.VMEM((cols, 2 * rows), BF16),
             pltpu.VMEM((n_dp, 8, 128), F32),
-            pltpu.VMEM((2, 8, 128), F32),
-            pltpu.VMEM((chips, 8, 128), F32),
+            pltpu.VMEM((n_mp, 8, 128), F32),
+            pltpu.VMEM((rank, 2 * rows), F32),
             pltpu.VMEM((rows, rank), F32),
             pltpu.VMEM((n_dp - 1, rows // n_dp, rank), F32),
             pltpu.VMEM((rows, rank), F32),
@@ -459,31 +527,32 @@
             pltpu.VMEM((rank, rank), F32),
             pltpu.VMEM((rank, rank), F32),
             pltpu.VMEM((rank, rank), F32),
-            pltpu.VMEM((half, block, rank), BF16),
-            pltpu.VMEM((half, block, rank), BF16),
-            pltpu.VMEM((half, block, rank), BF16),
-            pltpu.VMEM((half, block, rank), BF16),
-            pltpu.VMEM((block, rank), F32),
-            pltpu.VMEM((block, rank), F32),
+            pltpu.VMEM((chips, window, rank), BF16),
+            pltpu.VMEM((chips, window, rank), BF16),
+            pltpu.VMEM((chips - 1, window, rank), BF16),
+            pltpu.VMEM((chips - 1, window, rank), BF16),
+            pltpu.VMEM((window, rank), F32),
             pltpu.VMEM((n_dp, 8, 128), F32),
-            pltpu.VMEM((chips, 8, 128), F32),
+            pltpu.VMEM((n_mp, 8, 128), F32),
             dma((4,)),
             dma((2,)),
-            dma((4, half)),
+            dma((4, (n_far + 1) // 2)),
+            dma((2, n_near)),
             dma((2, n_dp - 1)),
-            dma((2,)),
-            dma((2, chips - 1)),
+            dma((2, n_mp - 1)),
             dma((2, n_dp - 1)),
             dma((2, n_dp - 1)),
             dma((2, chips - 1)),
             dma((2, 2 * n_dp - 1)),
             dma((2, chips - 1)),
-            dma((2, half)),
-            dma((2, half)),
+            dma((2, 4)),
+            dma((2, chips - 1)),
+            dma((2, chips - 1)),
+            dma((2, n_far)),
+            dma((2, n_near)),
             dma((2,)),
-            dma((4, half)),
             dma((2, n_dp - 1)),
-            dma((2, chips - 1)),
+            dma((2, n_mp - 1)),
         ],
         compiler_params=pltpu.CompilerParams(
             collective_id=0, has_side_effects=True, vmem_limit_bytes=VMEM_LIMIT

time: 72.3 us -> 73.4 us (1.015)
  Pallas kernels: 70.9 us -> 72 us
    pallas_call x1, Pallas kernels: 68.6 us -> 69.7 us  [mega_stage(): pl.pallas_call(functools.partial(mega_kernel, n_dp, n_mp), name='mega', o...]
where the time goes in v4:
time: 73.4 us; the launch traced here: 73.3 us
  Pallas kernels  72 us (98%)
  between operations  1.29 us (2%)
    pallas_call x1, Pallas kernels, mega_stage(): pl.pallas_call(functools.partial(mega_kernel, n_dp, n_mp), name='mega', o...  69.7 us
    pallas_call x1, Pallas kernels, finish_stage(): pl.pallas_call(functools.partial(finish_kernel, unit), name='finish', out...  2.3 us

profile of v4, /device:TPU:1, one launch (start us, length us, event | category | flops | bytes accessed | tf_op | source)
XLA Modules:
  0.0 73.3 jit_solution(8661882339901844941)
XLA Ops:
  1.3 69.7 %mega.1 = (bf16[256,128]{1,0:T(8,128)(2,1)S(1)}, bf16[3328,128]{1,0:T(8,128)(2,1)S(1)}, f32[8,128]{1,0:T(8,128)S(1)}, f32[104,128]{1,0:T(8,128)S(1)}, f32[256,3328]{1,0:T(8,128)S(1)}) custom-call(bf16[256,3328]{1,0:T(8,128)(2,1)} %mom_hbm.1, bf16[256,3328]{1,0:T(8,128)(2,1)} %tile_hbm.1, s32[2,26]{1,0:T(2,128)} %exps_hbm.1, f32[104,128]{1,0:T(8,128)} %prev_hbm.1, ...), custom_call_target="tpu_custom_call" | custom-call | tf_op jit(solution)/shard_map/mega/pallas_call | solution.py:499
  71.0 2.3 %finish.1 = (bf16[256,3328]{1,0:T(8,128)(2,1)}, bf16[256,3328]{1,0:T(8,128)(2,1)}, f32[104,128]{1,0:T(8,128)}) custom-call(f32[256,3328]{1,0:T(8,128)S(1)} %get-tuple-element.11.sums, bf16[256,128]{1,0:T(8,128)(2,1)S(1)} %get-tuple-element.12.ortho, bf16[3328,128]{1,0:T(8,128)(2,1)S(1)} %get-tuple-element.13.low, f32[8,128]{1,0:T(8,128)S(1)} %get-tuple-element.14.inv, ...), custom_call_target="tpu_custom_call" | custom-call | tf_op jit(solution)/shard_map/finish/pallas_call | solution.py:591

commit v5 on v4

--- a/solution.py
+++ b/solution.py
@@ -63,7 +63,7 @@
         self.near_to = [chips[o] for o in near]
         self.near_from = [back(o) for o in near]
         self.plane_peers = [(self.z, chip * 2 + self.core) for chip in self.plane]
-        self.plane_all = self.plane_peers + [(self.z, chip * 2 + self.other) for chip in self.plane] + [self.sibling]
+        self.plane_all = [(self.z, chip * 2 + core) for chip in self.plane for core in (self.core, self.other)] + [self.sibling]
         self.z_order = sorted(range(1, self.nz), key=lambda d: -torus(d, self.nz))
         self.zs = [lax.rem(self.z + d, self.nz) for d in self.z_order]
         self.z_peers = [(z, self.chip * 2 + self.core) for z in self.zs]
@@ -271,7 +271,7 @@
     mom_hbm, tile_hbm, exps_hbm, prev_hbm, over_ref,
     ortho_ref, low_ref, inv_ref, share_ref, sum_ref,
     both, exps, scale, pair, right, both_t, flag_z, flag_p, left_t,
-    part, left_in, left, gram, gram_p, gram_zc, gram_all, work, tri,
+    part, left_in, left, left_hl, gram, gram_p, gram_zc, gram_all, work, tri,
     core_send, core_in, core_out, plane_in, mine, sq_z, sq_p,
     sem_in, sem_pair, sem_gather, sem_near, sem_fz, sem_fp, sem_lr, sem_lg, sem_gp, sem_gz, sem_gg,
     sem_core, sem_plane, sem_low, sem_pass, sem_low_near, sem_own, sem_sz, sem_sp,
@@ -293,11 +293,11 @@
     for load in loads:
         load.start()
     barrier = pltpu.get_barrier_semaphore()
-    friends = place.plane_all + place.zc_peers[:-1]
+    friends = place.zc_peers[:-1] + place.plane_all
     for dev in friends:
         pl.semaphore_signal(barrier, inc=1, device_id=dev, device_id_type=MESH)
     kept = jnp.where(over_ref[0, 0] == 0, 1.0, 0.0).astype(F32)
-    flag_z[place.z] = jnp.full((8, 128), kept, F32)
+    flag_z[place.z] = jnp.full((1, 128), kept, F32)
     loads[1].wait()
     scales = jnp.exp2(exps[...].astype(F32)).astype(BF16).astype(F32) * kept
     for j in range(cols // BLOCK):
@@ -356,7 +356,7 @@
     for copy in fp:
         copy.wait_recv()
     healthy = jnp.sum(flag_p[...], axis=0)
-    factor = (float(n_dp * n_mp) / jnp.maximum(healthy, 1.0))[0:1, :]
+    factor = float(n_dp * n_mp) / jnp.maximum(healthy, 1.0)
     pending += [pair_copy] + fz + fp
     for r in range(0, rows, BLOCK):
         part[r:r + BLOCK, :] = (left_t[:, r:r + BLOCK] + factor * left_t[:, rows + r:rows + r + BLOCK]).T
@@ -386,8 +386,8 @@
         acc = acc + left_in[k]
     left[own] = acc
     pending += lr
+    lg = exchange(place.z_peers, lambda k: left.at[own], left.at[own], sem_lg)
     gram[...] = lax.dot_general(acc, acc, (((0,), (0,)), ((), ())), precision=HIGH, preferred_element_type=F32)
-
     gs = rank // place.chips
     piece = pl.ds(pl.multiple_of(place.chip * gs, 8), gs)
     gp = []
@@ -398,48 +398,35 @@
         )
         copy.start()
         gp.append(copy)
+    lax.fori_loop(0, cols // BLOCK, add, 0)
     acc = gram[piece]
-    lax.fori_loop(0, cols // BLOCK, add, 0)
     for k, copy in enumerate(gp):
         copy.wait_recv()
         acc = acc + gram_p[k]
-    pending += gp
     spot = place.z * 2 + place.core
     gram_zc[spot] = acc
     gz = exchange(place.zc_peers, lambda k: gram_zc.at[spot], gram_zc.at[spot], sem_gz)
-    for copy in gz:
-        copy.wait_recv()
-    gram_all[piece] = jnp.sum(gram_zc[...], axis=0)
-    pending += gz
-    gg = exchange(place.plane_peers, lambda k: gram_all.at[piece], gram_all.at[piece], sem_gg)
-    lg = exchange(place.z_peers, lambda k: left.at[own], left.at[own], sem_lg)
-    for copy in gg:
-        copy.wait_recv()
-    pending += gg + lg
-    work[...] = gram_all[...]
-    invert(work, tri)
     for copy in lg:
         copy.wait_recv()
-
-    ortho = lax.dot_general(
-        left[...], tri[...], (((1,), (1,)), ((), ())), precision=HIGH, preferred_element_type=F32
-    ).astype(BF16)
-    ortho_ref[...] = ortho
-
+    pending += lg + gp
+
+    high = left[...].astype(BF16)
+    left_hl[:, :rank] = high
+    left_hl[:, rank:] = (left[...] - high.astype(F32)).astype(BF16)
     window = share + -share % 16
     keep = block - window
 
-    def right_part(chip, core):
+    def raw_part(chip, core):
         at = pl.ds(pl.multiple_of(chip * block + core * keep, 16), window)
-        return jnp.dot(both_t[at, :rows], ortho, preferred_element_type=F32) + factor * jnp.dot(
-            both_t[at, rows:], ortho, preferred_element_type=F32
-        )
+        mom_two = jnp.dot(both_t[at, :rows], left_hl[...], preferred_element_type=F32)
+        grad_two = jnp.dot(both_t[at, rows:], left_hl[...], preferred_element_type=F32)
+        return mom_two[:, :rank] + mom_two[:, rank:] + factor * (grad_two[:, :rank] + grad_two[:, rank:])
 
     chips = place.plane + [place.chip]
     chunk = len(chips) // 4
     core_copies = []
     for k, chip in enumerate(chips):
-        core_send[k] = right_part(chip, place.other).astype(BF16)
+        core_send[k] = raw_part(chip, place.other)
         if k % chunk == chunk - 1:
             j = k // chunk
             at = pl.ds(j * chunk, chunk)
@@ -447,29 +434,47 @@
             copy.start()
             core_copies.append(copy)
     plane_copies = []
-    for k, chip in enumerate(chips):
-        total = right_part(chip, place.core)
-        if k % chunk == 0:
-            core_copies[k // chunk].wait_recv()
-        total = total + core_in[k].astype(F32)
-        if chip is place.chip:
-            break
-        core_out[k] = total.astype(BF16)
-        copy = remote(core_out.at[k], plane_in.at[k], sem_plane.at[0, k], sem_plane.at[1, k], place.plane_peers[k])
-        copy.start()
-        plane_copies.append(copy)
+
+    def send_sums(first, last):
+        for k in range(first, last):
+            if k % chunk == 0:
+                core_copies[k // chunk].wait_recv()
+            core_out[k] = raw_part(chips[k], place.core) + core_in[k]
+            copy = remote(core_out.at[k], plane_in.at[k], sem_plane.at[0, k], sem_plane.at[1, k], place.plane_peers[k])
+            copy.start()
+            plane_copies.append(copy)
+
+    last = len(chips) - 1
+    send_sums(0, 2 * chunk)
+    for copy in gz:
+        copy.wait_recv()
+    gram_all[piece] = jnp.sum(gram_zc[...], axis=0)
+    gg = exchange(place.plane_peers, lambda k: gram_all.at[piece], gram_all.at[piece], sem_gg)
+    send_sums(2 * chunk, last)
+    if last % chunk == 0:
+        core_copies[-1].wait_recv()
+    total = raw_part(chips[last], place.core) + core_in[last]
+    for copy in gg:
+        copy.wait_recv()
+    pending += gz + gg + core_copies + plane_copies
+    work[...] = gram_all[...]
+    invert(work, tri)
     for k, copy in enumerate(plane_copies):
         copy.wait_recv()
-        total = total + plane_in[k].astype(F32)
-    pending += core_copies + plane_copies
+        total = total + plane_in[k]
+    by_rank = (((1,), (1,)), ((), ()))
+    total = lax.dot_general(total, tri[...], by_rank, precision=HIGH, preferred_element_type=F32)
     mine[...] = total
     own_share = mine[pl.ds(pl.multiple_of(place.core * (window - share), 8), share)]
-    sq_z[place.z] = jnp.sum((own_share * own_share).reshape(share // 8, 8, rank), axis=0)
+    sq_z[place.z] = jnp.sum(own_share * own_share, axis=0, keepdims=True)
     sz = exchange(place.z_peers, lambda k: sq_z.at[place.z], sq_z.at[place.z], sem_sz)
     low_ref[pl.ds(pl.multiple_of(place.chip * block + place.core * keep, 16), window)] = total.astype(BF16)
     last_gather = WindowGather(place, low_ref, block, window, sem_low, sem_pass, sem_low_near, sem_own)
     last_gather.send()
     share_ref[...] = own_share
+    ortho_ref[...] = lax.dot_general(
+        left[...], tri[...], by_rank, precision=HIGH, preferred_element_type=F32
+    ).astype(BF16)
     for copy in sz:
         copy.wait_recv()
     sq_p[me] = jnp.sum(sq_z[...], axis=0)
@@ -477,7 +482,7 @@
     last_gather.receive()
     for copy in sp:
         copy.wait_recv()
-    squares = jnp.sum(jnp.sum(sq_p[...], axis=0), axis=0, keepdims=True)
+    squares = jnp.sum(sq_p[...], axis=0)
     inv_ref[...] = jnp.broadcast_to(lax.rsqrt(squares + EPSILON), inv_ref.shape)
     for copy in pending + sz + sp:
         copy.wait_send()
@@ -515,25 +520,26 @@
             pltpu.VMEM((block, rank), F32),
             pltpu.VMEM((cols, rank), BF16),
             pltpu.VMEM((cols, 2 * rows), BF16),
-            pltpu.VMEM((n_dp, 8, 128), F32),
-            pltpu.VMEM((n_mp, 8, 128), F32),
+            pltpu.VMEM((n_dp, 1, 128), F32),
+            pltpu.VMEM((n_mp, 1, 128), F32),
             pltpu.VMEM((rank, 2 * rows), F32),
             pltpu.VMEM((rows, rank), F32),
             pltpu.VMEM((n_dp - 1, rows // n_dp, rank), F32),
             pltpu.VMEM((rows, rank), F32),
+            pltpu.VMEM((rows, 2 * rank), BF16),
             pltpu.VMEM((rank, rank), F32),
             pltpu.VMEM((chips - 1, rank // chips, rank), F32),
             pltpu.VMEM((2 * n_dp, rank // chips, rank), F32),
             pltpu.VMEM((rank, rank), F32),
             pltpu.VMEM((rank, rank), F32),
             pltpu.VMEM((rank, rank), F32),
-            pltpu.VMEM((chips, window, rank), BF16),
-            pltpu.VMEM((chips, window, rank), BF16),
-            pltpu.VMEM((chips - 1, window, rank), BF16),
-            pltpu.VMEM((chips - 1, window, rank), BF16),
+            pltpu.VMEM((chips, window, rank), F32),
+            pltpu.VMEM((chips, window, rank), F32),
+            pltpu.VMEM((chips - 1, window, rank), F32),
+            pltpu.VMEM((chips - 1, window, rank), F32),
             pltpu.VMEM((window, rank), F32),
-            pltpu.VMEM((n_dp, 8, 128), F32),
-            pltpu.VMEM((n_mp, 8, 128), F32),
+            pltpu.VMEM((n_dp, 1, 128), F32),
+            pltpu.VMEM((n_mp, 1, 128), F32),
             dma((4,)),
             dma((2,)),
             dma((4, (n_far + 1) // 2)),

time: 73.4 us -> 67.9 us (0.925)
  Pallas kernels: 72 us -> 66.5 us
    pallas_call x1, Pallas kernels: 69.7 us -> 64.2 us  [mega_stage(): pl.pallas_call(functools.partial(mega_kernel, n_dp, n_mp), name='mega', o...]
where the time goes in v5:
time: 67.9 us; the launch traced here: 67.8 us
  Pallas kernels  66.5 us (98%)
  between operations  1.29 us (2%)
    pallas_call x1, Pallas kernels, mega_stage(): pl.pallas_call(functools.partial(mega_kernel, n_dp, n_mp), name='mega', o...  64.2 us
    pallas_call x1, Pallas kernels, finish_stage(): pl.pallas_call(functools.partial(finish_kernel, unit), name='finish', out...  2.31 us

profile of v5, /device:TPU:1, one launch (start us, length us, event | category | flops | bytes accessed | tf_op | source)
XLA Modules:
  0.0 67.8 jit_solution(6170521292122943713)
XLA Ops:
  1.3 64.2 %mega.1 = (bf16[256,128]{1,0:T(8,128)(2,1)S(1)}, bf16[3328,128]{1,0:T(8,128)(2,1)S(1)}, f32[8,128]{1,0:T(8,128)S(1)}, f32[104,128]{1,0:T(8,128)S(1)}, f32[256,3328]{1,0:T(8,128)S(1)}) custom-call(bf16[256,3328]{1,0:T(8,128)(2,1)} %mom_hbm.1, bf16[256,3328]{1,0:T(8,128)(2,1)} %tile_hbm.1, s32[2,26]{1,0:T(2,128)} %exps_hbm.1, f32[104,128]{1,0:T(8,128)} %prev_hbm.1, ...), custom_call_target="tpu_custom_call" | custom-call | tf_op jit(solution)/shard_map/mega/pallas_call | solution.py:504
  65.5 2.3 %finish.1 = (bf16[256,3328]{1,0:T(8,128)(2,1)}, bf16[256,3328]{1,0:T(8,128)(2,1)}, f32[104,128]{1,0:T(8,128)}) custom-call(f32[256,3328]{1,0:T(8,128)S(1)} %get-tuple-element.11.sums, bf16[256,128]{1,0:T(8,128)(2,1)S(1)} %get-tuple-element.12.ortho, bf16[3328,128]{1,0:T(8,128)(2,1)S(1)} %get-tuple-element.13.low, f32[8,128]{1,0:T(8,128)S(1)} %get-tuple-element.14.inv, ...), custom_call_target="tpu_custom_call" | custom-call | tf_op jit(solution)/shard_map/finish/pallas_call | solution.py:597

commit v6 on v5

--- a/solution.py
+++ b/solution.py
@@ -70,6 +70,7 @@
         self.zc_peers = [
             (z, self.chip * 2 + core) for z in self.zs for core in (self.core, self.other)
         ] + [self.sibling]
+        self.zc_spots = [z * 2 + core for z in self.zs for core in (self.core, self.other)] + [self.z * 2 + self.other]
 
     def same_core(self, chip):
         return (self.z, chip * 2 + self.core)
@@ -271,9 +272,9 @@
     mom_hbm, tile_hbm, exps_hbm, prev_hbm, over_ref,
     ortho_ref, low_ref, inv_ref, share_ref, sum_ref,
     both, exps, scale, pair, right, both_t, flag_z, flag_p, left_t,
-    part, left_in, left, left_hl, gram, gram_p, gram_zc, gram_all, work, tri,
+    part, left_in, left, left_hl, gram, gram_zc, gram_p, gram_all, work, tri,
     core_send, core_in, core_out, plane_in, mine, sq_z, sq_p,
-    sem_in, sem_pair, sem_gather, sem_near, sem_fz, sem_fp, sem_lr, sem_lg, sem_gp, sem_gz, sem_gg,
+    sem_in, sem_pair, sem_gather, sem_near, sem_fz, sem_fp, sem_lr, sem_lg, sem_gz, sem_gp, sem_gg,
     sem_core, sem_plane, sem_low, sem_pass, sem_low_near, sem_own, sem_sz, sem_sp,
 ):
     place = Place(n_dp, n_mp)
@@ -386,29 +387,28 @@
         acc = acc + left_in[k]
     left[own] = acc
     pending += lr
-    lg = exchange(place.z_peers, lambda k: left.at[own], left.at[own], sem_lg)
     gram[...] = lax.dot_general(acc, acc, (((0,), (0,)), ((), ())), precision=HIGH, preferred_element_type=F32)
-    gs = rank // place.chips
-    piece = pl.ds(pl.multiple_of(place.chip * gs, 8), gs)
-    gp = []
-    for k, chip in enumerate(place.plane):
+    gs = rank // (2 * place.nz)
+    gz = []
+    for k, spot in enumerate(place.zc_spots):
         copy = remote(
-            gram.at[pl.ds(pl.multiple_of(chip * gs, 8), gs)], gram_p.at[k], sem_gp.at[0, k], sem_gp.at[1, k],
-            place.plane_peers[k],
+            gram.at[pl.ds(pl.multiple_of(spot * gs, 8), gs)], gram_zc.at[k], sem_gz.at[0, k], sem_gz.at[1, k],
+            place.zc_peers[k],
         )
         copy.start()
-        gp.append(copy)
+        gz.append(copy)
+    lg = exchange(place.z_peers, lambda k: left.at[own], left.at[own], sem_lg)
     lax.fori_loop(0, cols // BLOCK, add, 0)
+    piece = pl.ds(pl.multiple_of((place.z * 2 + place.core) * gs, 8), gs)
     acc = gram[piece]
-    for k, copy in enumerate(gp):
-        copy.wait_recv()
-        acc = acc + gram_p[k]
-    spot = place.z * 2 + place.core
-    gram_zc[spot] = acc
-    gz = exchange(place.zc_peers, lambda k: gram_zc.at[spot], gram_zc.at[spot], sem_gz)
+    for k, copy in enumerate(gz):
+        copy.wait_recv()
+        acc = acc + gram_zc[k]
+    gram_p[place.chip] = acc
+    gp = exchange(place.plane_peers, lambda k: gram_p.at[place.chip], gram_p.at[place.chip], sem_gp)
     for copy in lg:
         copy.wait_recv()
-    pending += lg + gp
+    pending += lg + gz
 
     high = left[...].astype(BF16)
     left_hl[:, :rank] = high
@@ -446,17 +446,17 @@
 
     last = len(chips) - 1
     send_sums(0, 2 * chunk)
-    for copy in gz:
-        copy.wait_recv()
-    gram_all[piece] = jnp.sum(gram_zc[...], axis=0)
-    gg = exchange(place.plane_peers, lambda k: gram_all.at[piece], gram_all.at[piece], sem_gg)
+    for copy in gp:
+        copy.wait_recv()
+    gram_all[piece] = jnp.sum(gram_p[...], axis=0)
+    gg = exchange(place.zc_peers, lambda k: gram_all.at[piece], gram_all.at[piece], sem_gg)
     send_sums(2 * chunk, last)
     if last % chunk == 0:
         core_copies[-1].wait_recv()
     total = raw_part(chips[last], place.core) + core_in[last]
     for copy in gg:
         copy.wait_recv()
-    pending += gz + gg + core_copies + plane_copies
+    pending += gp + gg + core_copies + plane_copies
     work[...] = gram_all[...]
     invert(work, tri)
     for k, copy in enumerate(plane_copies):
@@ -528,8 +528,8 @@
             pltpu.VMEM((rows, rank), F32),
             pltpu.VMEM((rows, 2 * rank), BF16),
             pltpu.VMEM((rank, rank), F32),
-            pltpu.VMEM((chips - 1, rank // chips, rank), F32),
-            pltpu.VMEM((2 * n_dp, rank // chips, rank), F32),
+            pltpu.VMEM((2 * n_dp - 1, rank // (2 * n_dp), rank), F32),
+            pltpu.VMEM((chips, rank // (2 * n_dp), rank), F32),
             pltpu.VMEM((rank, rank), F32),
             pltpu.VMEM((rank, rank), F32),
             pltpu.VMEM((rank, rank), F32),
@@ -548,9 +548,9 @@
             dma((2, n_mp - 1)),
             dma((2, n_dp - 1)),
             dma((2, n_dp - 1)),
+            dma((2, 2 * n_dp - 1)),
             dma((2, chips - 1)),
             dma((2, 2 * n_dp - 1)),
-            dma((2, chips - 1)),
             dma((2, 4)),
             dma((2, chips - 1)),
             dma((2, chips - 1)),

time: 67.9 us -> 66.1 us (0.973)
  Pallas kernels: 66.5 us -> 64.7 us
    pallas_call x1, Pallas kernels: 64.2 us -> 62.4 us  [mega_stage(): pl.pallas_call(functools.partial(mega_kernel, n_dp, n_mp), name='mega', o...]
where the time goes in v6:
time: 66.1 us; the launch traced here: 66 us
  Pallas kernels  64.7 us (98%)
  between operations  1.29 us (2%)
    pallas_call x1, Pallas kernels, mega_stage(): pl.pallas_call(functools.partial(mega_kernel, n_dp, n_mp), name='mega', o...  62.4 us
    pallas_call x1, Pallas kernels, finish_stage(): pl.pallas_call(functools.partial(finish_kernel, unit), name='finish', out...  2.3 us

profile of v6, /device:TPU:1, one launch (start us, length us, event | category | flops | bytes accessed | tf_op | source)
XLA Modules:
  0.0 66.0 jit_solution(15543520124677579946)
XLA Ops:
  1.3 62.4 %mega.1 = (bf16[256,128]{1,0:T(8,128)(2,1)S(1)}, bf16[3328,128]{1,0:T(8,128)(2,1)S(1)}, f32[8,128]{1,0:T(8,128)S(1)}, f32[104,128]{1,0:T(8,128)S(1)}, f32[256,3328]{1,0:T(8,128)S(1)}) custom-call(bf16[256,3328]{1,0:T(8,128)(2,1)} %mom_hbm.1, bf16[256,3328]{1,0:T(8,128)(2,1)} %tile_hbm.1, s32[2,26]{1,0:T(2,128)} %exps_hbm.1, f32[104,128]{1,0:T(8,128)} %prev_hbm.1, ...), custom_call_target="tpu_custom_call" | custom-call | tf_op jit(solution)/shard_map/mega/pallas_call | solution.py:504
  63.7 2.3 %finish.1 = (bf16[256,3328]{1,0:T(8,128)(2,1)}, bf16[256,3328]{1,0:T(8,128)(2,1)}, f32[104,128]{1,0:T(8,128)}) custom-call(f32[256,3328]{1,0:T(8,128)S(1)} %get-tuple-element.11.sums, bf16[256,128]{1,0:T(8,128)(2,1)S(1)} %get-tuple-element.12.ortho, bf16[3328,128]{1,0:T(8,128)(2,1)S(1)} %get-tuple-element.13.low, f32[8,128]{1,0:T(8,128)S(1)} %get-tuple-element.14.inv, ...), custom_call_target="tpu_custom_call" | custom-call | tf_op jit(solution)/shard_map/finish/pallas_call | solution.py:597

commit v7 on v6

--- a/solution.py
+++ b/solution.py
@@ -86,42 +86,51 @@
 
 
 def exchange(peers, src_of, dst, sems):
-    copies = [remote(src_of(k), dst, sems.at[0, k], sems.at[1, k], dev) for k, dev in enumerate(peers)]
-    for copy in copies:
-        copy.start()
-    return copies
+    for k, dev in enumerate(peers):
+        remote(src_of(k), dst, sems.at[0], sems.at[1], dev).start()
+
+
+def arrived(place, ref, sems):
+    remote(ref, ref, sems.at[0], sems.at[1], place.sibling).wait_recv()
+
+
+def sent(place, ref, sems):
+    remote(ref, ref, sems.at[0], sems.at[1], place.sibling).wait_send()
 
 
 class BlockGather:
-    def __init__(self, place, buf, rows, sems, near_sems):
+    def __init__(self, place, buf, rows, sems):
         self.place = place
 
         def at(chip):
             return buf.at[pl.ds(pl.multiple_of(chip * rows, 16), rows)]
 
+        self.buf, self.rows, self.sems = buf, rows, sems
+        n = len(place.far_to)
+        far_in, pass_in, near_in = 3, 3 + n, 3 + 2 * n
         mine = at(place.chip)
         self.far = [
-            remote(mine, mine, sems.at[0, i], sems.at[1, i], place.same_core(chip))
+            remote(mine, mine, sems.at[0], sems.at[far_in + i], place.same_core(chip))
             for i, chip in enumerate(place.far_to)
         ]
         self.arrivals = [
-            remote(at(chip), at(chip), sems.at[0, i], sems.at[1, i], place.sibling)
+            remote(at(chip), at(chip), sems.at[0], sems.at[far_in + i], place.sibling)
             for i, chip in enumerate(place.far_from)
         ]
         self.passes = [
-            remote(at(chip), at(chip), sems.at[2, i], sems.at[3, i], place.sibling)
+            remote(at(chip), at(chip), sems.at[1], sems.at[pass_in + i], place.sibling)
             for i, chip in enumerate(place.far_from)
         ]
         self.passed = [
-            remote(at(chip), at(chip), sems.at[2, i], sems.at[3, i], place.sibling)
+            remote(at(chip), at(chip), sems.at[1], sems.at[pass_in + i], place.sibling)
             for i, chip in enumerate(place.far_passed)
         ]
         self.near = [
-            remote(mine, mine, near_sems.at[0, i], near_sems.at[1, i], place.same_core(chip))
+            remote(mine, mine, sems.at[2], sems.at[near_in + i], place.same_core(chip))
             for i, chip in enumerate(place.near_to)
         ]
         self.near_in = [
-            remote(at(chip), at(chip), near_sems.at[0, i], near_sems.at[1, i], place.sibling)
+            remote(at(chip), at(chip), sems.at[2], sems.at[near_in + i], place.sibling)
             for i, chip in enumerate(place.near_from)
         ]
 
@@ -154,18 +163,24 @@
         use(jnp.where(place.core == 1, place.far_from[-1], place.far_passed[-1]))
 
     def drain(self):
-        for copy in self.far[:-1] + self.passes[:-1] + self.near:
-            copy.wait_send()
-
-        def last():
-            self.far[-1].wait_send()
-            self.passes[-1].wait_send()
-
-        pl.when(self.place.core == 1)(last)
+        def left_here(which, count):
+            ref = self.buf.at[pl.ds(0, count * self.rows)]
+            remote(ref, ref, self.sems.at[which], self.sems.at[which], self.place.sibling).wait_send()
+
+        left_here(2, len(self.near))
+
+        def all_far(count):
+            left_here(0, count)
+            left_here(1, count)
+
+        n = len(self.far)
+        pl.when(self.place.core == 1)(lambda: all_far(n))
+        if n > 1:
+            pl.when(self.place.core == 0)(lambda: all_far(n - 1))
 
 
 class WindowGather:
-    def __init__(self, place, buf, block, window, sems, pass_sems, near_sems, own_sems):
+    def __init__(self, place, buf, block, window, sems):
         self.place = place
         keep = block - window
 
@@ -175,51 +190,49 @@
         def rest(chip, core):
             return buf.at[pl.ds(pl.multiple_of(chip * block + core * window, 16), keep)]
 
+        self.buf, self.window, self.keep, self.sems = buf, window, keep, sems
         mine, lacking = whole(place.chip), rest(place.chip, place.core)
-        other = place.other
-        self.own = remote(lacking, lacking, own_sems.at[0], own_sems.at[1], place.sibling)
-        self.own_in = remote(
-            rest(place.chip, other), rest(place.chip, other), own_sems.at[0], own_sems.at[1], place.sibling
-        )
-        self.sends = [
-            remote(mine, mine, sems.at[0, k], sems.at[1, k], dev) for k, dev in enumerate(place.plane_peers)
-        ]
+        first = 8
+        far = place.plane_from[:place.n_far]
+        self.copies = [
+            remote(mine, mine, sems.at[0], sems.at[first + k if k < place.n_far else 7], dev)
+            for k, dev in enumerate(place.plane_peers)
+        ] + [
+            remote(lacking, lacking, sems.at[3], sems.at[4], place.other_core(chip)) for chip in place.near_to
+        ] + [remote(lacking, lacking, sems.at[5], sems.at[6], place.sibling)]
         self.arrivals = [
-            remote(whole(chip), whole(chip), sems.at[0, k], sems.at[1, k], place.sibling)
-            for k, chip in enumerate(place.plane_from)
-        ]
-        far = place.plane_from[:place.n_far]
+            remote(whole(chip), whole(chip), sems.at[0], sems.at[first + k], place.sibling)
+            for k, chip in enumerate(far)
+        ]
         self.passes = [
-            remote(rest(chip, place.core), rest(chip, place.core), pass_sems.at[0, k], pass_sems.at[1, k], place.sibling)
-            for k, chip in enumerate(far)
-        ]
-        self.passed = [
-            remote(rest(chip, other), rest(chip, other), pass_sems.at[0, k], pass_sems.at[1, k], place.sibling)
-            for k, chip in enumerate(far)
-        ]
-        self.near = [
-            remote(lacking, lacking, near_sems.at[0, k], near_sems.at[1, k], place.other_core(chip))
-            for k, chip in enumerate(place.near_to)
-        ]
-        self.near_in = [
-            remote(rest(chip, other), rest(chip, other), near_sems.at[0, k], near_sems.at[1, k], place.sibling)
-            for k, chip in enumerate(place.near_from)
-        ]
+            remote(rest(chip, place.core), rest(chip, place.core), sems.at[1], sems.at[2], place.sibling)
+            for chip in far
+        ]
+
+    def total(self, send, recv, rows):
+        ref = self.buf.at[pl.ds(0, rows)]
+        return remote(ref, ref, self.sems.at[send], self.sems.at[recv], self.place.sibling)
 
     def send(self):
-        for copy in self.sends + self.near + [self.own]:
+        for copy in self.copies:
             copy.start()
 
     def receive(self):
+        place = self.place
         for arrival, onward in zip(self.arrivals, self.passes):
             arrival.wait_recv()
             onward.start()
-        for copy in self.arrivals[self.place.n_far:] + self.near_in + [self.own_in] + self.passed:
-            copy.wait_recv()
+        self.total(0, 7, place.n_near * self.window).wait_recv()
+        self.total(3, 4, place.n_near * self.keep).wait_recv()
+        self.total(5, 6, self.keep).wait_recv()
+        self.total(1, 2, place.n_far * self.keep).wait_recv()
 
     def drain(self):
-        for copy in self.sends + self.near + [self.own] + self.passes:
-            copy.wait_send()
+        place = self.place
+        self.total(0, 7, (place.n_far + place.n_near) * self.window).wait_send()
+        self.total(1, 2, place.n_far * self.keep).wait_send()
+        self.total(3, 4, place.n_near * self.keep).wait_send()
+        self.total(5, 6, self.keep).wait_send()
 
 
 def invert(work, out_ref):
@@ -274,8 +287,8 @@
     both, exps, scale, pair, right, both_t, flag_z, flag_p, left_t,
     part, left_in, left, left_hl, gram, gram_zc, gram_p, gram_all, work, tri,
     core_send, core_in, core_out, plane_in, mine, sq_z, sq_p,
-    sem_in, sem_pair, sem_gather, sem_near, sem_fz, sem_fp, sem_lr, sem_lg, sem_gz, sem_gp, sem_gg,
-    sem_core, sem_plane, sem_low, sem_pass, sem_low_near, sem_own, sem_sz, sem_sp,
+    sem_in, sem_pair, sem_gather, sem_fz, sem_fp, sem_lr, sem_lg, sem_gz, sem_gp, sem_gg,
+    sem_core, sem_plane, sem_low, sem_sz, sem_sp,
 ):
     place = Place(n_dp, n_mp)
     rows, cols = mom_hbm.shape
@@ -306,14 +319,13 @@
             scale[b, :, j * BLOCK:(j + 1) * BLOCK] = jnp.broadcast_to(scales[b:b + 1, j:j + 1], (16, BLOCK)).astype(BF16)
     loads[0].wait()
     pl.semaphore_wait(barrier, len(friends))
-    pending = []
-
-    fz = exchange(place.z_peers, lambda k: flag_z.at[place.z], flag_z.at[place.z], sem_fz)
+
+    exchange(place.z_peers, lambda k: flag_z.at[place.z], flag_z.at[place.z], sem_fz)
     pair_copy = remote(pair.at[my_share], pair.at[my_share], sem_pair.at[0], sem_pair.at[1], place.sibling)
     pair_copy.start()
     pair_copy.wait_recv()
     right[pl.ds(pl.multiple_of(place.chip * block, 16), block)] = pair[...].astype(BF16)
-    gather = BlockGather(place, right, block, sem_gather, sem_near)
+    gather = BlockGather(place, right, block, sem_gather)
     gather.send()
 
     loads[2].wait()
@@ -329,11 +341,11 @@
 
     lax.fori_loop(0, cols // BLOCK, decode, 0)
 
-    for copy in fz:
-        copy.wait_recv()
+    all_z = flag_z.at[pl.ds(0, n_dp - 1)]
+    arrived(place, all_z, sem_fz)
     me = place.chip * 2 + place.core
     flag_p[me] = jnp.sum(flag_z[...], axis=0)
-    fp = exchange(place.plane_all, lambda k: flag_p.at[me], flag_p.at[me], sem_fp)
+    exchange(place.plane_all, lambda k: flag_p.at[me], flag_p.at[me], sem_fp)
 
     def transpose(j, carry):
         at = pl.ds(pl.multiple_of(j * BLOCK, BLOCK), BLOCK)
@@ -354,23 +366,19 @@
 
     use(place.chip)
     gather.receive(use)
-    for copy in fp:
-        copy.wait_recv()
+    all_p = flag_p.at[pl.ds(0, n_mp - 1)]
+    arrived(place, all_p, sem_fp)
     healthy = jnp.sum(flag_p[...], axis=0)
     factor = float(n_dp * n_mp) / jnp.maximum(healthy, 1.0)
-    pending += [pair_copy] + fz + fp
     for r in range(0, rows, BLOCK):
         part[r:r + BLOCK, :] = (left_t[:, r:r + BLOCK] + factor * left_t[:, rows + r:rows + r + BLOCK]).T
 
     rz = rows // place.nz
-    lr = []
     for k, z in enumerate(place.zs):
-        copy = remote(
-            part.at[pl.ds(pl.multiple_of(z * rz, 8), rz)], left_in.at[k], sem_lr.at[0, k], sem_lr.at[1, k],
+        remote(
+            part.at[pl.ds(pl.multiple_of(z * rz, 8), rz)], left_in.at[k], sem_lr.at[0], sem_lr.at[1],
             place.z_peers[k],
-        )
-        copy.start()
-        lr.append(copy)
+        ).start()
 
     wide = jnp.broadcast_to(factor[:, 0:1], (16, BLOCK))
 
@@ -382,33 +390,28 @@
 
     own = pl.ds(pl.multiple_of(place.z * rz, 8), rz)
     acc = part[own]
-    for k, copy in enumerate(lr):
-        copy.wait_recv()
+    arrived(place, left_in, sem_lr)
+    for k in range(n_dp - 1):
         acc = acc + left_in[k]
     left[own] = acc
-    pending += lr
+    exchange(place.z_peers, lambda k: left.at[own], left.at[own], sem_lg)
     gram[...] = lax.dot_general(acc, acc, (((0,), (0,)), ((), ())), precision=HIGH, preferred_element_type=F32)
     gs = rank // (2 * place.nz)
-    gz = []
     for k, spot in enumerate(place.zc_spots):
-        copy = remote(
-            gram.at[pl.ds(pl.multiple_of(spot * gs, 8), gs)], gram_zc.at[k], sem_gz.at[0, k], sem_gz.at[1, k],
+        remote(
+            gram.at[pl.ds(pl.multiple_of(spot * gs, 8), gs)], gram_zc.at[k], sem_gz.at[0], sem_gz.at[1],
             place.zc_peers[k],
-        )
-        copy.start()
-        gz.append(copy)
-    lg = exchange(place.z_peers, lambda k: left.at[own], left.at[own], sem_lg)
+        ).start()
     lax.fori_loop(0, cols // BLOCK, add, 0)
     piece = pl.ds(pl.multiple_of((place.z * 2 + place.core) * gs, 8), gs)
     acc = gram[piece]
-    for k, copy in enumerate(gz):
-        copy.wait_recv()
+    arrived(place, gram_zc, sem_gz)
+    for k in range(2 * n_dp - 1):
         acc = acc + gram_zc[k]
     gram_p[place.chip] = acc
-    gp = exchange(place.plane_peers, lambda k: gram_p.at[place.chip], gram_p.at[place.chip], sem_gp)
-    for copy in lg:
-        copy.wait_recv()
-    pending += lg + gz
+    exchange(place.plane_peers, lambda k: gram_p.at[place.chip], gram_p.at[place.chip], sem_gp)
+    all_left = left.at[pl.ds(0, rows - rz)]
+    arrived(place, all_left, sem_lg)
 
     high = left[...].astype(BF16)
     left_hl[:, :rank] = high
@@ -430,62 +433,61 @@
         if k % chunk == chunk - 1:
             j = k // chunk
             at = pl.ds(j * chunk, chunk)
-            copy = remote(core_send.at[at], core_in.at[at], sem_core.at[0, j], sem_core.at[1, j], place.sibling)
+            copy = remote(core_send.at[at], core_in.at[at], sem_core.at[0], sem_core.at[1 + j], place.sibling)
             copy.start()
             core_copies.append(copy)
-    plane_copies = []
 
     def send_sums(first, last):
         for k in range(first, last):
             if k % chunk == 0:
                 core_copies[k // chunk].wait_recv()
             core_out[k] = raw_part(chips[k], place.core) + core_in[k]
-            copy = remote(core_out.at[k], plane_in.at[k], sem_plane.at[0, k], sem_plane.at[1, k], place.plane_peers[k])
-            copy.start()
-            plane_copies.append(copy)
+            remote(core_out.at[k], plane_in.at[k], sem_plane.at[0], sem_plane.at[1], place.plane_peers[k]).start()
 
     last = len(chips) - 1
     send_sums(0, 2 * chunk)
-    for copy in gp:
-        copy.wait_recv()
+    all_gp = gram_p.at[pl.ds(0, last)]
+    arrived(place, all_gp, sem_gp)
     gram_all[piece] = jnp.sum(gram_p[...], axis=0)
-    gg = exchange(place.zc_peers, lambda k: gram_all.at[piece], gram_all.at[piece], sem_gg)
+    exchange(place.zc_peers, lambda k: gram_all.at[piece], gram_all.at[piece], sem_gg)
     send_sums(2 * chunk, last)
     if last % chunk == 0:
         core_copies[-1].wait_recv()
     total = raw_part(chips[last], place.core) + core_in[last]
-    for copy in gg:
-        copy.wait_recv()
-    pending += gp + gg + core_copies + plane_copies
+    all_gram = gram_all.at[pl.ds(0, rank - gs)]
+    arrived(place, all_gram, sem_gg)
     work[...] = gram_all[...]
     invert(work, tri)
-    for k, copy in enumerate(plane_copies):
-        copy.wait_recv()
+    arrived(place, plane_in, sem_plane)
+    for k in range(last):
         total = total + plane_in[k]
     by_rank = (((1,), (1,)), ((), ()))
     total = lax.dot_general(total, tri[...], by_rank, precision=HIGH, preferred_element_type=F32)
     mine[...] = total
     own_share = mine[pl.ds(pl.multiple_of(place.core * (window - share), 8), share)]
     sq_z[place.z] = jnp.sum(own_share * own_share, axis=0, keepdims=True)
-    sz = exchange(place.z_peers, lambda k: sq_z.at[place.z], sq_z.at[place.z], sem_sz)
+    exchange(place.z_peers, lambda k: sq_z.at[place.z], sq_z.at[place.z], sem_sz)
     low_ref[pl.ds(pl.multiple_of(place.chip * block + place.core * keep, 16), window)] = total.astype(BF16)
-    last_gather = WindowGather(place, low_ref, block, window, sem_low, sem_pass, sem_low_near, sem_own)
+    last_gather = WindowGather(place, low_ref, block, window, sem_low)
     last_gather.send()
     share_ref[...] = own_share
     ortho_ref[...] = lax.dot_general(
         left[...], tri[...], by_rank, precision=HIGH, preferred_element_type=F32
     ).astype(BF16)
-    for copy in sz:
-        copy.wait_recv()
+    arrived(place, sq_z.at[pl.ds(0, n_dp - 1)], sem_sz)
     sq_p[me] = jnp.sum(sq_z[...], axis=0)
-    sp = exchange(place.plane_all, lambda k: sq_p.at[me], sq_p.at[me], sem_sp)
+    exchange(place.plane_all, lambda k: sq_p.at[me], sq_p.at[me], sem_sp)
     last_gather.receive()
-    for copy in sp:
-        copy.wait_recv()
+    arrived(place, sq_p.at[pl.ds(0, n_mp - 1)], sem_sp)
     squares = jnp.sum(sq_p[...], axis=0)
     inv_ref[...] = jnp.broadcast_to(lax.rsqrt(squares + EPSILON), inv_ref.shape)
-    for copy in pending + sz + sp:
-        copy.wait_send()
+    pair_copy.wait_send()
+    for ref, sems in [
+        (all_z, sem_fz), (all_p, sem_fp), (left_in, sem_lr), (all_left, sem_lg), (gram_zc, sem_gz), (all_gp, sem_gp),
+        (all_gram, sem_gg), (plane_in, sem_plane), (core_send, sem_core),
+        (sq_z.at[pl.ds(0, n_dp - 1)], sem_sz), (sq_p.at[pl.ds(0, n_mp - 1)], sem_sp),
+    ]:
+        sent(place, ref, sems)
     gather.drain()
     last_gather.drain()
 
@@ -542,23 +544,19 @@
             pltpu.VMEM((n_mp, 1, 128), F32),
             dma((4,)),
             dma((2,)),
-            dma((4, (n_far + 1) // 2)),
-            dma((2, n_near)),
-            dma((2, n_dp - 1)),
-            dma((2, n_mp - 1)),
-            dma((2, n_dp - 1)),
-            dma((2, n_dp - 1)),
-            dma((2, 2 * n_dp - 1)),
-            dma((2, chips - 1)),
-            dma((2, 2 * n_dp - 1)),
-            dma((2, 4)),
-            dma((2, chips - 1)),
-            dma((2, chips - 1)),
-            dma((2, n_far)),
-            dma((2, n_near)),
-            dma((2,)),
-            dma((2, n_dp - 1)),
-            dma((2, n_mp - 1)),
+            dma((3 + 2 * ((n_far + 1) // 2) + n_near,)),
+            dma((2,)),
+            dma((2,)),
+            dma((2,)),
+            dma((2,)),
+            dma((2,)),
+            dma((2,)),
+            dma((2,)),
+            dma((5,)),
+            dma((2,)),
+            dma((8 + n_far,)),
+            dma((2,)),
+            dma((2,)),
         ],
         compiler_params=pltpu.CompilerParams(
             collective_id=0, has_side_effects=True, vmem_limit_bytes=VMEM_LIMIT

time: 66.1 us -> 62.4 us (0.944)
  Pallas kernels: 64.7 us -> 61 us
    pallas_call x1, Pallas kernels: 62.4 us -> 58.7 us  [mega_stage(): pl.pallas_call(functools.partial(mega_kernel, n_dp, n_mp), name='mega', o...]
where the time goes in v7:
time: 62.4 us; the launch traced here: 62.3 us
  Pallas kernels  61 us (98%)
  between operations  1.29 us (2%)
    pallas_call x1, Pallas kernels, mega_stage(): pl.pallas_call(functools.partial(mega_kernel, n_dp, n_mp), name='mega', o...  58.7 us
    pallas_call x1, Pallas kernels, finish_stage(): pl.pallas_call(functools.partial(finish_kernel, unit), name='finish', out...  2.31 us

profile of v7, /device:TPU:1, one launch (start us, length us, event | category | flops | bytes accessed | tf_op | source)
XLA Modules:
  0.0 62.3 jit_solution(12601850237353931317)
XLA Ops:
  1.3 58.7 %mega.1 = (bf16[256,128]{1,0:T(8,128)(2,1)S(1)}, bf16[3328,128]{1,0:T(8,128)(2,1)S(1)}, f32[8,128]{1,0:T(8,128)S(1)}, f32[104,128]{1,0:T(8,128)S(1)}, f32[256,3328]{1,0:T(8,128)S(1)}) custom-call(bf16[256,3328]{1,0:T(8,128)(2,1)} %mom_hbm.1, bf16[256,3328]{1,0:T(8,128)(2,1)} %tile_hbm.1, s32[2,26]{1,0:T(2,128)} %exps_hbm.1, f32[104,128]{1,0:T(8,128)} %prev_hbm.1, ...), custom_call_target="tpu_custom_call" | custom-call | tf_op jit(solution)/shard_map/mega/pallas_call | solution.py:506
  60.0 2.3 %finish.1 = (bf16[256,3328]{1,0:T(8,128)(2,1)}, bf16[256,3328]{1,0:T(8,128)(2,1)}, f32[104,128]{1,0:T(8,128)}) custom-call(f32[256,3328]{1,0:T(8,128)S(1)} %get-tuple-element.11.sums, bf16[256,128]{1,0:T(8,128)(2,1)S(1)} %get-tuple-element.12.ortho, bf16[3328,128]{1,0:T(8,128)(2,1)S(1)} %get-tuple-element.13.low, f32[8,128]{1,0:T(8,128)S(1)} %get-tuple-element.14.inv, ...), custom_call_target="tpu_custom_call" | custom-call | tf_op jit(solution)/shard_map/finish/pallas_call | solution.py:595

commit v8 on v7

--- a/solution.py
+++ b/solution.py
@@ -70,6 +70,16 @@
         self.zc_peers = [
             (z, self.chip * 2 + core) for z in self.zs for core in (self.core, self.other)
         ] + [self.sibling]
+        assert self.nx == self.ny
+        self.steps = sorted(range(self.nx), key=lambda d: -torus(d, self.nx))
+
+        def cross(core, a, b):
+            return jnp.where(core == 0, chips[a, b], chips[b, a])
+
+        self.group = [[cross(self.core, a, b) for b in range(self.nx)] for a in range(self.nx)]
+        self.other_group = [[cross(self.other, a, b) for b in range(self.nx)] for a in range(self.nx)]
+        self.step_one = [self.same_core(cross(self.core, a, 0)) for a in range(self.nx)]
+        self.step_two = [self.same_core(cross(self.core, 0, a)) for a in range(self.nx)]
         self.zc_spots = [z * 2 + core for z in self.zs for core in (self.core, self.other)] + [self.z * 2 + self.other]
 
     def same_core(self, chip):
@@ -286,9 +296,9 @@
     ortho_ref, low_ref, inv_ref, share_ref, sum_ref,
     both, exps, scale, pair, right, both_t, flag_z, flag_p, left_t,
     part, left_in, left, left_hl, gram, gram_zc, gram_p, gram_all, work, tri,
-    core_send, core_in, core_out, plane_in, mine, sq_z, sq_p,
+    core_send, core_in, core_out, plane_in, step_out, step_in, mine, sq_z, sq_p,
     sem_in, sem_pair, sem_gather, sem_fz, sem_fp, sem_lr, sem_lg, sem_gz, sem_gp, sem_gg,
-    sem_core, sem_plane, sem_low, sem_sz, sem_sp,
+    sem_core, sem_plane, sem_step, sem_low, sem_sz, sem_sp,
 ):
     place = Place(n_dp, n_mp)
     rows, cols = mom_hbm.shape
@@ -425,42 +435,48 @@
         grad_two = jnp.dot(both_t[at, rows:], left_hl[...], preferred_element_type=F32)
         return mom_two[:, :rank] + mom_two[:, rank:] + factor * (grad_two[:, :rank] + grad_two[:, rank:])
 
-    chips = place.plane + [place.chip]
-    chunk = len(chips) // 4
-    core_copies = []
-    for k, chip in enumerate(chips):
-        core_send[k] = raw_part(chip, place.other)
-        if k % chunk == chunk - 1:
-            j = k // chunk
-            at = pl.ds(j * chunk, chunk)
-            copy = remote(core_send.at[at], core_in.at[at], sem_core.at[0], sem_core.at[1 + j], place.sibling)
-            copy.start()
-            core_copies.append(copy)
-
-    def send_sums(first, last):
-        for k in range(first, last):
-            if k % chunk == 0:
-                core_copies[k // chunk].wait_recv()
-            core_out[k] = raw_part(chips[k], place.core) + core_in[k]
-            remote(core_out.at[k], plane_in.at[k], sem_plane.at[0], sem_plane.at[1], place.plane_peers[k]).start()
-
-    last = len(chips) - 1
-    send_sums(0, 2 * chunk)
+    core_copies = {}
+
+    def for_sibling(a):
+        for b, chip in enumerate(place.other_group[a]):
+            core_send[a, b] = raw_part(chip, place.other)
+        core_copies[a] = remote(core_send.at[a], core_in.at[a], sem_core.at[0], sem_core.at[1 + a], place.sibling)
+        core_copies[a].start()
+
+    def for_plane(a):
+        parts = [raw_part(chip, place.core) for chip in place.group[a]]
+        core_copies[a].wait_recv()
+        for b, value in enumerate(parts):
+            core_out[a, b] = value + core_in[a, b]
+        if a:
+            remote(core_out.at[a], plane_in.at[a - 1], sem_plane.at[0], sem_plane.at[1], place.step_one[a]).start()
+
+    n_side = place.nx
+    for_sibling(place.steps[0])
+    for ahead, a in zip(place.steps[1:], place.steps):
+        for_sibling(ahead)
+        for_plane(a)
+    last = place.chips - 1
     all_gp = gram_p.at[pl.ds(0, last)]
     arrived(place, all_gp, sem_gp)
     gram_all[piece] = jnp.sum(gram_p[...], axis=0)
     exchange(place.zc_peers, lambda k: gram_all.at[piece], gram_all.at[piece], sem_gg)
-    send_sums(2 * chunk, last)
-    if last % chunk == 0:
-        core_copies[-1].wait_recv()
-    total = raw_part(chips[last], place.core) + core_in[last]
+    for_plane(0)
+    arrived(place, plane_in, sem_plane)
+    for b in place.steps:
+        total = core_out[0, b]
+        for a in range(n_side - 1):
+            total = total + plane_in[a, b]
+        if b:
+            step_out[b - 1] = total
+            remote(step_out.at[b - 1], step_in.at[b - 1], sem_step.at[0], sem_step.at[1], place.step_two[b]).start()
     all_gram = gram_all.at[pl.ds(0, rank - gs)]
     arrived(place, all_gram, sem_gg)
     work[...] = gram_all[...]
     invert(work, tri)
-    arrived(place, plane_in, sem_plane)
-    for k in range(last):
-        total = total + plane_in[k]
+    arrived(place, step_in, sem_step)
+    for b in range(n_side - 1):
+        total = total + step_in[b]
     by_rank = (((1,), (1,)), ((), ()))
     total = lax.dot_general(total, tri[...], by_rank, precision=HIGH, preferred_element_type=F32)
     mine[...] = total
@@ -484,7 +500,7 @@
     pair_copy.wait_send()
     for ref, sems in [
         (all_z, sem_fz), (all_p, sem_fp), (left_in, sem_lr), (all_left, sem_lg), (gram_zc, sem_gz), (all_gp, sem_gp),
-        (all_gram, sem_gg), (plane_in, sem_plane), (core_send, sem_core),
+        (all_gram, sem_gg), (plane_in, sem_plane), (step_in, sem_step), (core_send, sem_core),
         (sq_z.at[pl.ds(0, n_dp - 1)], sem_sz), (sq_p.at[pl.ds(0, n_mp - 1)], sem_sp),
     ]:
         sent(place, ref, sems)
@@ -498,7 +514,8 @@
     chips = n_mp // 2
     block = 2 * share
     window = share + -share % 16
-    n_near = 4 if chips == 16 else 2
+    side = int(round(math.sqrt(chips)))
+    n_near = 4 if side > 2 else 2
     n_far = chips - 1 - n_near
     vmem = pl.BlockSpec(memory_space=pltpu.VMEM)
     hbm = pl.BlockSpec(memory_space=pltpu.HBM)
@@ -535,10 +552,12 @@
             pltpu.VMEM((rank, rank), F32),
             pltpu.VMEM((rank, rank), F32),
             pltpu.VMEM((rank, rank), F32),
-            pltpu.VMEM((chips, window, rank), F32),
-            pltpu.VMEM((chips, window, rank), F32),
-            pltpu.VMEM((chips - 1, window, rank), F32),
-            pltpu.VMEM((chips - 1, window, rank), F32),
+            pltpu.VMEM((side, side, window, rank), F32),
+            pltpu.VMEM((side, side, window, rank), F32),
+            pltpu.VMEM((side, side, window, rank), F32),
+            pltpu.VMEM((side - 1, side, window, rank), F32),
+            pltpu.VMEM((side - 1, window, rank), F32),
+            pltpu.VMEM((side - 1, window, rank), F32),
             pltpu.VMEM((window, rank), F32),
             pltpu.VMEM((n_dp, 1, 128), F32),
             pltpu.VMEM((n_mp, 1, 128), F32),
@@ -552,7 +571,8 @@
             dma((2,)),
             dma((2,)),
             dma((2,)),
-            dma((5,)),
+            dma((1 + side,)),
+            dma((2,)),
             dma((2,)),
             dma((8 + n_far,)),
             dma((2,)),
@@ -570,9 +590,8 @@
     base = ortho[...]
     scaled = (base.astype(F32) * inv[0:1, :]).astype(BF16)
     both = (((1,), (1,)), ((), ()))
-    share_copy = pltpu.make_async_copy(share, share_out, sem.at[2, 0])
+    share_copy = pltpu.make_async_copy(share, share_out, sem.at[2])
     share_copy.start()
-    copies = [share_copy]
     for t in range(cols // step):
         at = slice(t * step, (t + 1) * step)
         piece = low[at, :]
@@ -581,11 +600,10 @@
         direction = lax.dot_general(scaled, piece, both, preferred_element_type=F32)
         upd_v[:, at] = (unit * direction).astype(BF16)
         for k, (src, dst) in enumerate([(new_v, new), (upd_v, upd)]):
-            copy = pltpu.make_async_copy(src.at[:, at], dst.at[:, at], sem.at[k, t])
-            copy.start()
-            copies.append(copy)
-    for copy in copies:
-        copy.wait()
+            pltpu.make_async_copy(src.at[:, at], dst.at[:, at], sem.at[k]).start()
+    share_copy.wait()
+    for k, (src, dst) in enumerate([(new_v, new), (upd_v, upd)]):
+        pltpu.make_async_copy(src, dst, sem.at[k]).wait()
 
 
 def finish_stage(unit, sums, ortho, low, inv, share):
@@ -605,7 +623,7 @@
         scratch_shapes=[
             pltpu.VMEM((rows, cols), BF16),
             pltpu.VMEM((rows, cols), BF16),
-            pltpu.SemaphoreType.DMA((3, cols // 256)),
+            pltpu.SemaphoreType.DMA((3,)),
         ],
         compiler_params=pltpu.CompilerParams(vmem_limit_bytes=VMEM_LIMIT),
     )(sums, ortho, low, inv, share)

time: 62.4 us -> 60.2 us (0.965)
  Pallas kernels: 61 us -> 58.8 us
    pallas_call x1, Pallas kernels: 58.7 us -> 56.9 us  [mega_stage(): pl.pallas_call(functools.partial(mega_kernel, n_dp, n_mp), name='mega', o...]
where the time goes in v8:
time: 60.2 us; the launch traced here: 60.1 us
  Pallas kernels  58.8 us (98%)
  between operations  1.29 us (2%)
    pallas_call x1, Pallas kernels, mega_stage(): pl.pallas_call(functools.partial(mega_kernel, n_dp, n_mp), name='mega', o...  56.9 us
    pallas_call x1, Pallas kernels, finish_stage(): pl.pallas_call(functools.partial(finish_kernel, unit), name='finish', out...  1.98 us

profile of v8, /device:TPU:1, one launch (start us, length us, event | category | flops | bytes accessed | tf_op | source)
XLA Modules:
  0.0 60.1 jit_solution(625427535289688611)
XLA Ops:
  1.3 56.9 %mega.1 = (bf16[256,128]{1,0:T(8,128)(2,1)S(1)}, bf16[3328,128]{1,0:T(8,128)(2,1)S(1)}, f32[8,128]{1,0:T(8,128)S(1)}, f32[104,128]{1,0:T(8,128)S(1)}, f32[256,3328]{1,0:T(8,128)S(1)}) custom-call(bf16[256,3328]{1,0:T(8,128)(2,1)} %mom_hbm.1, bf16[256,3328]{1,0:T(8,128)(2,1)} %tile_hbm.1, s32[2,26]{1,0:T(2,128)} %exps_hbm.1, f32[104,128]{1,0:T(8,128)} %prev_hbm.1, ...), custom_call_target="tpu_custom_call" | custom-call | tf_op jit(solution)/shard_map/mega/pallas_call | solution.py:523
  58.2 2.0 %finish.1 = (bf16[256,3328]{1,0:T(8,128)(2,1)}, bf16[256,3328]{1,0:T(8,128)(2,1)}, f32[104,128]{1,0:T(8,128)}) custom-call(f32[256,3328]{1,0:T(8,128)S(1)} %get-tuple-element.11.sums, bf16[256,128]{1,0:T(8,128)(2,1)S(1)} %get-tuple-element.12.ortho, bf16[3328,128]{1,0:T(8,128)(2,1)S(1)} %get-tuple-element.13.low, f32[8,128]{1,0:T(8,128)S(1)} %get-tuple-element.14.inv, ...), custom_call_target="tpu_custom_call" | custom-call | tf_op jit(solution)/shard_map/finish/pallas_call | solution.py:613

commit v9 on v8

--- a/solution.py
+++ b/solution.py
@@ -55,11 +55,6 @@
         far = [o for o in offsets if away(o) > 1]
         near = [o for o in offsets if away(o) == 1]
         self.n_far, self.n_near = len(far), len(near)
-        odd = far[0::2]
-        even = far[1::2] + odd[-1:]
-        self.far_to = [jnp.where(self.core == 0, chips[a], chips[b]) for a, b in zip(even, odd)]
-        self.far_from = [jnp.where(self.core == 0, back(a), back(b)) for a, b in zip(even, odd)]
-        self.far_passed = [jnp.where(self.core == 0, back(b), back(a)) for a, b in zip(even, odd)]
         self.near_to = [chips[o] for o in near]
         self.near_from = [back(o) for o in near]
         self.plane_peers = [(self.z, chip * 2 + self.core) for chip in self.plane]
@@ -108,87 +103,6 @@
     remote(ref, ref, sems.at[0], sems.at[1], place.sibling).wait_send()
 
 
-class BlockGather:
-    def __init__(self, place, buf, rows, sems):
-        self.place = place
-
-        def at(chip):
-            return buf.at[pl.ds(pl.multiple_of(chip * rows, 16), rows)]
-
-        self.buf, self.rows, self.sems = buf, rows, sems
-        n = len(place.far_to)
-        far_in, pass_in, near_in = 3, 3 + n, 3 + 2 * n
-        mine = at(place.chip)
-        self.far = [
-            remote(mine, mine, sems.at[0], sems.at[far_in + i], place.same_core(chip))
-            for i, chip in enumerate(place.far_to)
-        ]
-        self.arrivals = [
-            remote(at(chip), at(chip), sems.at[0], sems.at[far_in + i], place.sibling)
-            for i, chip in enumerate(place.far_from)
-        ]
-        self.passes = [
-            remote(at(chip), at(chip), sems.at[1], sems.at[pass_in + i], place.sibling)
-            for i, chip in enumerate(place.far_from)
-        ]
-        self.passed = [
-            remote(at(chip), at(chip), sems.at[1], sems.at[pass_in + i], place.sibling)
-            for i, chip in enumerate(place.far_passed)
-        ]
-        self.near = [
-            remote(mine, mine, sems.at[2], sems.at[near_in + i], place.same_core(chip))
-            for i, chip in enumerate(place.near_to)
-        ]
-        self.near_in = [
-            remote(at(chip), at(chip), sems.at[2], sems.at[near_in + i], place.sibling)
-            for i, chip in enumerate(place.near_from)
-        ]
-
-    def send(self):
-        for copy in self.far[:-1]:
-            copy.start()
-        pl.when(self.place.core == 1)(self.far[-1].start)
-        for copy in self.near:
-            copy.start()
-
-    def receive(self, use):
-        place = self.place
-        for arrival, onward, chip in list(zip(self.arrivals, self.passes, place.far_from))[:-1]:
-            arrival.wait_recv()
-            onward.start()
-            use(chip)
-
-        def go():
-            self.arrivals[-1].wait_recv()
-            self.passes[-1].start()
-
-        pl.when(place.core == 1)(go)
-        for copy, chip in zip(self.near_in, place.near_from):
-            copy.wait_recv()
-            use(chip)
-        for copy, chip in list(zip(self.passed, place.far_passed))[:-1]:
-            copy.wait_recv()
-            use(chip)
-        pl.when(place.core == 0)(self.passed[-1].wait_recv)
-        use(jnp.where(place.core == 1, place.far_from[-1], place.far_passed[-1]))
-
-    def drain(self):
-        def left_here(which, count):
-            ref = self.buf.at[pl.ds(0, count * self.rows)]
-            remote(ref, ref, self.sems.at[which], self.sems.at[which], self.place.sibling).wait_send()
-
-        left_here(2, len(self.near))
-
-        def all_far(count):
-            left_here(0, count)
-            left_here(1, count)
-
-        n = len(self.far)
-        pl.when(self.place.core == 1)(lambda: all_far(n))
-        if n > 1:
-            pl.when(self.place.core == 0)(lambda: all_far(n - 1))
-
-
 class WindowGather:
     def __init__(self, place, buf, block, window, sems):
         self.place = place
@@ -202,21 +116,25 @@
 
         self.buf, self.window, self.keep, self.sems = buf, window, keep, sems
         mine, lacking = whole(place.chip), rest(place.chip, place.core)
-        first = 8
         far = place.plane_from[:place.n_far]
+        first, onward = 7, 7 + place.n_far
         self.copies = [
-            remote(mine, mine, sems.at[0], sems.at[first + k if k < place.n_far else 7], dev)
+            remote(mine, mine, sems.at[0], sems.at[first + k if k < place.n_far else 6], dev)
             for k, dev in enumerate(place.plane_peers)
         ] + [
-            remote(lacking, lacking, sems.at[3], sems.at[4], place.other_core(chip)) for chip in place.near_to
-        ] + [remote(lacking, lacking, sems.at[5], sems.at[6], place.sibling)]
+            remote(lacking, lacking, sems.at[2], sems.at[3], place.other_core(chip)) for chip in place.near_to
+        ] + [remote(lacking, lacking, sems.at[4], sems.at[5], place.sibling)]
         self.arrivals = [
             remote(whole(chip), whole(chip), sems.at[0], sems.at[first + k], place.sibling)
             for k, chip in enumerate(far)
         ]
         self.passes = [
-            remote(rest(chip, place.core), rest(chip, place.core), sems.at[1], sems.at[2], place.sibling)
-            for chip in far
+            remote(rest(chip, place.core), rest(chip, place.core), sems.at[1], sems.at[onward + k], place.sibling)
+            for k, chip in enumerate(far)
+        ]
+        self.passed = [
+            remote(rest(chip, place.other), rest(chip, place.other), sems.at[1], sems.at[onward + k], place.sibling)
+            for k, chip in enumerate(far)
         ]
 
     def total(self, send, recv, rows):
@@ -227,22 +145,28 @@
         for copy in self.copies:
             copy.start()
 
-    def receive(self):
+    def receive(self, use=None):
         place = self.place
         for arrival, onward in zip(self.arrivals, self.passes):
             arrival.wait_recv()
             onward.start()
-        self.total(0, 7, place.n_near * self.window).wait_recv()
-        self.total(3, 4, place.n_near * self.keep).wait_recv()
-        self.total(5, 6, self.keep).wait_recv()
-        self.total(1, 2, place.n_far * self.keep).wait_recv()
+        self.total(0, 6, place.n_near * self.window).wait_recv()
+        self.total(2, 3, place.n_near * self.keep).wait_recv()
+        self.total(4, 5, self.keep).wait_recv()
+        if use is not None:
+            for chip in [place.chip] + place.near_from:
+                use(chip)
+        for copy, chip in zip(self.passed, place.plane_from):
+            copy.wait_recv()
+            if use is not None:
+                use(chip)
 
     def drain(self):
         place = self.place
-        self.total(0, 7, (place.n_far + place.n_near) * self.window).wait_send()
-        self.total(1, 2, place.n_far * self.keep).wait_send()
-        self.total(3, 4, place.n_near * self.keep).wait_send()
-        self.total(5, 6, self.keep).wait_send()
+        self.total(0, 6, (place.n_far + place.n_near) * self.window).wait_send()
+        self.total(1, 6, place.n_far * self.keep).wait_send()
+        self.total(2, 3, place.n_near * self.keep).wait_send()
+        self.total(4, 5, self.keep).wait_send()
 
 
 def invert(work, out_ref):
@@ -294,22 +218,23 @@
     n_dp, n_mp,
     mom_hbm, tile_hbm, exps_hbm, prev_hbm, over_ref,
     ortho_ref, low_ref, inv_ref, share_ref, sum_ref,
-    both, exps, scale, pair, right, both_t, flag_z, flag_p, left_t,
+    both, exps, scale, prev, right, both_t, flag_z, flag_p, left_t,
     part, left_in, left, left_hl, gram, gram_zc, gram_p, gram_all, work, tri,
     core_send, core_in, core_out, plane_in, step_out, step_in, mine, sq_z, sq_p,
-    sem_in, sem_pair, sem_gather, sem_fz, sem_fp, sem_lr, sem_lg, sem_gz, sem_gp, sem_gg,
+    sem_in, sem_gather, sem_fz, sem_fp, sem_lr, sem_lg, sem_gz, sem_gp, sem_gg,
     sem_core, sem_plane, sem_step, sem_low, sem_sz, sem_sp,
 ):
     place = Place(n_dp, n_mp)
     rows, cols = mom_hbm.shape
     share, rank = share_ref.shape
     block = 2 * share
-    my_share = pl.ds(pl.multiple_of(place.core * share, 8), share)
+    window = share + -share % 16
+    keep = block - window
     loads = [
         pltpu.make_async_copy(src, dst, sem_in.at[k])
         for k, (src, dst) in enumerate(
             [
-                (prev_hbm, pair.at[my_share]), (exps_hbm, exps),
+                (prev_hbm, prev), (exps_hbm, exps),
                 (mom_hbm, both.at[0:rows]), (tile_hbm, both.at[rows:2 * rows]),
             ]
         )
@@ -328,14 +253,15 @@
         for b in range(rows // BLOCK):
             scale[b, :, j * BLOCK:(j + 1) * BLOCK] = jnp.broadcast_to(scales[b:b + 1, j:j + 1], (16, BLOCK)).astype(BF16)
     loads[0].wait()
+    gather = WindowGather(place, right, 2 * window, window, sem_gather)
+    mine_low = prev[...].astype(BF16).astype(F32)
+    if window > share:
+        mine_low = jnp.concatenate([mine_low, jnp.zeros((window - share, rank), F32)], axis=0)
+    me = place.chip * 2 + place.core
+    right[pl.ds(pl.multiple_of(me * window, 16), window)] = mine_low.astype(BF16)
     pl.semaphore_wait(barrier, len(friends))
 
     exchange(place.z_peers, lambda k: flag_z.at[place.z], flag_z.at[place.z], sem_fz)
-    pair_copy = remote(pair.at[my_share], pair.at[my_share], sem_pair.at[0], sem_pair.at[1], place.sibling)
-    pair_copy.start()
-    pair_copy.wait_recv()
-    right[pl.ds(pl.multiple_of(place.chip * block, 16), block)] = pair[...].astype(BF16)
-    gather = BlockGather(place, right, block, sem_gather)
     gather.send()
 
     loads[2].wait()
@@ -353,7 +279,6 @@
 
     all_z = flag_z.at[pl.ds(0, n_dp - 1)]
     arrived(place, all_z, sem_fz)
-    me = place.chip * 2 + place.core
     flag_p[me] = jnp.sum(flag_z[...], axis=0)
     exchange(place.plane_all, lambda k: flag_p.at[me], flag_p.at[me], sem_fp)
 
@@ -371,10 +296,10 @@
     left_t[...] = jnp.zeros_like(left_t)
 
     def use(chip):
-        at = rows_of(chip)
-        left_t[...] += jnp.dot(right[at, :].T, both_t[at, :], preferred_element_type=F32)
-
-    use(place.chip)
+        got = right[pl.ds(pl.multiple_of(chip * 2 * window, 16), 2 * window), :].astype(F32)
+        got = jnp.concatenate([got[:share], got[window:window + share]], axis=0).astype(BF16)
+        left_t[...] += jnp.dot(got.T, both_t[rows_of(chip), :], preferred_element_type=F32)
+
     gather.receive(use)
     all_p = flag_p.at[pl.ds(0, n_mp - 1)]
     arrived(place, all_p, sem_fp)
@@ -404,7 +329,6 @@
     for k in range(n_dp - 1):
         acc = acc + left_in[k]
     left[own] = acc
-    exchange(place.z_peers, lambda k: left.at[own], left.at[own], sem_lg)
     gram[...] = lax.dot_general(acc, acc, (((0,), (0,)), ((), ())), precision=HIGH, preferred_element_type=F32)
     gs = rank // (2 * place.nz)
     for k, spot in enumerate(place.zc_spots):
@@ -412,6 +336,7 @@
             gram.at[pl.ds(pl.multiple_of(spot * gs, 8), gs)], gram_zc.at[k], sem_gz.at[0], sem_gz.at[1],
             place.zc_peers[k],
         ).start()
+    exchange(place.z_peers, lambda k: left.at[own], left.at[own], sem_lg)
     lax.fori_loop(0, cols // BLOCK, add, 0)
     piece = pl.ds(pl.multiple_of((place.z * 2 + place.core) * gs, 8), gs)
     acc = gram[piece]
@@ -426,9 +351,6 @@
     high = left[...].astype(BF16)
     left_hl[:, :rank] = high
     left_hl[:, rank:] = (left[...] - high.astype(F32)).astype(BF16)
-    window = share + -share % 16
-    keep = block - window
-
     def raw_part(chip, core):
         at = pl.ds(pl.multiple_of(chip * block + core * keep, 16), window)
         mom_two = jnp.dot(both_t[at, :rows], left_hl[...], preferred_element_type=F32)
@@ -497,7 +419,6 @@
     arrived(place, sq_p.at[pl.ds(0, n_mp - 1)], sem_sp)
     squares = jnp.sum(sq_p[...], axis=0)
     inv_ref[...] = jnp.broadcast_to(lax.rsqrt(squares + EPSILON), inv_ref.shape)
-    pair_copy.wait_send()
     for ref, sems in [
         (all_z, sem_fz), (all_p, sem_fp), (left_in, sem_lr), (all_left, sem_lg), (gram_zc, sem_gz), (all_gp, sem_gp),
         (all_gram, sem_gg), (plane_in, sem_plane), (step_in, sem_step), (core_send, sem_core),
@@ -536,8 +457,8 @@
             pltpu.VMEM((2 * rows, cols), BF16),
             pltpu.VMEM(exponents.shape, jnp.int32),
             pltpu.VMEM((rows // BLOCK, 16, cols), BF16),
-            pltpu.VMEM((block, rank), F32),
-            pltpu.VMEM((cols, rank), BF16),
+            pltpu.VMEM((share, rank), F32),
+            pltpu.VMEM((n_mp * window, rank), BF16),
             pltpu.VMEM((cols, 2 * rows), BF16),
             pltpu.VMEM((n_dp, 1, 128), F32),
             pltpu.VMEM((n_mp, 1, 128), F32),
@@ -562,8 +483,7 @@
             pltpu.VMEM((n_dp, 1, 128), F32),
             pltpu.VMEM((n_mp, 1, 128), F32),
             dma((4,)),
-            dma((2,)),
-            dma((3 + 2 * ((n_far + 1) // 2) + n_near,)),
+            dma((7 + 2 * n_far,)),
             dma((2,)),
             dma((2,)),
             dma((2,)),
@@ -574,7 +494,7 @@
             dma((1 + side,)),
             dma((2,)),
             dma((2,)),
-            dma((8 + n_far,)),
+            dma((7 + 2 * n_far,)),
             dma((2,)),
             dma((2,)),
         ],

time: 60.2 us -> 59.6 us (0.990)
  no operation moved by 1% of the time
where the time goes in v9:
time: 59.6 us
  Pallas kernels  58.3 us (98%)
  between operations  1.29 us (2%)
    pallas_call x1, Pallas kernels, mega_stage(): pl.pallas_call(functools.partial(mega_kernel, n_dp, n_mp), name='mega', o...  56.3 us
    pallas_call x1, Pallas kernels, finish_stage(): pl.pallas_call(functools.partial(finish_kernel, unit), name='finish', out...  1.99 us

profile of v9, /device:TPU:1, one launch (start us, length us, event | category | flops | bytes accessed | tf_op | source)
XLA Modules:
  0.0 59.6 jit_solution(6907119020904872961)
XLA Ops:
  1.3 56.3 %mega.1 = (bf16[256,128]{1,0:T(8,128)(2,1)S(1)}, bf16[3328,128]{1,0:T(8,128)(2,1)S(1)}, f32[8,128]{1,0:T(8,128)S(1)}, f32[104,128]{1,0:T(8,128)S(1)}, f32[256,3328]{1,0:T(8,128)S(1)}) custom-call(bf16[256,3328]{1,0:T(8,128)(2,1)} %mom_hbm.1, bf16[256,3328]{1,0:T(8,128)(2,1)} %tile_hbm.1, s32[2,26]{1,0:T(2,128)} %exps_hbm.1, f32[104,128]{1,0:T(8,128)} %prev_hbm.1, ...), custom_call_target="tpu_custom_call" | custom-call | tf_op jit(solution)/shard_map/mega/pallas_call | solution.py:444
  57.6 2.0 %finish.1 = (bf16[256,3328]{1,0:T(8,128)(2,1)}, bf16[256,3328]{1,0:T(8,128)(2,1)}, f32[104,128]{1,0:T(8,128)}) custom-call(f32[256,3328]{1,0:T(8,128)S(1)} %get-tuple-element.11.sums, bf16[256,128]{1,0:T(8,128)(2,1)S(1)} %get-tuple-element.12.ortho, bf16[3328,128]{1,0:T(8,128)(2,1)S(1)} %get-tuple-element.13.low, f32[8,128]{1,0:T(8,128)S(1)} %get-tuple-element.14.inv, ...), custom_call_target="tpu_custom_call" | custom-call | tf_op jit(solution)/shard_map/finish/pallas_call | solution.py:533

commit v10 on v9

--- a/solution.py
+++ b/solution.py
@@ -277,11 +277,6 @@
 
     lax.fori_loop(0, cols // BLOCK, decode, 0)
 
-    all_z = flag_z.at[pl.ds(0, n_dp - 1)]
-    arrived(place, all_z, sem_fz)
-    flag_p[me] = jnp.sum(flag_z[...], axis=0)
-    exchange(place.plane_all, lambda k: flag_p.at[me], flag_p.at[me], sem_fp)
-
     def transpose(j, carry):
         at = pl.ds(pl.multiple_of(j * BLOCK, BLOCK), BLOCK)
         both_t[at, :rows] = both[0:rows, at].T
@@ -290,10 +285,14 @@
 
     lax.fori_loop(0, cols // BLOCK, transpose, 0, unroll=2)
 
+    left_t[...] = jnp.zeros_like(left_t)
+    all_z = flag_z.at[pl.ds(0, n_dp - 1)]
+    arrived(place, all_z, sem_fz)
+    flag_p[me] = jnp.sum(flag_z[...], axis=0)
+    exchange(place.plane_all, lambda k: flag_p.at[me], flag_p.at[me], sem_fp)
+
     def rows_of(chip):
         return pl.ds(pl.multiple_of(chip * block, 16), block)
-
-    left_t[...] = jnp.zeros_like(left_t)
 
     def use(chip):
         got = right[pl.ds(pl.multiple_of(chip * 2 * window, 16), 2 * window), :].astype(F32)

time: 59.6 us -> 59.6 us (level)
  no operation moved by 1% of the time
where the time goes in v10:
time: 59.6 us
  Pallas kernels  58.3 us (98%)
  between operations  1.29 us (2%)
    pallas_call x1, Pallas kernels, mega_stage(): pl.pallas_call(functools.partial(mega_kernel, n_dp, n_mp), name='mega', o...  56.3 us
    pallas_call x1, Pallas kernels, finish_stage(): pl.pallas_call(functools.partial(finish_kernel, unit), name='finish', out...  1.99 us

profile of v10, /device:TPU:1, one launch (start us, length us, event | category | flops | bytes accessed | tf_op | source)
XLA Modules:
  0.0 59.6 jit_solution(1058881446734073391)
XLA Ops:
  1.3 56.3 %mega.1 = (bf16[256,128]{1,0:T(8,128)(2,1)S(1)}, bf16[3328,128]{1,0:T(8,128)(2,1)S(1)}, f32[8,128]{1,0:T(8,128)S(1)}, f32[104,128]{1,0:T(8,128)S(1)}, f32[256,3328]{1,0:T(8,128)S(1)}) custom-call(bf16[256,3328]{1,0:T(8,128)(2,1)} %mom_hbm.1, bf16[256,3328]{1,0:T(8,128)(2,1)} %tile_hbm.1, s32[2,26]{1,0:T(2,128)} %exps_hbm.1, f32[104,128]{1,0:T(8,128)} %prev_hbm.1, ...), custom_call_target="tpu_custom_call" | custom-call | tf_op jit(solution)/shard_map/mega/pallas_call | solution.py:443
  57.6 2.0 %finish.1 = (bf16[256,3328]{1,0:T(8,128)(2,1)}, bf16[256,3328]{1,0:T(8,128)(2,1)}, f32[104,128]{1,0:T(8,128)}) custom-call(f32[256,3328]{1,0:T(8,128)S(1)} %get-tuple-element.11.sums, bf16[256,128]{1,0:T(8,128)(2,1)S(1)} %get-tuple-element.12.ortho, bf16[3328,128]{1,0:T(8,128)(2,1)S(1)} %get-tuple-element.13.low, f32[8,128]{1,0:T(8,128)S(1)} %get-tuple-element.14.inv, ...), custom_call_target="tpu_custom_call" | custom-call | tf_op jit(solution)/shard_map/finish/pallas_call | solution.py:532

commit v11 on v10

--- a/solution.py
+++ b/solution.py
@@ -246,7 +246,8 @@
     for dev in friends:
         pl.semaphore_signal(barrier, inc=1, device_id=dev, device_id_type=MESH)
     kept = jnp.where(over_ref[0, 0] == 0, 1.0, 0.0).astype(F32)
-    flag_z[place.z] = jnp.full((1, 128), kept, F32)
+    me = place.chip * 2 + place.core
+    flag_p[me] = jnp.full((1, 128), kept, F32)
     loads[1].wait()
     scales = jnp.exp2(exps[...].astype(F32)).astype(BF16).astype(F32) * kept
     for j in range(cols // BLOCK):
@@ -257,11 +258,10 @@
     mine_low = prev[...].astype(BF16).astype(F32)
     if window > share:
         mine_low = jnp.concatenate([mine_low, jnp.zeros((window - share, rank), F32)], axis=0)
-    me = place.chip * 2 + place.core
     right[pl.ds(pl.multiple_of(me * window, 16), window)] = mine_low.astype(BF16)
     pl.semaphore_wait(barrier, len(friends))
 
-    exchange(place.z_peers, lambda k: flag_z.at[place.z], flag_z.at[place.z], sem_fz)
+    exchange(place.plane_all, lambda k: flag_p.at[me], flag_p.at[me], sem_fp)
     gather.send()
 
     loads[2].wait()
@@ -286,10 +286,10 @@
     lax.fori_loop(0, cols // BLOCK, transpose, 0, unroll=2)
 
     left_t[...] = jnp.zeros_like(left_t)
-    all_z = flag_z.at[pl.ds(0, n_dp - 1)]
-    arrived(place, all_z, sem_fz)
-    flag_p[me] = jnp.sum(flag_z[...], axis=0)
-    exchange(place.plane_all, lambda k: flag_p.at[me], flag_p.at[me], sem_fp)
+    all_p = flag_p.at[pl.ds(0, n_mp - 1)]
+    arrived(place, all_p, sem_fp)
+    flag_z[place.z] = jnp.sum(flag_p[...], axis=0)
+    exchange(place.z_peers, lambda k: flag_z.at[place.z], flag_z.at[place.z], sem_fz)
 
     def rows_of(chip):
         return pl.ds(pl.multiple_of(chip * block, 16), block)
@@ -300,9 +300,9 @@
         left_t[...] += jnp.dot(got.T, both_t[rows_of(chip), :], preferred_element_type=F32)
 
     gather.receive(use)
-    all_p = flag_p.at[pl.ds(0, n_mp - 1)]
-    arrived(place, all_p, sem_fp)
-    healthy = jnp.sum(flag_p[...], axis=0)
+    all_z = flag_z.at[pl.ds(0, n_dp - 1)]
+    arrived(place, all_z, sem_fz)
+    healthy = jnp.sum(flag_z[...], axis=0)
     factor = float(n_dp * n_mp) / jnp.maximum(healthy, 1.0)
     for r in range(0, rows, BLOCK):
         part[r:r + BLOCK, :] = (left_t[:, r:r + BLOCK] + factor * left_t[:, rows + r:rows + r + BLOCK]).T
@@ -402,8 +402,8 @@
     total = lax.dot_general(total, tri[...], by_rank, precision=HIGH, preferred_element_type=F32)
     mine[...] = total
     own_share = mine[pl.ds(pl.multiple_of(place.core * (window - share), 8), share)]
-    sq_z[place.z] = jnp.sum(own_share * own_share, axis=0, keepdims=True)
-    exchange(place.z_peers, lambda k: sq_z.at[place.z], sq_z.at[place.z], sem_sz)
+    sq_p[me] = jnp.sum(own_share * own_share, axis=0, keepdims=True)
+    exchange(place.plane_all, lambda k: sq_p.at[me], sq_p.at[me], sem_sp)
     low_ref[pl.ds(pl.multiple_of(place.chip * block + place.core * keep, 16), window)] = total.astype(BF16)
     last_gather = WindowGather(place, low_ref, block, window, sem_low)
     last_gather.send()
@@ -411,12 +411,12 @@
     ortho_ref[...] = lax.dot_general(
         left[...], tri[...], by_rank, precision=HIGH, preferred_element_type=F32
     ).astype(BF16)
+    arrived(place, sq_p.at[pl.ds(0, n_mp - 1)], sem_sp)
+    sq_z[place.z] = jnp.sum(sq_p[...], axis=0)
+    exchange(place.z_peers, lambda k: sq_z.at[place.z], sq_z.at[place.z], sem_sz)
+    last_gather.receive()
     arrived(place, sq_z.at[pl.ds(0, n_dp - 1)], sem_sz)
-    sq_p[me] = jnp.sum(sq_z[...], axis=0)
-    exchange(place.plane_all, lambda k: sq_p.at[me], sq_p.at[me], sem_sp)
-    last_gather.receive()
-    arrived(place, sq_p.at[pl.ds(0, n_mp - 1)], sem_sp)
-    squares = jnp.sum(sq_p[...], axis=0)
+    squares = jnp.sum(sq_z[...], axis=0)
     inv_ref[...] = jnp.broadcast_to(lax.rsqrt(squares + EPSILON), inv_ref.shape)
     for ref, sems in [
         (all_z, sem_fz), (all_p, sem_fp), (left_in, sem_lr), (all_left, sem_lg), (gram_zc, sem_gz), (all_gp, sem_gp),

time: 59.6 us -> 59.6 us (level)
  no operation moved by 1% of the time
where the time goes in v11:
time: 59.6 us; the launch traced here: 59.5 us
  Pallas kernels  58.2 us (98%)
  between operations  1.29 us (2%)
    pallas_call x1, Pallas kernels, mega_stage(): pl.pallas_call(functools.partial(mega_kernel, n_dp, n_mp), name='mega', o...  56.2 us
    pallas_call x1, Pallas kernels, finish_stage(): pl.pallas_call(functools.partial(finish_kernel, unit), name='finish', out...  1.99 us

profile of v11, /device:TPU:1, one launch (start us, length us, event | category | flops | bytes accessed | tf_op | source)
XLA Modules:
  0.0 59.5 jit_solution(17652641500370442854)
XLA Ops:
  1.3 56.2 %mega.1 = (bf16[256,128]{1,0:T(8,128)(2,1)S(1)}, bf16[3328,128]{1,0:T(8,128)(2,1)S(1)}, f32[8,128]{1,0:T(8,128)S(1)}, f32[104,128]{1,0:T(8,128)S(1)}, f32[256,3328]{1,0:T(8,128)S(1)}) custom-call(bf16[256,3328]{1,0:T(8,128)(2,1)} %mom_hbm.1, bf16[256,3328]{1,0:T(8,128)(2,1)} %tile_hbm.1, s32[2,26]{1,0:T(2,128)} %exps_hbm.1, f32[104,128]{1,0:T(8,128)} %prev_hbm.1, ...), custom_call_target="tpu_custom_call" | custom-call | tf_op jit(solution)/shard_map/mega/pallas_call | solution.py:443
  57.5 2.0 %finish.1 = (bf16[256,3328]{1,0:T(8,128)(2,1)}, bf16[256,3328]{1,0:T(8,128)(2,1)}, f32[104,128]{1,0:T(8,128)}) custom-call(f32[256,3328]{1,0:T(8,128)S(1)} %get-tuple-element.11.sums, bf16[256,128]{1,0:T(8,128)(2,1)S(1)} %get-tuple-element.12.ortho, bf16[3328,128]{1,0:T(8,128)(2,1)S(1)} %get-tuple-element.13.low, f32[8,128]{1,0:T(8,128)S(1)} %get-tuple-element.14.inv, ...), custom_call_target="tpu_custom_call" | custom-call | tf_op jit(solution)/shard_map/finish/pallas_call | solution.py:532
